TPU v7x, 32 devices: a whole 2x2x4 slice. The times are simulated.
32 devices in a mesh: rep: 8 (over z, x), par: 4 (over y, core).
Axes of the slice: x: 2, y: 2, z: 4, core: 2. Of those that a mesh axis runs over, the one named last changes fastest.
Arguments:
- activations: bfloat16 [2, 16384, 8192], P(None, 'rep', 'par'), may hold values from -12 to 12, as said below
- output_grads: bfloat16 [2, 16384, 1024], P(None, 'rep'), may hold values from -12 to 12, as said below
Outputs:
- combined: bfloat16 [2, 8192, 1024], P(None, ('par', 'rep'))
Inputs may be any that keep to these rules, and one draw needn't show every extreme that they name: `activations`: activations of one replica and layer. `output_grads`: output gradients of one replica and layer.
All inputs are finite; a program needn't handle non-finite values.
Results may differ from a plain program's by a relative error of at most 0.0062.
Values may be sent and summed in bfloat16 or wider, within the bound.
No kernel may reach another device: no remote copies, remote signals or barrier semaphores. Data moves between devices by JAX's collectives and lax.ppermute only.
A program may use at most 128 MiB of HBM per device.

v0:
```python
import jax
import jax.numpy as jnp
from jax import lax
from jax.sharding import PartitionSpec as P

epsilon = 1e-06


def swapped(value, axis, stride):
    return lax.ppermute(value, axis, [(i, i ^ 1 << stride) for i in range(lax.axis_size(axis))])


def pair_statistics(first_part, second_part):
    first_wide = first_part.astype(jnp.float32)
    second_wide = second_part.astype(jnp.float32)
    return jnp.stack(
        [
            jnp.sum(first_wide * second_wide, axis=(1, 2)),
            jnp.sum(first_wide * first_wide, axis=(1, 2)),
            jnp.sum(second_wide * second_wide, axis=(1, 2)),
        ]
    )


def combine_parts(first_part, second_part, totals):
    dot_value = totals[0][:, None, None]
    first_scale = 1.0 - dot_value / (2.0 * (totals[1][:, None, None] + epsilon))
    second_scale = 1.0 - dot_value / (2.0 * (totals[2][:, None, None] + epsilon))
    result = first_scale * first_part.astype(jnp.float32) + second_scale * second_part.astype(
        jnp.float32
    )
    return result.astype(jnp.bfloat16)


def body(activations, output_grads):
    gradient = jnp.einsum(
        "ltd,ltk->ldk", activations, output_grads, preferred_element_type=jnp.float32
    ).astype(jnp.bfloat16)
    replicas = lax.axis_size("rep")
    levels = replicas.bit_length() - 1
    rank_rep = lax.axis_index("rep")
    layers = gradient.shape[0]
    width_out = gradient.shape[2]
    fine_rows = gradient.shape[1] // replicas
    segment = gradient
    for level_bit in range(levels):
        blocks_left = replicas >> level_bit
        paired = segment.reshape(layers, blocks_left // 2, 2, fine_rows, width_out)
        lower_part = paired[:, :, 0].reshape(layers, blocks_left // 2 * fine_rows, width_out)
        higher_part = paired[:, :, 1].reshape(layers, blocks_left // 2 * fine_rows, width_out)
        is_upper = rank_rep >> level_bit & 1 == 1
        kept_part = jnp.where(is_upper, higher_part, lower_part)
        sent_part = jnp.where(is_upper, lower_part, higher_part)
        partner = swapped(sent_part, "rep", level_bit)
        first_part = jnp.where(is_upper, partner, kept_part)
        second_part = jnp.where(is_upper, kept_part, partner)
        statistics = pair_statistics(first_part, second_part)
        statistics = lax.psum(statistics, "par")
        for bit_index in range(level_bit + 1):
            statistics = statistics + swapped(statistics, "rep", bit_index)
        segment = combine_parts(first_part, second_part, statistics)
    return segment


def solution(mesh):
    return jax.shard_map(
        body,
        mesh=mesh,
        in_specs=(P(None, "rep", "par"), P(None, "rep", None)),
        out_specs=P(None, ("par", "rep"), None),
        check_vma=False,
    )
```

profile of v0, /device:TPU:0, one launch (start us, length us, event | category | flops | bytes accessed | tf_op | source)
XLA Modules:
  0.0 283.0 jit_solution(17193531158070219688)
XLA Ops:
  0.0 22.8 %convolution_convert_fusion = bf16[2,2048,1024]{2,1,0:T(8,128)(2,1)S(1)} fusion(bf16[2,2048,2048]{2,1,0:T(8,128)(2,1)} %param.2, bf16[2,2048,1024]{2,1,0:T(8,128)(2,1)} %param.3), kind=kOutput, calls=%fused_computation.15 | convolution fusion | flops 17184063488 | bytes 33554432 | tf_op jit(solution)/shard_map/ltd,ltk->ldk/dot_general | solution.py:36
  22.8 3.6 %broadcast_select_fusion = (bf16[2,4,1,256,1024]{4,3,2,1,0:T(8,128)(2,1)}, bf16[2,4,1,256,1024]{4,3,2,1,0:T(8,128)(2,1)}) fusion(pred[]{:T(512)S(6)} %eq.11, bf16[2,4,2,256,1024]{4,3,2,1,0:T(8,128)(2,1)S(1)} %bitcast.69), kind=kLoop, calls=%fused_computation.23 | loop fusion | flops 4194304 | bytes 16777216 | tf_op jit(solution)/shard_map/jit(_where)/select_n | solution.py:52
  26.4 2.9 %collective-permute-start = (bf16[2,1024,1024]{2,1,0:T(8,128)(2,1)}, bf16[2,1024,1024]{2,1,0:T(8,128)(2,1)}, u32[]{:S(2)}, u32[]{:S(2)}) collective-permute-start(bf16[2,1024,1024]{2,1,0:T(8,128)(2,1)} %bitcast.1), channel_id=1, source_target_pairs={{0,4},{4,0},{8,12},{12,8},{16,20},{20,16},{24,28},{28,24},{1,5},{5... | collective-permute-start | bytes 12582920 | tf_op jit(solution)/shard_map/ppermute | solution.py:10
  29.3 90.9 %collective-permute-done = bf16[2,1024,1024]{2,1,0:T(8,128)(2,1)} collective-permute-done((bf16[2,1024,1024]{2,1,0:T(8,128)(2,1)}, bf16[2,1024,1024]{2,1,0:T(8,128)(2,1)}, u32[]{:S(2)}, u32[]{:S(2)}) %collective-permute-start) | collective-permute-done | bytes 4194336 | tf_op jit(solution)/shard_map/ppermute | solution.py:10
  120.2 9.5 %fusion.3 = (f32[2]{0:T(128)S(1)}, f32[2]{0:T(128)S(1)}, f32[2]{0:T(128)S(1)}, bf16[2,1024,1024]{2,1,0:T(8,128)(2,1)}, bf16[2,1024,1024]{2,1,0:T(8,128)(2,1)}) fusion(bf16[2,1024,1024]{2,1,0:T(8,128)(2,1)} %collective-permute-done, bf16[2,4,1,256,1024]{4,3,2,1,0:T(8,128)(2,1)} %get-tuple-element.20, pred[]{:T(512)S(6)} %eq.11), kind=kLoop, calls=%fused_computation.8 | loop fusion | flops 20971514 | bytes 16777240 | tf_op jit(solution)/shard_map/reduce_sum | solution.py:18
  129.7 6.0 %psum.21 = f32[3,2]{1,0:T(4,128)S(1)} all-reduce(f32[3,2]{1,0:T(4,128)S(1)} %pad_maximum_fusion), channel_id=1, replica_groups=mesh['rep'=8,'par'=4] {'par'}, use_global_device_ids=true, to_apply=%region_3.4 | all-reduce | flops 6 | bytes 48 | tf_op jit(solution)/shard_map/psum | solution.py:58
  137.2 2.1 collective-permute-done.1
  139.3 5.8 %fusion.2 = bf16[2,1024,1024]{2,1,0:T(8,128)(2,1)S(1)} fusion(bf16[2,1024,1024]{2,1,0:T(8,128)(2,1)} %get-tuple-element.19, bf16[2,1024,1024]{2,1,0:T(8,128)(2,1)} %get-tuple-element.18, f32[2]{0:T(128)S(1)} %get-tuple-element.29, f32[2]{0:T(128)S(1)} %get-tuple-element.28), kind=kLoop, calls=%fused_computation.7 | loop fusion | flops 12582912 | bytes 12582928 | tf_op jit(solution)/shard_map/convert_element_type | solution.py:32
  145.2 2.2 broadcast_select_fusion.2
  148.9 44.7 %collective-permute-done.2 = bf16[2,512,1024]{2,1,0:T(8,128)(2,1)S(1)} collective-permute-done((bf16[2,512,1024]{2,1,0:T(8,128)(2,1)}, bf16[2,512,1024]{2,1,0:T(8,128)(2,1)S(1)}, u32[]{:S(2)}, u32[]{:S(2)}) %collective-permute-start.2) | collective-permute-done | bytes 2097184 | tf_op jit(solution)/shard_map/ppermute | solution.py:10
  194.9 5.2 %fusion.8 = (f32[2]{0:T(128)S(1)}, f32[2]{0:T(128)S(1)}, f32[2]{0:T(128)S(1)}, bf16[2,512,1024]{2,1,0:T(8,128)(2,1)S(1)}, bf16[2,512,1024]{2,1,0:T(8,128)(2,1)}) fusion(bf16[2,512,1024]{2,1,0:T(8,128)(2,1)} %copy-done, bf16[2,2,1,256,1024]{4,3,2,1,0:T(8,128)(2,1)} %get-tuple-element.22, pred[]{:T(512)S(6)} %eq.10), kind=kLoop, calls=%fused_computation.19 | loop fusion | flops 10485754 | bytes 8388633 | tf_op jit(solution)/shard_map/reduce_sum | solution.py:18
  200.1 5.8 %psum.22 = f32[3,2]{1,0:T(4,128)S(1)} all-reduce(f32[3,2]{1,0:T(4,128)S(1)} %pad_maximum_fusion.1), channel_id=1, replica_groups=mesh['rep'=8,'par'=4] {'par'}, use_global_device_ids=true, to_apply=%region_7.8 | all-reduce | flops 6 | bytes 48 | tf_op jit(solution)/shard_map/psum | solution.py:58
  206.0 1.6 collective-permute-start.3
  207.6 2.0 collective-permute-done.3
  209.6 1.7 collective-permute-start.4
  211.3 1.9 collective-permute-done.4
  213.2 2.8 fusion.7
  216.1 2.8 collective-permute-start.5
  218.8 43.4 %collective-permute-done.5 = bf16[2,256,1024]{2,1,0:T(8,128)(2,1)S(1)} collective-permute-done((bf16[2,256,1024]{2,1,0:T(8,128)(2,1)S(1)}, bf16[2,256,1024]{2,1,0:T(8,128)(2,1)S(1)}, u32[]{:S(2)}, u32[]{:S(2)}) %collective-permute-start.5) | collective-permute-done | bytes 1048608 | tf_op jit(solution)/shard_map/ppermute | solution.py:10
  263.7 5.8 %psum.23 = f32[3,2]{1,0:T(4,128)S(1)} all-reduce(f32[3,2]{1,0:T(4,128)S(1)} %pad_maximum_fusion.2), channel_id=1, replica_groups=mesh['rep'=8,'par'=4] {'par'}, use_global_device_ids=true, to_apply=%region_11.12 | all-reduce | flops 6 | bytes 48 | tf_op jit(solution)/shard_map/psum | solution.py:58
  271.0 2.1 collective-permute-done.6
  273.1 1.9 collective-permute-start.7
  275.0 1.7 collective-permute-done.7
  276.7 3.2 %collective-permute-start.8 = (f32[3,2]{1,0:T(4,128)S(1)}, f32[3,2]{1,0:T(4,128)S(1)}, u32[]{:S(2)}, u32[]{:S(2)}) collective-permute-start(f32[3,2]{1,0:T(4,128)S(1)} %add.97), channel_id=1, source_target_pairs={{0,16},{4,20},{8,24},{12,28},{16,0},{20,4},{24,8},{28,12},{1,17},{... | collective-permute-start | bytes 80 | tf_op jit(solution)/shard_map/ppermute | solution.py:10
  (21 shorter events, 10.7 us)
Async XLA Ops:
  26.4 93.8 %collective-permute-start = (bf16[2,1024,1024]{2,1,0:T(8,128)(2,1)}, bf16[2,1024,1024]{2,1,0:T(8,128)(2,1)}, u32[]{:S(2)}, u32[]{:S(2)}) collective-permute-start(bf16[2,1024,1024]{2,1,0:T(8,128)(2,1)} %bitcast.1), channel_id=1, source_target_pairs={{0,4},{4,0},{8,12},{12,8},{16,20},{20,16},{24,28},{28,24},{1,5},{5... | collective-permute-start | bytes 12582920 | tf_op jit(solution)/shard_map/ppermute | solution.py:10
  135.7 3.6 %collective-permute-start.1 = (f32[3,2]{1,0:T(4,128)S(1)}, f32[3,2]{1,0:T(4,128)S(1)}, u32[]{:S(2)}, u32[]{:S(2)}) collective-permute-start(f32[3,2]{1,0:T(4,128)S(1)} %psum.21), channel_id=1, source_target_pairs={{0,4},{4,0},{8,12},{12,8},{16,20},{20,16},{24,28},{28,24},{1,5},{5... | collective-permute-start | bytes 80 | tf_op jit(solution)/shard_map/ppermute | solution.py:10
  147.4 46.3 %collective-permute-start.2 = (bf16[2,512,1024]{2,1,0:T(8,128)(2,1)}, bf16[2,512,1024]{2,1,0:T(8,128)(2,1)S(1)}, u32[]{:S(2)}, u32[]{:S(2)}) collective-permute-start(bf16[2,512,1024]{2,1,0:T(8,128)(2,1)} %bitcast.9), channel_id=1, source_target_pairs={{0,8},{4,12},{8,0},{12,4},{16,24},{20,28},{24,16},{28,20},{1,9},{5... | collective-permute-start | bytes 6291464 | tf_op jit(solution)/shard_map/ppermute | solution.py:10
  193.6 1.3 copy-start
  206.0 3.6 %collective-permute-start.3 = (f32[3,2]{1,0:T(4,128)S(1)}, f32[3,2]{1,0:T(4,128)S(1)}, u32[]{:S(2)}, u32[]{:S(2)}) collective-permute-start(f32[3,2]{1,0:T(4,128)S(1)} %psum.22), channel_id=1, source_target_pairs={{0,4},{4,0},{8,12},{12,8},{16,20},{20,16},{24,28},{28,24},{1,5},{5... | collective-permute-start | bytes 80 | tf_op jit(solution)/shard_map/ppermute | solution.py:10
  209.6 3.6 %collective-permute-start.4 = (f32[3,2]{1,0:T(4,128)S(1)}, f32[3,2]{1,0:T(4,128)S(1)}, u32[]{:S(2)}, u32[]{:S(2)}) collective-permute-start(f32[3,2]{1,0:T(4,128)S(1)} %add.91), channel_id=1, source_target_pairs={{0,8},{4,12},{8,0},{12,4},{16,24},{20,28},{24,16},{28,20},{1,9},{5... | collective-permute-start | bytes 80 | tf_op jit(solution)/shard_map/ppermute | solution.py:10
  216.1 46.1 %collective-permute-start.5 = (bf16[2,256,1024]{2,1,0:T(8,128)(2,1)S(1)}, bf16[2,256,1024]{2,1,0:T(8,128)(2,1)S(1)}, u32[]{:S(2)}, u32[]{:S(2)}) collective-permute-start(bf16[2,256,1024]{2,1,0:T(8,128)(2,1)S(1)} %fusion.16), channel_id=1, source_target_pairs={{0,16},{4,20},{8,24},{12,28},{16,0},{20,4},{24,8},{28,12},{1,17},{... | collective-permute-start | bytes 3145736 | tf_op jit(solution)/shard_map/ppermute | solution.py:10
  269.5 3.6 %collective-permute-start.6 = (f32[3,2]{1,0:T(4,128)S(1)}, f32[3,2]{1,0:T(4,128)S(1)}, u32[]{:S(2)}, u32[]{:S(2)}) collective-permute-start(f32[3,2]{1,0:T(4,128)S(1)} %psum.23), channel_id=1, source_target_pairs={{0,4},{4,0},{8,12},{12,8},{16,20},{20,16},{24,28},{28,24},{1,5},{5... | collective-permute-start | bytes 80 | tf_op jit(solution)/shard_map/ppermute | solution.py:10
  273.1 3.6 %collective-permute-start.7 = (f32[3,2]{1,0:T(4,128)S(1)}, f32[3,2]{1,0:T(4,128)S(1)}, u32[]{:S(2)}, u32[]{:S(2)}) collective-permute-start(f32[3,2]{1,0:T(4,128)S(1)} %add.96), channel_id=1, source_target_pairs={{0,8},{4,12},{8,0},{12,4},{16,24},{20,28},{24,16},{28,20},{1,9},{5... | collective-permute-start | bytes 80 | tf_op jit(solution)/shard_map/ppermute | solution.py:10
  276.7 4.8 %collective-permute-start.8 = (f32[3,2]{1,0:T(4,128)S(1)}, f32[3,2]{1,0:T(4,128)S(1)}, u32[]{:S(2)}, u32[]{:S(2)}) collective-permute-start(f32[3,2]{1,0:T(4,128)S(1)} %add.97), channel_id=1, source_target_pairs={{0,16},{4,20},{8,24},{12,28},{16,0},{20,4},{24,8},{28,12},{1,17},{... | collective-permute-start | bytes 80 | tf_op jit(solution)/shard_map/ppermute | solution.py:10
where the time goes:
time: 283 us
  waiting for transfers between devices  190 us (67%)
  other arithmetic  32.2 us (11%)
  matrix products  22.8 us (8%)
  starting transfers between devices  18.7 us (7%)
  blocking collectives  17.6 us (6%)
    ppermute x9, waiting for transfers between devices, swapped(): lax.ppermute(value, axis, [(i, i ^ 1 << stride) for i in range(lax.axis_s...  190 us
    dot_general x1, matrix products, body(): jnp.einsum('ltd,ltk->ldk', activations, output_grads, preferred_element_t...  22.8 us
    ppermute x9, starting transfers between devices, swapped(): lax.ppermute(value, axis, [(i, i ^ 1 << stride) for i in range(lax.axis_s...  18.7 us
    psum x3, blocking collectives, body(): statistics = lax.psum(statistics, 'par')  17.6 us
    reduce_sum x3, other arithmetic, pair_statistics(): jnp.sum(first_wide * second_wide, axis=(1, 2))  16.1 us
    convert_element_type x3, other arithmetic, combine_parts(): return result.astype(jnp.bfloat16)  10.1 us
    select_n x2, other arithmetic, body(): kept_part = jnp.where(is_upper, higher_part, lower_part)  5.78 us
  transfers between devices with their start and end apart: 9, of which 9 were waited for; matrix products, arithmetic and copies ran while one was open for 0% of the time, Pallas kernels for 0%

commit v1 on v0

v1 whole, which is shorter than its diff:
```python
import functools

import jax
import jax.numpy as jnp
from jax import lax
from jax.experimental import pallas as pl
from jax.experimental.pallas import tpu as pltpu
from jax.sharding import PartitionSpec as P

epsilon = 1e-06
VMEM_LIMIT = 50 * 1024 * 1024
LANES = 128


def exchange(value, axis, mask):
    return lax.ppermute(value, axis, [(i, i ^ mask) for i in range(lax.axis_size(axis))])


def gradient_blocks(activations, output_grads, layer, blocks, rows):
    tokens, width_out = output_grads.shape[1:]
    count = len(blocks)
    depth = min(512, tokens)
    steps = tokens // depth
    wide_rows = max(rows, LANES)
    shared = wide_rows // rows

    def kernel(ids, a_ref, b_ref, *refs):
        outs, total = refs[:count], refs[count]
        unit, step = pl.program_id(0), pl.program_id(1)
        part = lax.dot_general(
            a_ref[0],
            b_ref[0, pl.ds(pl.multiple_of(step * depth, depth), depth), :],
            (((0,), (0,)), ((), ())),
            preferred_element_type=jnp.float32,
        )

        @pl.when(step == 0)
        def _():
            total[...] = part

        @pl.when(step > 0)
        def _():
            total[...] += part

        for index in range(count):

            @pl.when((unit == index) & (step == steps - 1))
            def _(index=index):
                first = pl.multiple_of(lax.rem(ids[unit], shared) * rows, rows)
                outs[index][...] = total[pl.ds(first, rows), :].astype(jnp.bfloat16)

    shape = jax.ShapeDtypeStruct((rows, width_out), jnp.bfloat16)
    return pl.pallas_call(
        kernel,
        grid_spec=pltpu.PrefetchScalarGridSpec(
            num_scalar_prefetch=1,
            grid=(count, steps),
            in_specs=[
                pl.BlockSpec((1, depth, wide_rows), lambda u, k, ids: (layer, k, ids[u] // shared)),
                pl.BlockSpec((1, tokens, width_out), lambda u, k, ids: (layer, 0, 0)),
            ],
            out_specs=[pl.BlockSpec((rows, width_out), lambda u, k, ids: (0, 0))] * count,
            scratch_shapes=[pltpu.VMEM((wide_rows, width_out), jnp.float32)],
        ),
        out_shape=[shape] * count,
        compiler_params=pltpu.CompilerParams(vmem_limit_bytes=VMEM_LIMIT),
        cost_estimate=pl.CostEstimate(
            flops=2 * count * tokens * rows * width_out,
            bytes_accessed=2 * (tokens * width_out + count * rows * (tokens + width_out)),
            transcendentals=0,
        ),
        name="gradient_blocks",
    )(jnp.stack(blocks), activations, output_grads)


def pair_row(first, second, count):
    low, high = jnp.minimum(first, second), jnp.maximum(first, second)
    return low * (2 * count - 1 - low) // 2 + high


def gram_rows(rank, parts):
    count = len(parts)
    rows, width = parts[0].shape
    pairs = [(u, v) for u in range(count) for v in range(u, count)]
    padded = -(-len(pairs) // 8) * 8
    stride = 16

    def kernel(rank_ref, *refs):
        ins, out = refs[:count], refs[count]

        def body(index, totals):
            where = pl.ds(pl.multiple_of(index * stride, stride), stride)
            totals = list(totals)
            for column in range(0, width, LANES):
                wide = [ref[where, column : column + LANES].astype(jnp.float32) for ref in ins]
                for number, (u, v) in enumerate(pairs):
                    product = wide[u] * wide[v]
                    totals[number] = totals[number] + (product[:8] + product[8:])
            return tuple(totals)

        zero = jnp.zeros((8, LANES), jnp.float32)
        totals = lax.fori_loop(0, rows // stride, body, (zero,) * len(pairs))
        out[...] = jnp.zeros_like(out)
        mine = rank_ref[0]
        for number, (u, v) in enumerate(pairs):
            row = pair_row(mine ^ u, mine ^ v, count)
            out[pl.ds(row, 1), :] = jnp.sum(totals[number], axis=0, keepdims=True)

    return pl.pallas_call(
        kernel,
        in_specs=[pl.BlockSpec(memory_space=pltpu.SMEM)]
        + [pl.BlockSpec(memory_space=pltpu.VMEM)] * count,
        out_specs=pl.BlockSpec(memory_space=pltpu.VMEM),
        out_shape=jax.ShapeDtypeStruct((padded, LANES), jnp.float32),
        compiler_params=pltpu.CompilerParams(vmem_limit_bytes=VMEM_LIMIT),
        cost_estimate=pl.CostEstimate(
            flops=2 * len(pairs) * rows * width,
            bytes_accessed=2 * count * rows * width,
            transcendentals=0,
        ),
        name="gram_rows",
    )(rank, *parts)


def tree_weights(gram, count):
    factors = [1.0] * count
    scales = []
    size = 1
    while size < count:
        level = []
        for start in range(0, count, 2 * size):
            first = range(start, start + size)
            second = range(start + size, start + 2 * size)

            def form(left, right):
                terms = [factors[i] * factors[j] * gram(i, j) for i in left for j in right]
                return functools.reduce(lambda a, b: a + b, terms)

            dot_value = form(first, second)
            norm_first = jnp.maximum(form(first, first), 0.0)
            norm_second = jnp.maximum(form(second, second), 0.0)
            first_scale = 1.0 - dot_value / (2.0 * (norm_first + epsilon))
            second_scale = 1.0 - dot_value / (2.0 * (norm_second + epsilon))
            level += [first_scale, second_scale]
            for i in first:
                factors[i] = factors[i] * first_scale
            for i in second:
                factors[i] = factors[i] * second_scale
        scales.append(level)
        size *= 2
    return scales


def combine(rank, grams, layer_parts):
    layers, count = len(layer_parts), len(layer_parts[0])
    rows, width = layer_parts[0][0].shape
    levels = count.bit_length() - 1
    stride = 16

    def kernel(rank_ref, gram_ref, *refs):
        out = refs[layers * count]
        mine = rank_ref[0]
        padded = gram_ref.shape[0] // layers
        sums = jnp.sum(gram_ref[...], axis=1, keepdims=True)
        for layer in range(layers):
            ins = refs[layer * count : (layer + 1) * count]

            def gram(i, j):
                low, high = min(i, j), max(i, j)
                row = layer * padded + low * (2 * count - 1 - low) // 2 + high
                return sums[row : row + 1]

            scales = tree_weights(gram, count)
            relative = []
            for level, values in enumerate(scales):
                group = mine >> level
                moved = list(values)
                for bit in range(levels - level):
                    flip = ((group >> bit) & 1) == 1
                    moved = [
                        jnp.where(flip, moved[i ^ (1 << bit)], moved[i]) for i in range(len(moved))
                    ]
                relative.append([jnp.broadcast_to(value, (stride, LANES)) for value in moved])

            def body(index, carry):
                where = pl.ds(pl.multiple_of(index * stride, stride), stride)
                for column in range(0, width, LANES):
                    held = [ref[where, column : column + LANES] for ref in ins]
                    for level in range(levels):
                        wide = [value.astype(jnp.float32) for value in held]
                        held = [
                            (
                                relative[level][2 * pair] * wide[2 * pair]
                                + relative[level][2 * pair + 1] * wide[2 * pair + 1]
                            ).astype(jnp.bfloat16)
                            for pair in range(len(held) // 2)
                        ]
                    out[layer, where, column : column + LANES] = held[0]
                return carry

            lax.fori_loop(0, rows // stride, body, 0)

    return pl.pallas_call(
        kernel,
        in_specs=[pl.BlockSpec(memory_space=pltpu.SMEM)]
        + [pl.BlockSpec(memory_space=pltpu.VMEM)] * (1 + layers * count),
        out_specs=pl.BlockSpec(memory_space=pltpu.VMEM),
        out_shape=jax.ShapeDtypeStruct((layers, rows, width), jnp.bfloat16),
        compiler_params=pltpu.CompilerParams(vmem_limit_bytes=VMEM_LIMIT),
        cost_estimate=pl.CostEstimate(
            flops=3 * layers * count * rows * width,
            bytes_accessed=2 * layers * (count + 1) * rows * width,
            transcendentals=0,
        ),
        name="combine",
    )(rank, grams, *[part for parts in layer_parts for part in parts])


def level_masks(levels):
    masks = [1 << level for level in range(levels)]
    if levels >= 3:
        masks[-1] |= masks[-2]
    return masks


def spread(code, masks):
    value = 0
    for bit, mask in enumerate(masks):
        if code >> bit & 1:
            value ^= mask
    return value


def transfer_rounds(levels, layers):
    count = 1 << levels
    queues = []
    for level in range(levels):
        units = []
        for block in range(count):
            if block & ((2 << level) - 1) == 1 << level:
                for part in range(1 << level):
                    units.append((block, part))
        queues.append(units)
    arrival = {}
    rounds = []
    for slot in range(count // 2):
        chosen = []
        for level in range(levels):

            def ready(unit):
                block, part = unit
                if part == 0:
                    return -1
                top = part.bit_length() - 1
                return arrival.get((top, block | 1 << top, part ^ 1 << top), count)

            able = [unit for unit in queues[level] if ready(unit) < slot]
            able.sort(key=lambda unit: (-(unit[0] >> (level + 1)), -unit[1]))
            unit = able[0]
            queues[level].remove(unit)
            chosen.append(unit)
        for level, unit in enumerate(chosen):
            arrival[(level,) + unit] = slot
        rounds += [[(layer,) + unit for unit in chosen] for layer in range(layers)]
    return rounds


def body(activations, output_grads):
    replicas = lax.axis_size("rep")
    levels = replicas.bit_length() - 1
    layers, _, width = activations.shape
    rows = width // replicas
    rank = lax.axis_index("rep")
    masks = level_masks(levels)
    rounds = transfer_rounds(levels, layers)

    held = {}

    def make(layer, codes):
        blocks = [rank ^ spread(code, masks) for code in codes]
        for code, value in zip(codes, gradient_blocks(activations, output_grads, layer, blocks, rows)):
            held[layer, code, 0] = value

    wanted = [[] for _ in range(layers)]
    for chosen in rounds:
        for level, (layer, block, part) in enumerate(chosen):
            for code in (block,):
                if part == 0 and code not in wanted[layer]:
                    wanted[layer].append(code)
    wanted = [codes + [0] for codes in wanted]
    early = [[chosen[level][1] for level in range(levels)] for chosen in rounds[:layers]]
    for layer in range(layers):
        make(layer, early[layer])
    for layer in range(layers):
        make(layer, [code for code in wanted[layer] if code not in early[layer]])

    in_flight = []
    for chosen in rounds:
        sent = [held[unit] for unit in chosen]
        if len(in_flight) >= layers:
            keys = in_flight.pop(0)
            joined = lax.optimization_barrier(tuple(sent) + tuple(held[key] for key in keys))
            sent = joined[: len(sent)]
            for key, value in zip(keys, joined[len(sent) :]):
                held[key] = value
        keys = []
        for level, (layer, block, part) in enumerate(chosen):
            key = (layer, block ^ 1 << level, part | 1 << level)
            held[key] = exchange(sent[level], "rep", masks[level])
            keys.append(key)
        in_flight.append(keys)

    order = {spread(code, masks): code for code in range(replicas)}
    parts = [[held[layer, 0, order[step]] for step in range(replicas)] for layer in range(layers)]
    position = jnp.reshape(rank, (1,)).astype(jnp.int32)
    grams = jnp.concatenate([gram_rows(position, parts[layer]) for layer in range(layers)])
    par = lax.axis_size("par")
    stride = 1
    while stride < par:
        grams = grams + exchange(grams, "par", stride)
        stride *= 2
    for mask in masks:
        grams = grams + exchange(grams, "rep", mask)
    return combine(position, grams, parts)


def solution(mesh):
    return jax.shard_map(
        body,
        mesh=mesh,
        in_specs=(P(None, "rep", "par"), P(None, "rep", None)),
        out_specs=P(None, ("par", "rep"), None),
        check_vma=False,
    )
```

time: 283 us -> 232 us (0.82)
  waiting for transfers between devices: 190 us -> 113 us
  Pallas kernels: 0 us -> 76.6 us
  other arithmetic: 32.2 us -> 0.12 us
  matrix products: 22.8 us -> 0 us
  starting transfers between devices: 18.7 us -> 39.3 us
  blocking collectives: 17.6 us -> 0 us
    ppermute x9 -> x29, waiting for transfers between devices: 190 us -> 113 us  [exchange(): lax.ppermute(value, axis, [(i, i ^ mask) for i in range(lax.axis_size(axi...]
    pallas_call x0 -> x7, Pallas kernels: none -> 76.6 us  [the longest x4 61.5 us: gradient_blocks(): pl.pallas_call(kernel, grid_spec=pltpu.PrefetchScalarGridSpec(num_scalar_...]
    dot_general x1 -> x0, matrix products: 22.8 us -> none  [body(): jnp.einsum('ltd,ltk->ldk', activations, output_grads, preferred_element_t...]
    ppermute x9 -> x29, starting transfers between devices: 18.7 us -> 39.3 us  [exchange(): lax.ppermute(value, axis, [(i, i ^ mask) for i in range(lax.axis_size(axi...]
    psum x3 -> x0, blocking collectives: 17.6 us -> none  [body(): statistics = lax.psum(statistics, 'par')]
    reduce_sum x3 -> x0, other arithmetic: 16.1 us -> none  [pair_statistics(): jnp.sum(first_wide * second_wide, axis=(1, 2))]
    convert_element_type x3 -> x0, other arithmetic: 10.1 us -> none  [combine_parts(): return result.astype(jnp.bfloat16)]
    select_n x3 -> x0, other arithmetic: 5.89 us -> none  [the longest x2 5.78 us: body(): kept_part = jnp.where(is_upper, higher_part, lower_part)]
  transfers between devices with their start and end apart: 9 -> 29, of which waited for: 9 -> 17; matrix products, arithmetic and copies ran while one was open for 0% -> 0% of each run, Pallas kernels for 0% -> 23%
where the time goes in v1:
time: 232 us; the launch traced here: 231 us
  waiting for transfers between devices  113 us (49%)
  Pallas kernels  76.6 us (33%)
  starting transfers between devices  39.3 us (17%)
    ppermute x29, waiting for transfers between devices, exchange(): lax.ppermute(value, axis, [(i, i ^ mask) for i in range(lax.axis_size(axi...  113 us
    pallas_call x4, Pallas kernels, gradient_blocks(): pl.pallas_call(kernel, grid_spec=pltpu.PrefetchScalarGridSpec(num_scalar_...  61.5 us
    ppermute x29, starting transfers between devices, exchange(): lax.ppermute(value, axis, [(i, i ^ mask) for i in range(lax.axis_size(axi...  39.3 us
    pallas_call x2, Pallas kernels, gram_rows(): pl.pallas_call(kernel, in_specs=[pl.BlockSpec(memory_space=pltpu.SMEM)] +...  8.56 us
    pallas_call x1, Pallas kernels, combine(): pl.pallas_call(kernel, in_specs=[pl.BlockSpec(memory_space=pltpu.SMEM)] +...  6.57 us
  transfers between devices with their start and end apart: 29, of which 17 were waited for; matrix products, arithmetic and copies ran while one was open for 0% of the time, Pallas kernels for 23%

profile of v1, /device:TPU:0, one launch (start us, length us, event | category | flops | bytes accessed | tf_op | source)
XLA Modules:
  0.0 230.9 jit_solution(15899935759545498215)
XLA Ops:
  0.1 12.7 %gradient_blocks.5 = (bf16[256,1024]{1,0:T(8,128)(2,1)}, bf16[256,1024]{1,0:T(8,128)(2,1)S(1)}, bf16[256,1024]{1,0:T(8,128)(2,1)S(1)}) custom-call(s32[3]{0:T(128)S(1)} %pad_add_fusion.ids, bf16[2,2048,2048]{2,1,0:T(8,128)(2,1)} %a_ref.7, bf16[2,2048,1024]{2,1,0:T(8,128)(2,1)} %b_ref.7), custom_call_target="tpu_custom_call" | custom-call | flops 3221225472 | bytes 8912896 | tf_op jit(solution)/shard_map/gradient_blocks/pallas_call | solution.py:53
  12.8 2.9 %collective-permute-start = (bf16[256,1024]{1,0:T(8,128)(2,1)}, bf16[256,1024]{1,0:T(8,128)(2,1)}, u32[]{:S(2)}, u32[]{:S(2)}) collective-permute-start(bf16[256,1024]{1,0:T(8,128)(2,1)} %get-tuple-element.54), channel_id=1, source_target_pairs={{0,4},{4,0},{8,12},{12,8},{16,20},{20,16},{24,28},{28,24},{1,5},{5... | collective-permute-start | bytes 1572872 | tf_op jit(solution)/shard_map/ppermute | solution.py:16
  19.8 12.0 %gradient_blocks.7 = (bf16[256,1024]{1,0:T(8,128)(2,1)S(1)}, bf16[256,1024]{1,0:T(8,128)(2,1)S(1)}, bf16[256,1024]{1,0:T(8,128)(2,1)S(1)}) custom-call(s32[3]{0:T(128)S(1)} %pad_add_fusion.ids, bf16[2,2048,2048]{2,1,0:T(8,128)(2,1)} %a_ref.7, bf16[2,2048,1024]{2,1,0:T(8,128)(2,1)} %b_ref.7), custom_call_target="tpu_custom_call" | custom-call | flops 3221225472 | bytes 8912896 | tf_op jit(solution)/shard_map/gradient_blocks/pallas_call | solution.py:53
  34.0 18.3 %gradient_blocks.4 = (bf16[256,1024]{1,0:T(8,128)(2,1)S(1)}, bf16[256,1024]{1,0:T(8,128)(2,1)S(1)}, bf16[256,1024]{1,0:T(8,128)(2,1)S(1)}, bf16[256,1024]{1,0:T(8,128)(2,1)S(1)}, bf16[256,1024]{1,0:T(8,128)(2,1)S(1)}) custom-call(s32[5]{0:T(128)S(1)} %stack.42.ids, bf16[2,2048,2048]{2,1,0:T(8,128)(2,1)} %a_ref.7, bf16[2,2048,1024]{2,1,0:T(8,128)(2,1)} %b_ref.7), custom_call_target="tpu_custom_call" | custom-call | flops 5368709120 | bytes 12058624 | tf_op jit(solution)/shard_map/gradient_blocks/pallas_call | solution.py:53
  57.3 18.5 %gradient_blocks.6 = (bf16[256,1024]{1,0:T(8,128)(2,1)S(1)}, bf16[256,1024]{1,0:T(8,128)(2,1)S(1)}, bf16[256,1024]{1,0:T(8,128)(2,1)S(1)}, bf16[256,1024]{1,0:T(8,128)(2,1)S(1)}, bf16[256,1024]{1,0:T(8,128)(2,1)S(1)}) custom-call(s32[5]{0:T(128)S(1)} %stack.42.ids, bf16[2,2048,2048]{2,1,0:T(8,128)(2,1)} %a_ref.7, bf16[2,2048,1024]{2,1,0:T(8,128)(2,1)} %b_ref.7), custom_call_target="tpu_custom_call" | custom-call | flops 5368709120 | bytes 12058624 | tf_op jit(solution)/shard_map/gradient_blocks/pallas_call | solution.py:53
  79.6 9.4 %collective-permute-done.5.refs_4_ = bf16[256,1024]{1,0:T(8,128)(2,1)S(1)} collective-permute-done((bf16[256,1024]{1,0:T(8,128)(2,1)}, bf16[256,1024]{1,0:T(8,128)(2,1)S(1)}, u32[]{:S(2)}, u32[]{:S(2)}) %collective-permute-start.5) | collective-permute-done | bytes 524320 | tf_op jit(solution)/shard_map/ppermute | solution.py:16
  89.5 12.1 %collective-permute-done.15 = bf16[256,1024]{1,0:T(8,128)(2,1)S(1)} collective-permute-done((bf16[256,1024]{1,0:T(8,128)(2,1)}, bf16[256,1024]{1,0:T(8,128)(2,1)S(1)}, u32[]{:S(2)}, u32[]{:S(2)}) %collective-permute-start.15) | collective-permute-done | bytes 524320 | tf_op jit(solution)/shard_map/ppermute | solution.py:16
  101.7 8.4 %collective-permute-start.8 = (bf16[256,1024]{1,0:T(8,128)(2,1)S(1)}, bf16[256,1024]{1,0:T(8,128)(2,1)S(1)}, u32[]{:S(2)}, u32[]{:S(2)}) collective-permute-start(bf16[256,1024]{1,0:T(8,128)(2,1)S(1)} %collective-permute-done.3), channel_id=1, source_target_pairs={{0,24},{4,28},{8,16},{12,20},{16,8},{20,12},{24,0},{28,4},{1,25},{... | collective-permute-start | bytes 1572872 | tf_op jit(solution)/shard_map/ppermute | solution.py:16
  112.1 2.7 %collective-permute-start.20 = (bf16[256,1024]{1,0:T(8,128)(2,1)S(1)}, bf16[256,1024]{1,0:T(8,128)(2,1)S(1)}, u32[]{:S(2)}, u32[]{:S(2)}) collective-permute-start(bf16[256,1024]{1,0:T(8,128)(2,1)S(1)} %collective-permute-done.15), channel_id=1, source_target_pairs={{0,24},{4,28},{8,16},{12,20},{16,8},{20,12},{24,0},{28,4},{1,25},{... | collective-permute-start | bytes 1572872 | tf_op jit(solution)/shard_map/ppermute | solution.py:16
  114.8 8.0 %collective-permute-done.7.refs_2_ = bf16[256,1024]{1,0:T(8,128)(2,1)S(1)} collective-permute-done((bf16[256,1024]{1,0:T(8,128)(2,1)S(1)}, bf16[256,1024]{1,0:T(8,128)(2,1)S(1)}, u32[]{:S(2)}, u32[]{:S(2)}) %collective-permute-start.7) | collective-permute-done | bytes 524320 | tf_op jit(solution)/shard_map/ppermute | solution.py:16
  122.9 11.2 %collective-permute-done.8.refs_5_ = bf16[256,1024]{1,0:T(8,128)(2,1)S(1)} collective-permute-done((bf16[256,1024]{1,0:T(8,128)(2,1)S(1)}, bf16[256,1024]{1,0:T(8,128)(2,1)S(1)}, u32[]{:S(2)}, u32[]{:S(2)}) %collective-permute-start.8) | collective-permute-done | bytes 524320 | tf_op jit(solution)/shard_map/ppermute | solution.py:16
  134.6 2.7 %collective-permute-start.11 = (bf16[256,1024]{1,0:T(8,128)(2,1)S(1)}, bf16[256,1024]{1,0:T(8,128)(2,1)S(1)}, u32[]{:S(2)}, u32[]{:S(2)}) collective-permute-start(bf16[256,1024]{1,0:T(8,128)(2,1)S(1)} %collective-permute-done.4), channel_id=1, source_target_pairs={{0,24},{4,28},{8,16},{12,20},{16,8},{20,12},{24,0},{28,4},{1,25},{... | collective-permute-start | bytes 1572872 | tf_op jit(solution)/shard_map/ppermute | solution.py:16
  137.3 8.1 %collective-permute-done.19.refs_2_.refs_10_ = bf16[256,1024]{1,0:T(8,128)(2,1)S(1)} collective-permute-done((bf16[256,1024]{1,0:T(8,128)(2,1)S(1)}, bf16[256,1024]{1,0:T(8,128)(2,1)S(1)}, u32[]{:S(2)}, u32[]{:S(2)}) %collective-permute-start.19) | collective-permute-done | bytes 524320 | tf_op jit(solution)/shard_map/ppermute | solution.py:16
  145.3 11.2 %collective-permute-done.20.refs_5_.refs_13_ = bf16[256,1024]{1,0:T(8,128)(2,1)S(1)} collective-permute-done((bf16[256,1024]{1,0:T(8,128)(2,1)S(1)}, bf16[256,1024]{1,0:T(8,128)(2,1)S(1)}, u32[]{:S(2)}, u32[]{:S(2)}) %collective-permute-start.20) | collective-permute-done | bytes 524320 | tf_op jit(solution)/shard_map/ppermute | solution.py:16
  159.7 8.0 %collective-permute-done.10.refs_3_ = bf16[256,1024]{1,0:T(8,128)(2,1)S(1)} collective-permute-done((bf16[256,1024]{1,0:T(8,128)(2,1)S(1)}, bf16[256,1024]{1,0:T(8,128)(2,1)S(1)}, u32[]{:S(2)}, u32[]{:S(2)}) %collective-permute-start.10) | collective-permute-done | bytes 524320 | tf_op jit(solution)/shard_map/ppermute | solution.py:16
  167.8 11.3 %collective-permute-done.11.refs_7_ = bf16[256,1024]{1,0:T(8,128)(2,1)S(1)} collective-permute-done((bf16[256,1024]{1,0:T(8,128)(2,1)S(1)}, bf16[256,1024]{1,0:T(8,128)(2,1)S(1)}, u32[]{:S(2)}, u32[]{:S(2)}) %collective-permute-start.11) | collective-permute-done | bytes 524320 | tf_op jit(solution)/shard_map/ppermute | solution.py:16
  179.9 4.3 %gram_rows.2 = f32[40,128]{1,0:T(8,128)S(1)} custom-call(s32[1]{0:T(128)} %bitcast.rank_ref, bf16[256,1024]{1,0:T(8,128)(2,1)S(1)} %get-tuple-element.49.refs_0_, bf16[256,1024]{1,0:T(8,128)(2,1)S(1)} %collective-permute-done.9.refs_1_, bf16[256,1024]{1,0:T(8,128)(2,1)S(1)} %collective-permute-done.7.refs_2_, ...), custom_call_target="tpu_custom_call" | custom-call | flops 18874368 | bytes 4194304 | tf_op jit(solution)/shard_map/gram_rows/pallas_call | solution.py:109
  184.2 5.5 %collective-permute-done.22.refs_3_.refs_11_ = bf16[256,1024]{1,0:T(8,128)(2,1)S(1)} collective-permute-done((bf16[256,1024]{1,0:T(8,128)(2,1)S(1)}, bf16[256,1024]{1,0:T(8,128)(2,1)S(1)}, u32[]{:S(2)}, u32[]{:S(2)}) %collective-permute-start.22) | collective-permute-done | bytes 524320 | tf_op jit(solution)/shard_map/ppermute | solution.py:16
  189.7 10.4 %collective-permute-done.23.refs_7_.refs_15_ = bf16[256,1024]{1,0:T(8,128)(2,1)S(1)} collective-permute-done((bf16[256,1024]{1,0:T(8,128)(2,1)S(1)}, bf16[256,1024]{1,0:T(8,128)(2,1)S(1)}, u32[]{:S(2)}, u32[]{:S(2)}) %collective-permute-start.23) | collective-permute-done | bytes 524320 | tf_op jit(solution)/shard_map/ppermute | solution.py:16
  200.8 4.3 %gram_rows.3 = f32[40,128]{1,0:T(8,128)S(1)} custom-call(s32[1]{0:T(128)} %bitcast.rank_ref, bf16[256,1024]{1,0:T(8,128)(2,1)S(1)} %get-tuple-element.71.refs_0_.refs_8_, bf16[256,1024]{1,0:T(8,128)(2,1)S(1)} %collective-permute-done.21.refs_1_.refs_9_, bf16[256,1024]{1,0:T(8,128)(2,1)S(1)} %collective-permute-done.19.refs_2_.refs_10_, ...), custom_call_target="tpu_custom_call" | custom-call | flops 18874368 | bytes 4194304 | tf_op jit(solution)/shard_map/gram_rows/pallas_call | solution.py:109
  211.0 3.5 %collective-permute-done.26 = f32[80,128]{1,0:T(8,128)S(1)} collective-permute-done((f32[80,128]{1,0:T(8,128)S(1)}, f32[80,128]{1,0:T(8,128)S(1)}, u32[]{:S(2)}, u32[]{:S(2)}) %collective-permute-start.26) | collective-permute-done | bytes 40992 | tf_op jit(solution)/shard_map/ppermute | solution.py:16
  214.5 4.0 %collective-permute-done.27 = f32[80,128]{1,0:T(8,128)S(1)} collective-permute-done((f32[80,128]{1,0:T(8,128)S(1)}, f32[80,128]{1,0:T(8,128)S(1)}, u32[]{:S(2)}, u32[]{:S(2)}) %collective-permute-start.27) | collective-permute-done | bytes 40992 | tf_op jit(solution)/shard_map/ppermute | solution.py:16
  219.8 4.4 %collective-permute-done.28 = f32[80,128]{1,0:T(8,128)S(1)} collective-permute-done((f32[80,128]{1,0:T(8,128)S(1)}, f32[80,128]{1,0:T(8,128)S(1)}, u32[]{:S(2)}, u32[]{:S(2)}) %collective-permute-start.28) | collective-permute-done | bytes 40992 | tf_op jit(solution)/shard_map/ppermute | solution.py:16
  224.3 6.6 %combine.1 = bf16[2,256,1024]{2,1,0:T(8,128)(2,1)} custom-call(s32[1]{0:T(128)} %bitcast.rank_ref, f32[80,128]{1,0:T(8,128)S(1)} %add.19.gram_ref, bf16[256,1024]{1,0:T(8,128)(2,1)S(1)} %get-tuple-element.49.refs_0_, bf16[256,1024]{1,0:T(8,128)(2,1)S(1)} %collective-permute-done.9.refs_1_, bf16[256,1024]{1,0:T(8,128)(2,1)S(1)} %collective-permute-done.7.refs_2_, ...), custom_call_target="tpu_custom_call" | custom-call | flops 12582912 | bytes 9437184 | tf_op jit(solution)/shard_map/combine/pallas_call | solution.py:203
  (67 shorter events, 30.2 us)
Async XLA Ops:
  12.8 20.4 %collective-permute-start = (bf16[256,1024]{1,0:T(8,128)(2,1)}, bf16[256,1024]{1,0:T(8,128)(2,1)}, u32[]{:S(2)}, u32[]{:S(2)}) collective-permute-start(bf16[256,1024]{1,0:T(8,128)(2,1)} %get-tuple-element.54), channel_id=1, source_target_pairs={{0,4},{4,0},{8,12},{12,8},{16,20},{20,16},{24,28},{28,24},{1,5},{5... | collective-permute-start | bytes 1572872 | tf_op jit(solution)/shard_map/ppermute | solution.py:16
  15.7 36.7 %collective-permute-start.1 = (bf16[256,1024]{1,0:T(8,128)(2,1)S(1)}, bf16[256,1024]{1,0:T(8,128)(2,1)}, u32[]{:S(2)}, u32[]{:S(2)}) collective-permute-start(bf16[256,1024]{1,0:T(8,128)(2,1)S(1)} %get-tuple-element.55), channel_id=1, source_target_pairs={{0,8},{4,12},{8,0},{12,4},{16,24},{20,28},{24,16},{28,20},{1,9},{5... | collective-permute-start | bytes 1572872 | tf_op jit(solution)/shard_map/ppermute | solution.py:16
  17.3 35.1 %collective-permute-start.2 = (bf16[256,1024]{1,0:T(8,128)(2,1)S(1)}, bf16[256,1024]{1,0:T(8,128)(2,1)S(1)}, u32[]{:S(2)}, u32[]{:S(2)}) collective-permute-start(bf16[256,1024]{1,0:T(8,128)(2,1)S(1)} %get-tuple-element.56), channel_id=1, source_target_pairs={{0,24},{4,28},{8,16},{12,20},{16,8},{20,12},{24,0},{28,4},{1,25},{... | collective-permute-start | bytes 1572872 | tf_op jit(solution)/shard_map/ppermute | solution.py:16
  31.8 23.1 %collective-permute-start.12 = (bf16[256,1024]{1,0:T(8,128)(2,1)S(1)}, bf16[256,1024]{1,0:T(8,128)(2,1)}, u32[]{:S(2)}, u32[]{:S(2)}) collective-permute-start(bf16[256,1024]{1,0:T(8,128)(2,1)S(1)} %get-tuple-element.76), channel_id=1, source_target_pairs={{0,4},{4,0},{8,12},{12,8},{16,20},{20,16},{24,28},{28,24},{1,5},{5... | collective-permute-start | bytes 1572872 | tf_op jit(solution)/shard_map/ppermute | solution.py:16
  32.4 43.5 %collective-permute-start.13 = (bf16[256,1024]{1,0:T(8,128)(2,1)S(1)}, bf16[256,1024]{1,0:T(8,128)(2,1)}, u32[]{:S(2)}, u32[]{:S(2)}) collective-permute-start(bf16[256,1024]{1,0:T(8,128)(2,1)S(1)} %get-tuple-element.77), channel_id=1, source_target_pairs={{0,8},{4,12},{8,0},{12,4},{16,24},{20,28},{24,16},{28,20},{1,9},{5... | collective-permute-start | bytes 1572872 | tf_op jit(solution)/shard_map/ppermute | solution.py:16
  33.1 42.7 %collective-permute-start.14 = (bf16[256,1024]{1,0:T(8,128)(2,1)S(1)}, bf16[256,1024]{1,0:T(8,128)(2,1)S(1)}, u32[]{:S(2)}, u32[]{:S(2)}) collective-permute-start(bf16[256,1024]{1,0:T(8,128)(2,1)S(1)} %get-tuple-element.78), channel_id=1, source_target_pairs={{0,24},{4,28},{8,16},{12,20},{16,8},{20,12},{24,0},{28,4},{1,25},{... | collective-permute-start | bytes 1572872 | tf_op jit(solution)/shard_map/ppermute | solution.py:16
  52.4 25.3 %collective-permute-start.3 = (bf16[256,1024]{1,0:T(8,128)(2,1)}, bf16[256,1024]{1,0:T(8,128)(2,1)S(1)}, u32[]{:S(2)}, u32[]{:S(2)}) collective-permute-start(bf16[256,1024]{1,0:T(8,128)(2,1)} %collective-permute-done), channel_id=1, source_target_pairs={{0,8},{4,12},{8,0},{12,4},{16,24},{20,28},{24,16},{28,20},{1,9},{5... | collective-permute-start | bytes 1572872 | tf_op jit(solution)/shard_map/ppermute | solution.py:16
  53.4 26.2 %collective-permute-start.4 = (bf16[256,1024]{1,0:T(8,128)(2,1)S(1)}, bf16[256,1024]{1,0:T(8,128)(2,1)S(1)}, u32[]{:S(2)}, u32[]{:S(2)}) collective-permute-start(bf16[256,1024]{1,0:T(8,128)(2,1)S(1)} %get-tuple-element.58), channel_id=1, source_target_pairs={{0,4},{4,0},{8,12},{12,8},{16,20},{20,16},{24,28},{28,24},{1,5},{5... | collective-permute-start | bytes 1572872 | tf_op jit(solution)/shard_map/ppermute | solution.py:16
  54.9 34.1 %collective-permute-start.5 = (bf16[256,1024]{1,0:T(8,128)(2,1)}, bf16[256,1024]{1,0:T(8,128)(2,1)S(1)}, u32[]{:S(2)}, u32[]{:S(2)}) collective-permute-start(bf16[256,1024]{1,0:T(8,128)(2,1)} %collective-permute-done.1), channel_id=1, source_target_pairs={{0,24},{4,28},{8,16},{12,20},{16,8},{20,12},{24,0},{28,4},{1,25},{... | collective-permute-start | bytes 1572872 | tf_op jit(solution)/shard_map/ppermute | solution.py:16
  75.9 25.8 %collective-permute-start.15 = (bf16[256,1024]{1,0:T(8,128)(2,1)}, bf16[256,1024]{1,0:T(8,128)(2,1)S(1)}, u32[]{:S(2)}, u32[]{:S(2)}) collective-permute-start(bf16[256,1024]{1,0:T(8,128)(2,1)} %collective-permute-done.12), channel_id=1, source_target_pairs={{0,8},{4,12},{8,0},{12,4},{16,24},{20,28},{24,16},{28,20},{1,9},{5... | collective-permute-start | bytes 1572872 | tf_op jit(solution)/shard_map/ppermute | solution.py:16
  76.6 33.4 %collective-permute-start.16 = (bf16[256,1024]{1,0:T(8,128)(2,1)S(1)}, bf16[256,1024]{1,0:T(8,128)(2,1)S(1)}, u32[]{:S(2)}, u32[]{:S(2)}) collective-permute-start(bf16[256,1024]{1,0:T(8,128)(2,1)S(1)} %get-tuple-element.80), channel_id=1, source_target_pairs={{0,4},{4,0},{8,12},{12,8},{16,20},{20,16},{24,28},{28,24},{1,5},{5... | collective-permute-start | bytes 1572872 | tf_op jit(solution)/shard_map/ppermute | solution.py:16
  77.7 33.8 %collective-permute-start.17 = (bf16[256,1024]{1,0:T(8,128)(2,1)}, bf16[256,1024]{1,0:T(8,128)(2,1)S(1)}, u32[]{:S(2)}, u32[]{:S(2)}) collective-permute-start(bf16[256,1024]{1,0:T(8,128)(2,1)} %collective-permute-done.13), channel_id=1, source_target_pairs={{0,24},{4,28},{8,16},{12,20},{16,8},{20,12},{24,0},{28,4},{1,25},{... | collective-permute-start | bytes 1572872 | tf_op jit(solution)/shard_map/ppermute | solution.py:16
  89.0 23.1 %collective-permute-start.6 = (bf16[256,1024]{1,0:T(8,128)(2,1)S(1)}, bf16[256,1024]{1,0:T(8,128)(2,1)S(1)}, u32[]{:S(2)}, u32[]{:S(2)}) collective-permute-start(bf16[256,1024]{1,0:T(8,128)(2,1)S(1)} %get-tuple-element.60), channel_id=1, source_target_pairs={{0,4},{4,0},{8,12},{12,8},{16,20},{20,16},{24,28},{28,24},{1,5},{5... | collective-permute-start | bytes 1572872 | tf_op jit(solution)/shard_map/ppermute | solution.py:16
  89.5 33.3 %collective-permute-start.7 = (bf16[256,1024]{1,0:T(8,128)(2,1)S(1)}, bf16[256,1024]{1,0:T(8,128)(2,1)S(1)}, u32[]{:S(2)}, u32[]{:S(2)}) collective-permute-start(bf16[256,1024]{1,0:T(8,128)(2,1)S(1)} %get-tuple-element.62), channel_id=1, source_target_pairs={{0,8},{4,12},{8,0},{12,4},{16,24},{20,28},{24,16},{28,20},{1,9},{5... | collective-permute-start | bytes 1572872 | tf_op jit(solution)/shard_map/ppermute | solution.py:16
  101.7 32.4 %collective-permute-start.8 = (bf16[256,1024]{1,0:T(8,128)(2,1)S(1)}, bf16[256,1024]{1,0:T(8,128)(2,1)S(1)}, u32[]{:S(2)}, u32[]{:S(2)}) collective-permute-start(bf16[256,1024]{1,0:T(8,128)(2,1)S(1)} %collective-permute-done.3), channel_id=1, source_target_pairs={{0,24},{4,28},{8,16},{12,20},{16,8},{20,12},{24,0},{28,4},{1,25},{... | collective-permute-start | bytes 1572872 | tf_op jit(solution)/shard_map/ppermute | solution.py:16
  111.5 23.1 %collective-permute-start.18 = (bf16[256,1024]{1,0:T(8,128)(2,1)S(1)}, bf16[256,1024]{1,0:T(8,128)(2,1)S(1)}, u32[]{:S(2)}, u32[]{:S(2)}) collective-permute-start(bf16[256,1024]{1,0:T(8,128)(2,1)S(1)} %get-tuple-element.82), channel_id=1, source_target_pairs={{0,4},{4,0},{8,12},{12,8},{16,20},{20,16},{24,28},{28,24},{1,5},{5... | collective-permute-start | bytes 1572872 | tf_op jit(solution)/shard_map/ppermute | solution.py:16
  112.0 33.3 %collective-permute-start.19 = (bf16[256,1024]{1,0:T(8,128)(2,1)S(1)}, bf16[256,1024]{1,0:T(8,128)(2,1)S(1)}, u32[]{:S(2)}, u32[]{:S(2)}) collective-permute-start(bf16[256,1024]{1,0:T(8,128)(2,1)S(1)} %get-tuple-element.84), channel_id=1, source_target_pairs={{0,8},{4,12},{8,0},{12,4},{16,24},{20,28},{24,16},{28,20},{1,9},{5... | collective-permute-start | bytes 1572872 | tf_op jit(solution)/shard_map/ppermute | solution.py:16
  112.1 44.5 %collective-permute-start.20 = (bf16[256,1024]{1,0:T(8,128)(2,1)S(1)}, bf16[256,1024]{1,0:T(8,128)(2,1)S(1)}, u32[]{:S(2)}, u32[]{:S(2)}) collective-permute-start(bf16[256,1024]{1,0:T(8,128)(2,1)S(1)} %collective-permute-done.15), channel_id=1, source_target_pairs={{0,24},{4,28},{8,16},{12,20},{16,8},{20,12},{24,0},{28,4},{1,25},{... | collective-permute-start | bytes 1572872 | tf_op jit(solution)/shard_map/ppermute | solution.py:16
  134.0 23.1 %collective-permute-start.9 = (bf16[256,1024]{1,0:T(8,128)(2,1)S(1)}, bf16[256,1024]{1,0:T(8,128)(2,1)S(1)}, u32[]{:S(2)}, u32[]{:S(2)}) collective-permute-start(bf16[256,1024]{1,0:T(8,128)(2,1)S(1)} %get-tuple-element.64), channel_id=1, source_target_pairs={{0,4},{4,0},{8,12},{12,8},{16,20},{20,16},{24,28},{28,24},{1,5},{5... | collective-permute-start | bytes 1572872 | tf_op jit(solution)/shard_map/ppermute | solution.py:16
  134.6 33.2 %collective-permute-start.10 = (bf16[256,1024]{1,0:T(8,128)(2,1)S(1)}, bf16[256,1024]{1,0:T(8,128)(2,1)S(1)}, u32[]{:S(2)}, u32[]{:S(2)}) collective-permute-start(bf16[256,1024]{1,0:T(8,128)(2,1)S(1)} %collective-permute-done.6), channel_id=1, source_target_pairs={{0,8},{4,12},{8,0},{12,4},{16,24},{20,28},{24,16},{28,20},{1,9},{5... | collective-permute-start | bytes 1572872 | tf_op jit(solution)/shard_map/ppermute | solution.py:16
  134.6 44.5 %collective-permute-start.11 = (bf16[256,1024]{1,0:T(8,128)(2,1)S(1)}, bf16[256,1024]{1,0:T(8,128)(2,1)S(1)}, u32[]{:S(2)}, u32[]{:S(2)}) collective-permute-start(bf16[256,1024]{1,0:T(8,128)(2,1)S(1)} %collective-permute-done.4), channel_id=1, source_target_pairs={{0,24},{4,28},{8,16},{12,20},{16,8},{20,12},{24,0},{28,4},{1,25},{... | collective-permute-start | bytes 1572872 | tf_op jit(solution)/shard_map/ppermute | solution.py:16
  156.5 27.6 %collective-permute-start.21 = (bf16[256,1024]{1,0:T(8,128)(2,1)S(1)}, bf16[256,1024]{1,0:T(8,128)(2,1)S(1)}, u32[]{:S(2)}, u32[]{:S(2)}) collective-permute-start(bf16[256,1024]{1,0:T(8,128)(2,1)S(1)} %get-tuple-element.86), channel_id=1, source_target_pairs={{0,4},{4,0},{8,12},{12,8},{16,20},{20,16},{24,28},{28,24},{1,5},{5... | collective-permute-start | bytes 1572872 | tf_op jit(solution)/shard_map/ppermute | solution.py:16
  157.1 32.6 %collective-permute-start.22 = (bf16[256,1024]{1,0:T(8,128)(2,1)S(1)}, bf16[256,1024]{1,0:T(8,128)(2,1)S(1)}, u32[]{:S(2)}, u32[]{:S(2)}) collective-permute-start(bf16[256,1024]{1,0:T(8,128)(2,1)S(1)} %collective-permute-done.18), channel_id=1, source_target_pairs={{0,8},{4,12},{8,0},{12,4},{16,24},{20,28},{24,16},{28,20},{1,9},{5... | collective-permute-start | bytes 1572872 | tf_op jit(solution)/shard_map/ppermute | solution.py:16
  157.1 43.0 %collective-permute-start.23 = (bf16[256,1024]{1,0:T(8,128)(2,1)S(1)}, bf16[256,1024]{1,0:T(8,128)(2,1)S(1)}, u32[]{:S(2)}, u32[]{:S(2)}) collective-permute-start(bf16[256,1024]{1,0:T(8,128)(2,1)S(1)} %collective-permute-done.16), channel_id=1, source_target_pairs={{0,24},{4,28},{8,16},{12,20},{16,8},{20,12},{24,0},{28,4},{1,25},{... | collective-permute-start | bytes 1572872 | tf_op jit(solution)/shard_map/ppermute | solution.py:16
  (14 other events, 651.8 us)

commit v2 on v0

v2 whole, which is shorter than its diff:
```python
import jax
import jax.numpy as jnp
from jax import lax
from jax.experimental import pallas as pl
from jax.experimental.pallas import tpu as pltpu
from jax.sharding import PartitionSpec as P

epsilon = 1e-06
VMEM_LIMIT = 40 * 1024 * 1024
LANES = 128
STRIDE = 16
GROUP = 4
GRAM_ROWS = 16


def exchange(value, axis, mask):
    return lax.ppermute(value, axis, [(i, i ^ mask) for i in range(lax.axis_size(axis))])


def tied(values, others):
    joined = lax.optimization_barrier(tuple(values) + tuple(others))
    return list(joined[: len(values)]), list(joined[len(values) :])


def call(kernel, name, rank, inputs, outputs, flops):
    size = sum(x.size * x.dtype.itemsize for x in list(inputs) + list(outputs))
    return pl.pallas_call(
        kernel,
        in_specs=[pl.BlockSpec(memory_space=pltpu.SMEM)]
        + [pl.BlockSpec(memory_space=pltpu.VMEM)] * len(inputs),
        out_specs=[pl.BlockSpec(memory_space=pltpu.VMEM)] * len(outputs),
        out_shape=list(outputs),
        compiler_params=pltpu.CompilerParams(vmem_limit_bytes=VMEM_LIMIT),
        cost_estimate=pl.CostEstimate(flops=flops, bytes_accessed=size, transcendentals=0),
        name=name,
    )(rank, *inputs)


def pair_row(first, second):
    low, high = jnp.minimum(first, second), jnp.maximum(first, second)
    return low * (2 * GROUP - 1 - low) // 2 + high


def tiles(rows, width, step, start):
    def body(index, carry):
        where = pl.ds(pl.multiple_of(index * STRIDE, STRIDE), STRIDE)
        for column in range(0, width, LANES):
            carry = step(where, slice(column, column + LANES), carry)
        return carry

    return lax.fori_loop(0, rows // STRIDE, body, start)


def gram_rows(rank, parts, before):
    rows, width = parts[0].shape
    pairs = [(u, v) for u in range(GROUP) for v in range(u, GROUP)]

    def kernel(rank_ref, *refs):
        ins, old, out = refs[:GROUP], refs[GROUP], refs[GROUP + 1]

        def step(where, columns, totals):
            wide = [ref[where, columns].astype(jnp.float32) for ref in ins]
            new = []
            for total, (u, v) in zip(totals, pairs):
                product = wide[u] * wide[v]
                new.append(total + (product[:8] + product[8:]))
            return tuple(new)

        zero = jnp.zeros((8, LANES), jnp.float32)
        totals = tiles(rows, width, step, (zero,) * len(pairs))
        out[...] = old[...]
        mine = rank_ref[0] & (GROUP - 1)
        for total, (u, v) in zip(totals, pairs):
            row = pl.ds(pair_row(mine ^ u, mine ^ v), 1)
            out[row, :] = out[row, :] + jnp.sum(total, axis=0, keepdims=True)

    shape = jax.ShapeDtypeStruct((GRAM_ROWS, LANES), jnp.float32)
    flops = 2 * len(pairs) * rows * width
    return call(kernel, "gram_rows", rank, list(parts) + [before], [shape], flops)[0]


def scale_pair(dot_value, norm_first, norm_second):
    return (
        1.0 - dot_value / (2.0 * (norm_first + epsilon)),
        1.0 - dot_value / (2.0 * (norm_second + epsilon)),
    )


def weighted(first_scale, first_part, second_scale, second_part):
    result = first_scale * first_part.astype(jnp.float32)
    result = result + second_scale * second_part.astype(jnp.float32)
    return result.astype(jnp.bfloat16)


def group_combine(rank, gram, block_parts):
    rows, width = block_parts[0][0].shape

    def kernel(rank_ref, gram_ref, *refs):
        ins, outs = refs[: GROUP * len(block_parts)], refs[GROUP * len(block_parts) :]
        sums = jnp.sum(gram_ref[...], axis=1, keepdims=True)

        def entry(i, j):
            low, high = min(i, j), max(i, j)
            row = low * (2 * GROUP - 1 - low) // 2 + high
            return sums[row : row + 1]

        def norm(i, j, left, right):
            value = left * left * entry(i, i) + right * right * entry(j, j)
            return jnp.maximum(value + 2.0 * (left * right * entry(i, j)), 0.0)

        low_first, low_second = scale_pair(entry(0, 1), entry(0, 0), entry(1, 1))
        high_first, high_second = scale_pair(entry(2, 3), entry(2, 2), entry(3, 3))
        dot_value = (
            low_first * high_first * entry(0, 2)
            + low_first * high_second * entry(0, 3)
            + low_second * high_first * entry(1, 2)
            + low_second * high_second * entry(1, 3)
        )
        norm_low = norm(0, 1, low_first, low_second)
        norm_high = norm(2, 3, high_first, high_second)
        top_first, top_second = scale_pair(dot_value, norm_low, norm_high)

        odd = (rank_ref[0] & 1) == 1
        upper = (rank_ref[0] & 2) == 2
        low_first, low_second = (
            jnp.where(odd, low_second, low_first),
            jnp.where(odd, low_first, low_second),
        )
        high_first, high_second = (
            jnp.where(odd, high_second, high_first),
            jnp.where(odd, high_first, high_second),
        )
        scales = [
            jnp.where(upper, high_first, low_first),
            jnp.where(upper, high_second, low_second),
            jnp.where(upper, low_first, high_first),
            jnp.where(upper, low_second, high_second),
            jnp.where(upper, top_second, top_first),
            jnp.where(upper, top_first, top_second),
        ]
        scales = [jnp.broadcast_to(scale, (STRIDE, LANES)) for scale in scales]

        for number, out in enumerate(outs):
            block = ins[GROUP * number : GROUP * (number + 1)]

            def step(where, columns, carry, out=out, block=block):
                held = [ref[where, columns] for ref in block]
                near = weighted(scales[0], held[0], scales[1], held[1])
                far = weighted(scales[2], held[2], scales[3], held[3])
                out[where, columns] = weighted(scales[4], near, scales[5], far)
                return carry

            tiles(rows, width, step, 0)

    shape = jax.ShapeDtypeStruct((rows, width), jnp.bfloat16)
    inputs = [gram] + [part for parts in block_parts for part in parts]
    flops = 9 * len(block_parts) * rows * width
    return call(kernel, "group_combine", rank, inputs, [shape] * len(block_parts), flops)


def pair_rows(rank, kept, received, level, layer, before):
    rows, width = kept[0].shape

    def kernel(rank_ref, *refs):
        count = len(kept)
        mine, theirs, old, out = refs[:count], refs[count : 2 * count], refs[-2], refs[-1]
        totals = (jnp.zeros((8, LANES), jnp.float32),) * 3
        for left, right in zip(mine, theirs):

            def step(where, columns, totals, left=left, right=right):
                a, b = left[where, columns].astype(jnp.float32), right[where, columns].astype(jnp.float32)
                new = [
                    total + (product[:8] + product[8:])
                    for total, product in zip(totals, (a * b, a * a, b * b))
                ]
                return tuple(new)

            totals = tiles(rows, width, step, totals)
        upper = ((rank_ref[0] >> level) & 1) == 1
        dot_value, norm_mine, norm_theirs = [jnp.sum(t, axis=0, keepdims=True) for t in totals]
        out[...] = old[...]
        base = 3 * layer
        out[base : base + 1, :] = dot_value
        out[base + 1 : base + 2, :] = jnp.where(upper, norm_theirs, norm_mine)
        out[base + 2 : base + 3, :] = jnp.where(upper, norm_mine, norm_theirs)

    shape = jax.ShapeDtypeStruct(before.shape, jnp.float32)
    inputs = list(kept) + list(received) + [before]
    flops = 6 * len(kept) * rows * width
    return call(kernel, "pair_rows", rank, inputs, [shape], flops)[0]


def pair_combine(rank, sums, kept, received, level):
    layers, count = len(kept), len(kept[0])
    rows, width = kept[0][0].shape

    def kernel(rank_ref, sums_ref, *refs):
        ins, outs = refs[: 2 * layers * count], refs[2 * layers * count :]
        totals = jnp.sum(sums_ref[...], axis=1, keepdims=True)
        upper = ((rank_ref[0] >> level) & 1) == 1
        for layer in range(layers):
            dot_value, norm_first, norm_second = [
                totals[3 * layer + k : 3 * layer + k + 1] for k in range(3)
            ]
            first, second = scale_pair(dot_value, norm_first, norm_second)
            mine = jnp.broadcast_to(jnp.where(upper, second, first), (STRIDE, LANES))
            theirs = jnp.broadcast_to(jnp.where(upper, first, second), (STRIDE, LANES))
            for number in range(count):
                left, right = ins[2 * (layer * count + number) :][:2]
                out = outs[number]

                def step(where, columns, carry, left=left, right=right, out=out):
                    out[layer, where, columns] = weighted(
                        mine, left[where, columns], theirs, right[where, columns]
                    )
                    return carry

                tiles(rows, width, step, 0)

    shape = jax.ShapeDtypeStruct((layers, rows, width), jnp.bfloat16)
    inputs = [sums]
    for layer in range(layers):
        for left, right in zip(kept[layer], received[layer]):
            inputs += [left, right]
    flops = 3 * layers * count * rows * width
    return call(kernel, "pair_combine", rank, inputs, [shape] * count, flops)


def level_masks(levels):
    masks = [1 << level for level in range(levels)]
    if levels >= 3:
        masks[-1] |= masks[-2]
    return masks


def spread(code, masks):
    value = 0
    for bit, mask in enumerate(masks):
        if code >> bit & 1:
            value ^= mask
    return value


def body(activations, output_grads):
    replicas = lax.axis_size("rep")
    par = lax.axis_size("par")
    levels = replicas.bit_length() - 1
    layers, tokens, width = activations.shape
    rows = width // replicas
    rank = lax.axis_index("rep")
    position = jnp.reshape(rank, (1,)).astype(jnp.int32)
    masks = level_masks(levels)
    tails = [tail << 2 for tail in reversed(range(replicas // GROUP))]

    def near_pair(layer, code):
        first = ((rank ^ spread(code, masks)) >> 1) * (2 * rows)
        columns = lax.dynamic_slice(activations, (layer, 0, first), (1, tokens, 2 * rows))[0]
        product = lax.dot_general(
            columns,
            output_grads[layer],
            (((0,), (0,)), ((), ())),
            preferred_element_type=jnp.float32,
        ).astype(jnp.bfloat16)
        side = (rank ^ spread(code, masks)) & 1
        return (
            lax.dynamic_slice_in_dim(product, side * rows, rows, 0),
            lax.dynamic_slice_in_dim(product, (1 - side) * rows, rows, 0),
        )

    own, crossed, far, far_crossed = {}, {}, {}, {}
    rounds = []
    for layer in range(layers):
        codes = [2 | tail for tail in tails] + tails
        second = [("own", 2 | tail) for tail in tails] + [("crossed", 2 | tail) for tail in tails]
        rounds += [(layer, code, unit) for code, unit in zip(codes, second)]

    grams = []
    flying = []

    def land():
        layer, code, unit = flying.pop(0)
        return layer, code, unit

    def settle(sends):
        layer, code, (kind, block) = flying.pop(0)
        target = far if kind == "own" else far_crossed
        key, other = (layer, code), (layer, block ^ 2)
        sends, (crossed[key], target[other]) = tied(sends, [crossed[key], target[other]])
        return sends

    sums = [jnp.zeros((GRAM_ROWS, LANES), jnp.float32) for _ in range(layers)]

    def gather(layer, tail):
        key = (layer, tail)
        parts = [own[key], crossed[key], far[key], far_crossed[key]]
        sums[layer] = gram_rows(position, parts, sums[layer])

    for layer, code, (kind, block) in rounds:
        own[layer, code], sent = near_pair(layer, code)
        passed = own[layer, block] if kind == "own" else crossed[layer, block]
        if len(flying) == 2:
            sent, passed = settle([sent, passed])
        crossed[layer, code] = exchange(sent, "rep", masks[0])
        target = far if kind == "own" else far_crossed
        target[layer, block ^ 2] = exchange(passed, "rep", masks[1])
        flying.append((layer, code, (kind, block)))

    spans = []
    stride = 1
    while stride < par:
        spans.append(("par", stride))
        stride *= 2

    for layer in range(layers):
        for tail in tails:
            gather(layer, tail)
    combined = []
    for layer in range(layers):
        last = layer == layers - 1
        near = [("rep", masks[0])]
        hops = [("rep", masks[1])] + spans + near if last else spans + near + [("rep", masks[1])]
        for axis, mask in hops:
            sums[layer] = sums[layer] + exchange(sums[layer], axis, mask)
        parts = [
            [held[layer, tail] for held in (own, crossed, far, far_crossed)] for tail in tails
        ]
        combined.append(dict(zip(tails, group_combine(position, sums[layer], parts))))

    for level in range(2, levels):
        keep = [tail for tail in tails if not tail >> level & 1 and tail in combined[0]]
        totals = jnp.zeros((-(-3 * layers // 8) * 8, LANES), jnp.float32)
        kept, received = [], []
        for layer in range(layers):
            kept.append([combined[layer][tail] for tail in keep])
            received.append(
                [
                    exchange(combined[layer][tail | 1 << level], "rep", masks[level])
                    for tail in keep
                ]
            )
            totals = pair_rows(position, kept[layer], received[layer], level, layer, totals)
        for axis, mask in spans + [("rep", mask) for mask in masks[: level + 1]]:
            totals = totals + exchange(totals, axis, mask)
        results = pair_combine(position, totals, kept, received, level)
        if level < levels - 1:
            combined = [
                {tail: result[layer] for tail, result in zip(keep, results)} for layer in range(layers)
            ]
    return results[0]


def solution(mesh):
    return jax.shard_map(
        body,
        mesh=mesh,
        in_specs=(P(None, "rep", "par"), P(None, "rep", None)),
        out_specs=P(None, ("par", "rep"), None),
        check_vma=False,
    )
```

time: 283 us -> 191 us (0.67)
  waiting for transfers between devices: 190 us -> 78.5 us
  starting transfers between devices: 18.7 us -> 58.4 us
  other arithmetic: 32.2 us -> 0.04 us
  blocking collectives: 17.6 us -> 0 us
  matrix products: 22.8 us -> 40.4 us
  Pallas kernels: 0 us -> 9.46 us
    ppermute x9 -> x31, waiting for transfers between devices: 190 us -> 78.5 us  [exchange(): lax.ppermute(value, axis, [(i, i ^ mask) for i in range(lax.axis_size(axi...]
    ppermute x9 -> x31, starting transfers between devices: 18.7 us -> 58.4 us  [exchange(): lax.ppermute(value, axis, [(i, i ^ mask) for i in range(lax.axis_size(axi...]
    psum x3 -> x0, blocking collectives: 17.6 us -> none  [body(): statistics = lax.psum(statistics, 'par')]
    dot_general x1 -> x8, matrix products: 22.8 us -> 40.4 us  [near_pair(): lax.dot_general(columns, output_grads[layer], (((0,), (0,)), ((), ())), p...]
    reduce_sum x3 -> x0, other arithmetic: 16.1 us -> none  [pair_statistics(): jnp.sum(first_wide * second_wide, axis=(1, 2))]
    convert_element_type x3 -> x0, other arithmetic: 10.1 us -> none  [combine_parts(): return result.astype(jnp.bfloat16)]
    pallas_call x0 -> x9, Pallas kernels: none -> 9.46 us  [call(): pl.pallas_call(kernel, in_specs=[pl.BlockSpec(memory_space=pltpu.SMEM)] +...]
    select_n x3 -> x0, other arithmetic: 5.89 us -> none  [the longest x2 5.78 us: body(): kept_part = jnp.where(is_upper, higher_part, lower_part)]
  transfers between devices with their start and end apart: 9 -> 31, of which waited for: 9 -> 24; matrix products, arithmetic and copies ran while one was open for 0% -> 20% of each run, Pallas kernels for 0% -> 4%
where the time goes in v2:
time: 191 us
  waiting for transfers between devices  78.5 us (41%)
  starting transfers between devices  58.4 us (31%)
  matrix products  40.4 us (21%)
  Pallas kernels  9.46 us (5%)
  local copies, waits for them, and re-layouts  3.58 us (2%)
    ppermute x31, waiting for transfers between devices, exchange(): lax.ppermute(value, axis, [(i, i ^ mask) for i in range(lax.axis_size(axi...  78.5 us
    ppermute x31, starting transfers between devices, exchange(): lax.ppermute(value, axis, [(i, i ^ mask) for i in range(lax.axis_size(axi...  58.4 us
    dot_general x8, matrix products, near_pair(): lax.dot_general(columns, output_grads[layer], (((0,), (0,)), ((), ())), p...  40.4 us
    pallas_call x9, Pallas kernels, call(): pl.pallas_call(kernel, in_specs=[pl.BlockSpec(memory_space=pltpu.SMEM)] +...  9.46 us
  transfers between devices with their start and end apart: 31, of which 24 were waited for; matrix products, arithmetic and copies ran while one was open for 20% of the time, Pallas kernels for 4%

profile of v2, /device:TPU:0, one launch (start us, length us, event | category | flops | bytes accessed | tf_op | source)
XLA Modules:
  0.0 190.6 jit_solution(9811913829342529751)
XLA Ops:
  0.0 5.2 %fusion.75 = bf16[512,1024]{1,0:T(8,128)(2,1)S(1)} fusion(bf16[2,2048,1024]{2,1,0:T(8,128)(2,1)} %param.3, bf16[2,2048,2048]{2,1,0:T(8,128)(2,1)} %param.2, s32[]{:T(128)S(6)} %select_n.57), kind=kOutput, calls=%fused_computation.47 | convolution fusion | flops 2148007936 | bytes 7340036 | tf_op jit(solution)/shard_map/dot_general | solution.py:258
  6.2 2.9 %collective-permute-start.8 = (bf16[256,1024]{1,0:T(8,128)(2,1)}, bf16[256,1024]{1,0:T(8,128)(2,1)}, u32[]{:S(2)}, u32[]{:S(2)}) collective-permute-start(bf16[256,1024]{1,0:T(8,128)(2,1)} %get-tuple-element.58), channel_id=1, source_target_pairs={{0,4},{4,0},{8,12},{12,8},{16,20},{20,16},{24,28},{28,24},{1,5},{5... | collective-permute-start | bytes 1572872 | tf_op jit(solution)/shard_map/ppermute | solution.py:17
  10.8 5.2 %fusion.65 = bf16[512,1024]{1,0:T(8,128)(2,1)S(1)} fusion(bf16[2,2048,1024]{2,1,0:T(8,128)(2,1)} %param.3, bf16[2,2048,2048]{2,1,0:T(8,128)(2,1)} %param.2, s32[]{:T(128)S(6)} %select_n.51), kind=kOutput, calls=%fused_computation.45 | convolution fusion | flops 2148007936 | bytes 7340036 | tf_op jit(solution)/shard_map/dot_general | solution.py:258
  17.5 5.2 %fusion.55 = bf16[512,1024]{1,0:T(8,128)(2,1)S(1)} fusion(bf16[2,2048,1024]{2,1,0:T(8,128)(2,1)} %param.3, bf16[2,2048,2048]{2,1,0:T(8,128)(2,1)} %param.2, s32[]{:T(128)S(6)} %select_n.57), kind=kOutput, calls=%fused_computation.43 | convolution fusion | flops 2148007936 | bytes 7340036 | tf_op jit(solution)/shard_map/dot_general | solution.py:258
  22.7 6.2 %fusion.45 = bf16[512,1024]{1,0:T(8,128)(2,1)} fusion(bf16[2,2048,1024]{2,1,0:T(8,128)(2,1)} %param.3, bf16[2,2048,2048]{2,1,0:T(8,128)(2,1)} %param.2, s32[]{:T(128)S(6)} %select_n.51), kind=kOutput, calls=%fused_computation.41 | convolution fusion | flops 2148007936 | bytes 7340036 | tf_op jit(solution)/shard_map/dot_general | solution.py:258
  28.9 5.3 %fusion.70 = bf16[512,1024]{1,0:T(8,128)(2,1)S(1)} fusion(bf16[2,2048,1024]{2,1,0:T(8,128)(2,1)} %param.3, bf16[2,2048,2048]{2,1,0:T(8,128)(2,1)} %param.2, s32[]{:T(128)S(6)} %select_n.54), kind=kOutput, calls=%fused_computation.46 | convolution fusion | flops 2148007936 | bytes 7340036 | tf_op jit(solution)/shard_map/dot_general | solution.py:258
  35.4 5.3 %fusion.60 = bf16[512,1024]{1,0:T(8,128)(2,1)S(1)} fusion(bf16[2,2048,1024]{2,1,0:T(8,128)(2,1)} %param.3, bf16[2,2048,2048]{2,1,0:T(8,128)(2,1)} %param.2, s32[]{:T(128)S(6)} %select_n.48), kind=kOutput, calls=%fused_computation.44 | convolution fusion | flops 2148007936 | bytes 7340036 | tf_op jit(solution)/shard_map/dot_general | solution.py:258
  45.1 4.1 %fusion.50 = bf16[512,1024]{1,0:T(8,128)(2,1)S(1)} fusion(bf16[2,2048,1024]{2,1,0:T(8,128)(2,1)S(1)} %bitcast.76, bf16[2,2048,2048]{2,1,0:T(8,128)(2,1)} %param.2, s32[]{:T(128)S(6)} %select_n.54), kind=kOutput, calls=%fused_computation.42 | convolution fusion | flops 2148007936 | bytes 7340036 | tf_op jit(solution)/shard_map/dot_general | solution.py:258
  49.3 6.5 %collective-permute-done.10.refs_1_ = bf16[256,1024]{1,0:T(8,128)(2,1)S(1)} collective-permute-done((bf16[256,1024]{1,0:T(8,128)(2,1)S(1)}, bf16[256,1024]{1,0:T(8,128)(2,1)S(1)}, u32[]{:S(2)}, u32[]{:S(2)}) %collective-permute-start.10) | collective-permute-done | bytes 524320 | tf_op jit(solution)/shard_map/ppermute | solution.py:17
  55.8 2.1 %collective-permute-done.11.refs_3_ = bf16[256,1024]{1,0:T(8,128)(2,1)S(1)} collective-permute-done((bf16[256,1024]{1,0:T(8,128)(2,1)}, bf16[256,1024]{1,0:T(8,128)(2,1)S(1)}, u32[]{:S(2)}, u32[]{:S(2)}) %collective-permute-start.11) | collective-permute-done | bytes 524320 | tf_op jit(solution)/shard_map/ppermute | solution.py:17
  58.0 7.0 %collective-permute-done.2.refs_1_.refs_5_ = bf16[256,1024]{1,0:T(8,128)(2,1)S(1)} collective-permute-done((bf16[256,1024]{1,0:T(8,128)(2,1)S(1)}, bf16[256,1024]{1,0:T(8,128)(2,1)S(1)}, u32[]{:S(2)}, u32[]{:S(2)}) %collective-permute-start.2) | collective-permute-done | bytes 524320 | tf_op jit(solution)/shard_map/ppermute | solution.py:17
  70.7 3.9 %fusion.40 = bf16[512,1024]{1,0:T(8,128)(2,1)S(1)} fusion(bf16[2,2048,1024]{2,1,0:T(8,128)(2,1)S(1)} %bitcast.76, bf16[2,2048,2048]{2,1,0:T(8,128)(2,1)} %param.2, s32[]{:T(128)S(6)} %select_n.48), kind=kOutput, calls=%fused_computation.40 | convolution fusion | flops 2148007936 | bytes 7340036 | tf_op jit(solution)/shard_map/dot_general | solution.py:258
  74.6 6.9 %collective-permute-done.12 = bf16[256,1024]{1,0:T(8,128)(2,1)S(1)} collective-permute-done((bf16[256,1024]{1,0:T(8,128)(2,1)S(1)}, bf16[256,1024]{1,0:T(8,128)(2,1)S(1)}, u32[]{:S(2)}, u32[]{:S(2)}) %collective-permute-start.12) | collective-permute-done | bytes 524320 | tf_op jit(solution)/shard_map/ppermute | solution.py:17
  85.1 7.6 %collective-permute-done.4 = bf16[256,1024]{1,0:T(8,128)(2,1)S(1)} collective-permute-done((bf16[256,1024]{1,0:T(8,128)(2,1)S(1)}, bf16[256,1024]{1,0:T(8,128)(2,1)S(1)}, u32[]{:S(2)}, u32[]{:S(2)}) %collective-permute-start.4) | collective-permute-done | bytes 524320 | tf_op jit(solution)/shard_map/ppermute | solution.py:17
  98.4 5.6 %collective-permute-done.14.refs_1_ = bf16[256,1024]{1,0:T(8,128)(2,1)S(1)} collective-permute-done((bf16[256,1024]{1,0:T(8,128)(2,1)S(1)}, bf16[256,1024]{1,0:T(8,128)(2,1)S(1)}, u32[]{:S(2)}, u32[]{:S(2)}) %collective-permute-start.14) | collective-permute-done | bytes 524320 | tf_op jit(solution)/shard_map/ppermute | solution.py:17
  105.3 6.4 %collective-permute-done.6.refs_1_.refs_5_ = bf16[256,1024]{1,0:T(8,128)(2,1)S(1)} collective-permute-done((bf16[256,1024]{1,0:T(8,128)(2,1)S(1)}, bf16[256,1024]{1,0:T(8,128)(2,1)S(1)}, u32[]{:S(2)}, u32[]{:S(2)}) %collective-permute-start.6) | collective-permute-done | bytes 524320 | tf_op jit(solution)/shard_map/ppermute | solution.py:17
  127.0 2.5 %collective-permute-start.25 = (bf16[256,1024]{1,0:T(8,128)(2,1)S(1)}, bf16[256,1024]{1,0:T(8,128)(2,1)S(1)}, u32[]{:S(2)}, u32[]{:S(2)}) collective-permute-start(bf16[256,1024]{1,0:T(8,128)(2,1)S(1)} %get-tuple-element.52), channel_id=1, source_target_pairs={{0,24},{4,28},{8,16},{12,20},{16,8},{20,12},{24,0},{28,4},{1,25},{... | collective-permute-start | bytes 1572872 | tf_op jit(solution)/shard_map/ppermute | solution.py:17
  132.6 11.3 %collective-permute-done.25.refs_1_ = bf16[256,1024]{1,0:T(8,128)(2,1)S(1)} collective-permute-done((bf16[256,1024]{1,0:T(8,128)(2,1)S(1)}, bf16[256,1024]{1,0:T(8,128)(2,1)S(1)}, u32[]{:S(2)}, u32[]{:S(2)}) %collective-permute-start.25) | collective-permute-done | bytes 524320 | tf_op jit(solution)/shard_map/ppermute | solution.py:17
  144.2 6.8 %collective-permute-done.20.refs_1_.refs_3_ = bf16[256,1024]{1,0:T(8,128)(2,1)S(1)} collective-permute-done((bf16[256,1024]{1,0:T(8,128)(2,1)S(1)}, bf16[256,1024]{1,0:T(8,128)(2,1)S(1)}, u32[]{:S(2)}, u32[]{:S(2)}) %collective-permute-start.20) | collective-permute-done | bytes 524320 | tf_op jit(solution)/shard_map/ppermute | solution.py:17
  154.1 2.1 %collective-permute-done.27 = f32[8,128]{1,0:T(8,128)S(1)} collective-permute-done((f32[8,128]{1,0:T(8,128)S(1)}, f32[8,128]{1,0:T(8,128)S(1)}, u32[]{:S(2)}, u32[]{:S(2)}) %collective-permute-start.27) | collective-permute-done | bytes 4128 | tf_op jit(solution)/shard_map/ppermute | solution.py:17
  157.7 2.1 %collective-permute-done.28 = f32[8,128]{1,0:T(8,128)S(1)} collective-permute-done((f32[8,128]{1,0:T(8,128)S(1)}, f32[8,128]{1,0:T(8,128)S(1)}, u32[]{:S(2)}, u32[]{:S(2)}) %collective-permute-start.28) | collective-permute-done | bytes 4128 | tf_op jit(solution)/shard_map/ppermute | solution.py:17
  159.8 22.1 %collective-permute-start.29 = (f32[8,128]{1,0:T(8,128)S(1)}, f32[8,128]{1,0:T(8,128)S(1)}, u32[]{:S(2)}, u32[]{:S(2)}) collective-permute-start(f32[8,128]{1,0:T(8,128)S(1)} %add.109), channel_id=1, source_target_pairs={{0,8},{4,12},{8,0},{12,4},{16,24},{20,28},{24,16},{28,20},{1,9},{5... | collective-permute-start | bytes 12296 | tf_op jit(solution)/shard_map/ppermute | solution.py:17
  183.5 2.3 %collective-permute-start.30 = (f32[8,128]{1,0:T(8,128)S(1)}, f32[8,128]{1,0:T(8,128)S(1)}, u32[]{:S(2)}, u32[]{:S(2)}) collective-permute-start(f32[8,128]{1,0:T(8,128)S(1)} %add.110), channel_id=1, source_target_pairs={{0,24},{4,28},{8,16},{12,20},{16,8},{20,12},{24,0},{28,4},{1,25},{... | collective-permute-start | bytes 12296 | tf_op jit(solution)/shard_map/ppermute | solution.py:17
  185.8 3.1 %collective-permute-done.30 = f32[8,128]{1,0:T(8,128)S(1)} collective-permute-done((f32[8,128]{1,0:T(8,128)S(1)}, f32[8,128]{1,0:T(8,128)S(1)}, u32[]{:S(2)}, u32[]{:S(2)}) %collective-permute-start.30) | collective-permute-done | bytes 4128 | tf_op jit(solution)/shard_map/ppermute | solution.py:17
  (89 shorter events, 52.8 us)
Async XLA Ops:
  6.2 34.6 %collective-permute-start.8 = (bf16[256,1024]{1,0:T(8,128)(2,1)}, bf16[256,1024]{1,0:T(8,128)(2,1)}, u32[]{:S(2)}, u32[]{:S(2)}) collective-permute-start(bf16[256,1024]{1,0:T(8,128)(2,1)} %get-tuple-element.58), channel_id=1, source_target_pairs={{0,4},{4,0},{8,12},{12,8},{16,20},{20,16},{24,28},{28,24},{1,5},{5... | collective-permute-start | bytes 1572872 | tf_op jit(solution)/shard_map/ppermute | solution.py:17
  9.2 31.7 %collective-permute-start.9 = (bf16[256,1024]{1,0:T(8,128)(2,1)}, bf16[256,1024]{1,0:T(8,128)(2,1)S(1)}, u32[]{:S(2)}, u32[]{:S(2)}) collective-permute-start(bf16[256,1024]{1,0:T(8,128)(2,1)} %get-tuple-element.57), channel_id=1, source_target_pairs={{0,8},{4,12},{8,0},{12,4},{16,24},{20,28},{24,16},{28,20},{1,9},{5... | collective-permute-start | bytes 1572872 | tf_op jit(solution)/shard_map/ppermute | solution.py:17
  17.0 27.5 %collective-permute-start = (bf16[256,1024]{1,0:T(8,128)(2,1)}, bf16[256,1024]{1,0:T(8,128)(2,1)}, u32[]{:S(2)}, u32[]{:S(2)}) collective-permute-start(bf16[256,1024]{1,0:T(8,128)(2,1)} %get-tuple-element.64), channel_id=1, source_target_pairs={{0,4},{4,0},{8,12},{12,8},{16,20},{20,16},{24,28},{28,24},{1,5},{5... | collective-permute-start | bytes 1572872 | tf_op jit(solution)/shard_map/ppermute | solution.py:17
  17.5 26.9 %collective-permute-start.1 = (bf16[256,1024]{1,0:T(8,128)(2,1)}, bf16[256,1024]{1,0:T(8,128)(2,1)S(1)}, u32[]{:S(2)}, u32[]{:S(2)}) collective-permute-start(bf16[256,1024]{1,0:T(8,128)(2,1)} %get-tuple-element.63), channel_id=1, source_target_pairs={{0,8},{4,12},{8,0},{12,4},{16,24},{20,28},{24,16},{28,20},{1,9},{5... | collective-permute-start | bytes 1572872 | tf_op jit(solution)/shard_map/ppermute | solution.py:17
  40.9 14.9 %collective-permute-start.10 = (bf16[256,1024]{1,0:T(8,128)(2,1)S(1)}, bf16[256,1024]{1,0:T(8,128)(2,1)S(1)}, u32[]{:S(2)}, u32[]{:S(2)}) collective-permute-start(bf16[256,1024]{1,0:T(8,128)(2,1)S(1)} %get-tuple-element.36), channel_id=1, source_target_pairs={{0,4},{4,0},{8,12},{12,8},{16,20},{20,16},{24,28},{28,24},{1,5},{5... | collective-permute-start | bytes 1572872 | tf_op jit(solution)/shard_map/ppermute | solution.py:17
  42.9 15.1 %collective-permute-start.11 = (bf16[256,1024]{1,0:T(8,128)(2,1)}, bf16[256,1024]{1,0:T(8,128)(2,1)S(1)}, u32[]{:S(2)}, u32[]{:S(2)}) collective-permute-start(bf16[256,1024]{1,0:T(8,128)(2,1)} %collective-permute-done.8), channel_id=1, source_target_pairs={{0,8},{4,12},{8,0},{12,4},{16,24},{20,28},{24,16},{28,20},{1,9},{5... | collective-permute-start | bytes 1572872 | tf_op jit(solution)/shard_map/ppermute | solution.py:17
  44.5 20.5 %collective-permute-start.2 = (bf16[256,1024]{1,0:T(8,128)(2,1)S(1)}, bf16[256,1024]{1,0:T(8,128)(2,1)S(1)}, u32[]{:S(2)}, u32[]{:S(2)}) collective-permute-start(bf16[256,1024]{1,0:T(8,128)(2,1)S(1)} %get-tuple-element.29), channel_id=1, source_target_pairs={{0,4},{4,0},{8,12},{12,8},{16,20},{20,16},{24,28},{28,24},{1,5},{5... | collective-permute-start | bytes 1572872 | tf_op jit(solution)/shard_map/ppermute | solution.py:17
  45.1 21.5 %collective-permute-start.3 = (bf16[256,1024]{1,0:T(8,128)(2,1)}, bf16[256,1024]{1,0:T(8,128)(2,1)S(1)}, u32[]{:S(2)}, u32[]{:S(2)}) collective-permute-start(bf16[256,1024]{1,0:T(8,128)(2,1)} %collective-permute-done), channel_id=1, source_target_pairs={{0,8},{4,12},{8,0},{12,4},{16,24},{20,28},{24,16},{28,20},{1,9},{5... | collective-permute-start | bytes 1572872 | tf_op jit(solution)/shard_map/ppermute | solution.py:17
  66.6 14.9 %collective-permute-start.12 = (bf16[256,1024]{1,0:T(8,128)(2,1)S(1)}, bf16[256,1024]{1,0:T(8,128)(2,1)S(1)}, u32[]{:S(2)}, u32[]{:S(2)}) collective-permute-start(bf16[256,1024]{1,0:T(8,128)(2,1)S(1)} %copy-done.2), channel_id=1, source_target_pairs={{0,4},{4,0},{8,12},{12,8},{16,20},{20,16},{24,28},{28,24},{1,5},{5... | collective-permute-start | bytes 1572872 | tf_op jit(solution)/shard_map/ppermute | solution.py:17
  67.0 14.9 %collective-permute-start.13 = (bf16[256,1024]{1,0:T(8,128)(2,1)S(1)}, bf16[256,1024]{1,0:T(8,128)(2,1)S(1)}, u32[]{:S(2)}, u32[]{:S(2)}) collective-permute-start(bf16[256,1024]{1,0:T(8,128)(2,1)S(1)} %copy-done.1), channel_id=1, source_target_pairs={{0,8},{4,12},{8,0},{12,4},{16,24},{20,28},{24,16},{28,20},{1,9},{5... | collective-permute-start | bytes 1572872 | tf_op jit(solution)/shard_map/ppermute | solution.py:17
  68.7 24.0 %collective-permute-start.4 = (bf16[256,1024]{1,0:T(8,128)(2,1)S(1)}, bf16[256,1024]{1,0:T(8,128)(2,1)S(1)}, u32[]{:S(2)}, u32[]{:S(2)}) collective-permute-start(bf16[256,1024]{1,0:T(8,128)(2,1)S(1)} %get-tuple-element.31), channel_id=1, source_target_pairs={{0,4},{4,0},{8,12},{12,8},{16,20},{20,16},{24,28},{28,24},{1,5},{5... | collective-permute-start | bytes 1572872 | tf_op jit(solution)/shard_map/ppermute | solution.py:17
  70.2 22.9 %collective-permute-start.5 = (bf16[256,1024]{1,0:T(8,128)(2,1)S(1)}, bf16[256,1024]{1,0:T(8,128)(2,1)S(1)}, u32[]{:S(2)}, u32[]{:S(2)}) collective-permute-start(bf16[256,1024]{1,0:T(8,128)(2,1)S(1)} %get-tuple-element.32), channel_id=1, source_target_pairs={{0,8},{4,12},{8,0},{12,4},{16,24},{20,28},{24,16},{28,20},{1,9},{5... | collective-permute-start | bytes 1572872 | tf_op jit(solution)/shard_map/ppermute | solution.py:17
  81.8 22.1 %collective-permute-start.14 = (bf16[256,1024]{1,0:T(8,128)(2,1)S(1)}, bf16[256,1024]{1,0:T(8,128)(2,1)S(1)}, u32[]{:S(2)}, u32[]{:S(2)}) collective-permute-start(bf16[256,1024]{1,0:T(8,128)(2,1)S(1)} %get-tuple-element.40), channel_id=1, source_target_pairs={{0,4},{4,0},{8,12},{12,8},{16,20},{20,16},{24,28},{28,24},{1,5},{5... | collective-permute-start | bytes 1572872 | tf_op jit(solution)/shard_map/ppermute | solution.py:17
  83.5 20.8 %collective-permute-start.15 = (bf16[256,1024]{1,0:T(8,128)(2,1)S(1)}, bf16[256,1024]{1,0:T(8,128)(2,1)S(1)}, u32[]{:S(2)}, u32[]{:S(2)}) collective-permute-start(bf16[256,1024]{1,0:T(8,128)(2,1)S(1)} %collective-permute-done.12), channel_id=1, source_target_pairs={{0,8},{4,12},{8,0},{12,4},{16,24},{20,28},{24,16},{28,20},{1,9},{5... | collective-permute-start | bytes 1572872 | tf_op jit(solution)/shard_map/ppermute | solution.py:17
  93.1 18.6 %collective-permute-start.6 = (bf16[256,1024]{1,0:T(8,128)(2,1)S(1)}, bf16[256,1024]{1,0:T(8,128)(2,1)S(1)}, u32[]{:S(2)}, u32[]{:S(2)}) collective-permute-start(bf16[256,1024]{1,0:T(8,128)(2,1)S(1)} %get-tuple-element.33), channel_id=1, source_target_pairs={{0,4},{4,0},{8,12},{12,8},{16,20},{20,16},{24,28},{28,24},{1,5},{5... | collective-permute-start | bytes 1572872 | tf_op jit(solution)/shard_map/ppermute | solution.py:17
  94.7 17.3 %collective-permute-start.7 = (bf16[256,1024]{1,0:T(8,128)(2,1)S(1)}, bf16[256,1024]{1,0:T(8,128)(2,1)S(1)}, u32[]{:S(2)}, u32[]{:S(2)}) collective-permute-start(bf16[256,1024]{1,0:T(8,128)(2,1)S(1)} %collective-permute-done.4), channel_id=1, source_target_pairs={{0,8},{4,12},{8,0},{12,4},{16,24},{20,28},{24,16},{28,20},{1,9},{5... | collective-permute-start | bytes 1572872 | tf_op jit(solution)/shard_map/ppermute | solution.py:17
  98.3 16.2 %collective-permute-start.21 = (f32[16,128]{1,0:T(8,128)S(1)}, f32[16,128]{1,0:T(8,128)S(1)}, u32[]{:S(2)}, u32[]{:S(2)}) collective-permute-start(f32[16,128]{1,0:T(8,128)S(1)} %gram_rows.7), channel_id=1, source_target_pairs={{0,1},{1,0},{2,3},{3,2},{4,5},{5,4},{6,7},{7,6},{8,9},{9,8},{10,11... | collective-permute-start | bytes 24584 | tf_op jit(solution)/shard_map/ppermute | solution.py:17
  113.0 3.7 %collective-permute-start.16 = (f32[16,128]{1,0:T(8,128)S(1)}, f32[16,128]{1,0:T(8,128)S(1)}, u32[]{:S(2)}, u32[]{:S(2)}) collective-permute-start(f32[16,128]{1,0:T(8,128)S(1)} %gram_rows.5), channel_id=1, source_target_pairs={{0,8},{4,12},{8,0},{12,4},{16,24},{20,28},{24,16},{28,20},{1,9},{5... | collective-permute-start | bytes 24584 | tf_op jit(solution)/shard_map/ppermute | solution.py:17
  114.5 3.7 %collective-permute-start.22 = (f32[16,128]{1,0:T(8,128)S(1)}, f32[16,128]{1,0:T(8,128)S(1)}, u32[]{:S(2)}, u32[]{:S(2)}) collective-permute-start(f32[16,128]{1,0:T(8,128)S(1)} %add.103), channel_id=1, source_target_pairs={{0,2},{1,3},{2,0},{3,1},{4,6},{5,7},{6,4},{7,5},{8,10},{9,11},{10,... | collective-permute-start | bytes 24584 | tf_op jit(solution)/shard_map/ppermute | solution.py:17
  123.3 6.2 %collective-permute-start.19 = (f32[16,128]{1,0:T(8,128)S(1)}, f32[16,128]{1,0:T(8,128)S(1)}, u32[]{:S(2)}, u32[]{:S(2)}) collective-permute-start(f32[16,128]{1,0:T(8,128)S(1)} %add.101), channel_id=1, source_target_pairs={{0,4},{4,0},{8,12},{12,8},{16,20},{20,16},{24,28},{28,24},{1,5},{5... | collective-permute-start | bytes 24584 | tf_op jit(solution)/shard_map/ppermute | solution.py:17
  127.0 16.8 %collective-permute-start.25 = (bf16[256,1024]{1,0:T(8,128)(2,1)S(1)}, bf16[256,1024]{1,0:T(8,128)(2,1)S(1)}, u32[]{:S(2)}, u32[]{:S(2)}) collective-permute-start(bf16[256,1024]{1,0:T(8,128)(2,1)S(1)} %get-tuple-element.52), channel_id=1, source_target_pairs={{0,24},{4,28},{8,16},{12,20},{16,8},{20,12},{24,0},{28,4},{1,25},{... | collective-permute-start | bytes 1572872 | tf_op jit(solution)/shard_map/ppermute | solution.py:17
  131.1 19.8 %collective-permute-start.20 = (bf16[256,1024]{1,0:T(8,128)(2,1)S(1)}, bf16[256,1024]{1,0:T(8,128)(2,1)S(1)}, u32[]{:S(2)}, u32[]{:S(2)}) collective-permute-start(bf16[256,1024]{1,0:T(8,128)(2,1)S(1)} %get-tuple-element.44), channel_id=1, source_target_pairs={{0,24},{4,28},{8,16},{12,20},{16,8},{20,12},{24,0},{28,4},{1,25},{... | collective-permute-start | bytes 1572872 | tf_op jit(solution)/shard_map/ppermute | solution.py:17
  159.8 23.7 %collective-permute-start.29 = (f32[8,128]{1,0:T(8,128)S(1)}, f32[8,128]{1,0:T(8,128)S(1)}, u32[]{:S(2)}, u32[]{:S(2)}) collective-permute-start(f32[8,128]{1,0:T(8,128)S(1)} %add.109), channel_id=1, source_target_pairs={{0,8},{4,12},{8,0},{12,4},{16,24},{20,28},{24,16},{28,20},{1,9},{5... | collective-permute-start | bytes 12296 | tf_op jit(solution)/shard_map/ppermute | solution.py:17
  183.5 5.4 %collective-permute-start.30 = (f32[8,128]{1,0:T(8,128)S(1)}, f32[8,128]{1,0:T(8,128)S(1)}, u32[]{:S(2)}, u32[]{:S(2)}) collective-permute-start(f32[8,128]{1,0:T(8,128)S(1)} %add.110), channel_id=1, source_target_pairs={{0,24},{4,28},{8,16},{12,20},{16,8},{20,12},{24,0},{28,4},{1,25},{... | collective-permute-start | bytes 12296 | tf_op jit(solution)/shard_map/ppermute | solution.py:17
  (12 other events, 92.8 us)

commit v3 on v2

v3 whole, which is shorter than its diff:
```python
import jax
import jax.numpy as jnp
from jax import lax
from jax.experimental import pallas as pl
from jax.experimental.pallas import tpu as pltpu
from jax.sharding import PartitionSpec as P

epsilon = 1e-06
LARGE_LIMIT = 60 * 1024 * 1024
SMALL_LIMIT = 16 * 1024 * 1024
LANES = 128
STRIDE = 16
GROUP = 4
GRAM_ROWS = 16
COST = 1024
BLOCK_COST = 1_600_000_000
GRAM_COST = 3_200_000_000
CROSS_COST = 4_000_000_000


def exchange(value, axis, mask):
    return lax.ppermute(value, axis, [(i, i ^ mask) for i in range(lax.axis_size(axis))])


def tied(values, others):
    joined = lax.optimization_barrier(tuple(values) + tuple(others))
    return list(joined[: len(values)]), list(joined[len(values) :])


def call(kernel, name, rank, inputs, outputs, flops=COST):
    return pl.pallas_call(
        kernel,
        in_specs=[pl.BlockSpec(memory_space=pltpu.SMEM)]
        + [pl.BlockSpec(memory_space=pltpu.VMEM)] * len(inputs),
        out_specs=[pl.BlockSpec(memory_space=pltpu.VMEM)] * len(outputs),
        out_shape=list(outputs),
        compiler_params=pltpu.CompilerParams(vmem_limit_bytes=SMALL_LIMIT),
        cost_estimate=pl.CostEstimate(flops=flops, bytes_accessed=COST, transcendentals=0),
        name=name,
    )(rank, *inputs)


def block_pair(rank, activations, output_grads, layer, offset, rows):
    tokens, width_out = output_grads.shape[1:]
    columns = min(512, width_out)

    def kernel(rank_ref, a_ref, b_ref, kept, sent, product):
        product[...] = lax.dot_general(
            a_ref[0], b_ref[0], (((0,), (0,)), ((), ())), preferred_element_type=jnp.float32
        )
        side = (rank_ref[0] ^ offset) & 1
        kept[...] = product[pl.ds(pl.multiple_of(side * rows, rows), rows), :].astype(jnp.bfloat16)
        sent[...] = product[pl.ds(pl.multiple_of((1 - side) * rows, rows), rows), :].astype(jnp.bfloat16)

    shape = jax.ShapeDtypeStruct((rows, width_out), jnp.bfloat16)
    return pl.pallas_call(
        kernel,
        grid_spec=pltpu.PrefetchScalarGridSpec(
            num_scalar_prefetch=1,
            grid=(width_out // columns,),
            in_specs=[
                pl.BlockSpec((1, tokens, 2 * rows), lambda j, rank: (layer, 0, (rank[0] ^ offset) >> 1)),
                pl.BlockSpec((1, tokens, columns), lambda j, rank: (layer, 0, j)),
            ],
            out_specs=[pl.BlockSpec((rows, columns), lambda j, rank: (0, j))] * 2,
            scratch_shapes=[pltpu.VMEM((2 * rows, columns), jnp.float32)],
        ),
        out_shape=[shape, shape],
        compiler_params=pltpu.CompilerParams(vmem_limit_bytes=LARGE_LIMIT),
        cost_estimate=pl.CostEstimate(flops=BLOCK_COST, bytes_accessed=COST, transcendentals=0),
        name="block_pair",
    )(rank, activations, output_grads)


def pair_row(first, second):
    low, high = jnp.minimum(first, second), jnp.maximum(first, second)
    return low * (2 * GROUP - 1 - low) // 2 + high


def tiles(rows, width, step, start):
    def body(index, carry):
        where = pl.ds(pl.multiple_of(index * STRIDE, STRIDE), STRIDE)
        for column in range(0, width, LANES):
            carry = step(where, slice(column, column + LANES), carry)
        return carry

    return lax.fori_loop(0, rows // STRIDE, body, start)


def gram_rows(rank, parts, before, cost):
    rows, width = parts[0].shape
    pairs = [(u, v) for u in range(GROUP) for v in range(u, GROUP)]

    def kernel(rank_ref, *refs):
        ins, out = refs[:GROUP], refs[-1]

        def step(where, columns, totals):
            wide = [ref[where, columns].astype(jnp.float32) for ref in ins]
            new = []
            for total, (u, v) in zip(totals, pairs):
                product = wide[u] * wide[v]
                new.append(total + (product[:8] + product[8:]))
            return tuple(new)

        zero = jnp.zeros((8, LANES), jnp.float32)
        totals = tiles(rows, width, step, (zero,) * len(pairs))
        out[...] = jnp.zeros_like(out) if before is None else refs[GROUP][...]
        mine = rank_ref[0] & (GROUP - 1)
        for total, (u, v) in zip(totals, pairs):
            row = pl.ds(pair_row(mine ^ u, mine ^ v), 1)
            out[row, :] = out[row, :] + jnp.sum(total, axis=0, keepdims=True)

    shape = jax.ShapeDtypeStruct((GRAM_ROWS, LANES), jnp.float32)
    inputs = list(parts) + ([] if before is None else [before])
    return call(kernel, "gram_rows", rank, inputs, [shape], cost)[0]


def total(values, cost):
    def kernel(*refs):
        parts = [ref[...] for ref in refs[:-1]]
        while len(parts) > 1:
            parts = [left + right for left, right in zip(parts[::2], parts[1::2])]
        refs[-1][...] = parts[0]

    return pl.pallas_call(
        kernel,
        in_specs=[pl.BlockSpec(memory_space=pltpu.VMEM)] * len(values),
        out_specs=pl.BlockSpec(memory_space=pltpu.VMEM),
        out_shape=jax.ShapeDtypeStruct(values[0].shape, values[0].dtype),
        compiler_params=pltpu.CompilerParams(vmem_limit_bytes=SMALL_LIMIT),
        cost_estimate=pl.CostEstimate(flops=cost, bytes_accessed=COST, transcendentals=0),
        name="total",
    )(*values)


def scale_pair(dot_value, norm_first, norm_second):
    return (
        1.0 - dot_value / (2.0 * (norm_first + epsilon)),
        1.0 - dot_value / (2.0 * (norm_second + epsilon)),
    )


def weighted(first_scale, first_part, second_scale, second_part):
    result = first_scale * first_part.astype(jnp.float32)
    result = result + second_scale * second_part.astype(jnp.float32)
    return result.astype(jnp.bfloat16)


def group_combine(rank, gram, block_parts):
    rows, width = block_parts[0][0].shape

    def kernel(rank_ref, gram_ref, *refs):
        ins, outs = refs[: GROUP * len(block_parts)], refs[GROUP * len(block_parts) :]
        sums = jnp.sum(gram_ref[...], axis=1, keepdims=True)

        def entry(i, j):
            low, high = min(i, j), max(i, j)
            row = low * (2 * GROUP - 1 - low) // 2 + high
            return sums[row : row + 1]

        def norm(i, j, left, right):
            value = left * left * entry(i, i) + right * right * entry(j, j)
            return jnp.maximum(value + 2.0 * (left * right * entry(i, j)), 0.0)

        low_first, low_second = scale_pair(entry(0, 1), entry(0, 0), entry(1, 1))
        high_first, high_second = scale_pair(entry(2, 3), entry(2, 2), entry(3, 3))
        dot_value = (
            low_first * high_first * entry(0, 2)
            + low_first * high_second * entry(0, 3)
            + low_second * high_first * entry(1, 2)
            + low_second * high_second * entry(1, 3)
        )
        norm_low = norm(0, 1, low_first, low_second)
        norm_high = norm(2, 3, high_first, high_second)
        top_first, top_second = scale_pair(dot_value, norm_low, norm_high)

        odd = (rank_ref[0] & 1) == 1
        upper = (rank_ref[0] & 2) == 2
        low_first, low_second = (
            jnp.where(odd, low_second, low_first),
            jnp.where(odd, low_first, low_second),
        )
        high_first, high_second = (
            jnp.where(odd, high_second, high_first),
            jnp.where(odd, high_first, high_second),
        )
        scales = [
            jnp.where(upper, high_first, low_first),
            jnp.where(upper, high_second, low_second),
            jnp.where(upper, low_first, high_first),
            jnp.where(upper, low_second, high_second),
            jnp.where(upper, top_second, top_first),
            jnp.where(upper, top_first, top_second),
        ]
        scales = [jnp.broadcast_to(scale, (STRIDE, LANES)) for scale in scales]

        for number, out in enumerate(outs):
            block = ins[GROUP * number : GROUP * (number + 1)]

            def step(where, columns, carry, out=out, block=block):
                held = [ref[where, columns] for ref in block]
                near = weighted(scales[0], held[0], scales[1], held[1])
                far = weighted(scales[2], held[2], scales[3], held[3])
                out[where, columns] = weighted(scales[4], near, scales[5], far)
                return carry

            tiles(rows, width, step, 0)

    shape = jax.ShapeDtypeStruct((rows, width), jnp.bfloat16)
    inputs = [gram] + [part for parts in block_parts for part in parts]
    return call(kernel, "group_combine", rank, inputs, [shape] * len(block_parts))


def chosen_rows(rank_ref, level, candidates, where, columns):
    if len(candidates) == 1:
        return candidates[0][where, columns]
    middle = ((rank_ref[0] >> level) & 1) != ((rank_ref[0] >> (level - 1)) & 1)
    return jnp.where(middle, candidates[0][where, columns], candidates[1][where, columns])


def pair_rows(rank, kept, received, level, layer, layers, before):
    rows, width = kept[0].shape
    count, ways = len(kept), len(received[0])

    def kernel(rank_ref, *refs):
        mine, out = refs[:count], refs[-1]
        totals = (jnp.zeros((8, LANES), jnp.float32),) * 3
        for number, left in enumerate(mine):
            theirs = refs[count + ways * number :][:ways]

            def step(where, columns, totals, left=left, theirs=theirs):
                a = left[where, columns].astype(jnp.float32)
                b = chosen_rows(rank_ref, level, theirs, where, columns).astype(jnp.float32)
                new = [
                    total + (product[:8] + product[8:])
                    for total, product in zip(totals, (a * b, a * a, b * b))
                ]
                return tuple(new)

            totals = tiles(rows, width, step, totals)
        upper = ((rank_ref[0] >> level) & 1) == 1
        dot_value, norm_mine, norm_theirs = [jnp.sum(t, axis=0, keepdims=True) for t in totals]
        out[...] = jnp.zeros_like(out) if before is None else refs[-2][...]
        base = 3 * layer
        out[base : base + 1, :] = dot_value
        out[base + 1 : base + 2, :] = jnp.where(upper, norm_theirs, norm_mine)
        out[base + 2 : base + 3, :] = jnp.where(upper, norm_mine, norm_theirs)

    shape = jax.ShapeDtypeStruct((-(-3 * layers // 8) * 8, LANES), jnp.float32)
    inputs = list(kept) + [part for parts in received for part in parts]
    inputs += [] if before is None else [before]
    return call(kernel, "pair_rows", rank, inputs, [shape])[0]


def pair_combine(rank, sums, kept, received, level):
    layers, count = len(kept), len(kept[0])
    ways = len(received[0][0])
    rows, width = kept[0][0].shape

    def kernel(rank_ref, sums_ref, *refs):
        ins, outs = refs[:-count], refs[-count:]
        totals = jnp.sum(sums_ref[...], axis=1, keepdims=True)
        upper = ((rank_ref[0] >> level) & 1) == 1
        for layer in range(layers):
            dot_value, norm_first, norm_second = [
                totals[3 * layer + k : 3 * layer + k + 1] for k in range(3)
            ]
            first, second = scale_pair(dot_value, norm_first, norm_second)
            mine = jnp.broadcast_to(jnp.where(upper, second, first), (STRIDE, LANES))
            theirs = jnp.broadcast_to(jnp.where(upper, first, second), (STRIDE, LANES))
            for number in range(count):
                left, *others = ins[(1 + ways) * (layer * count + number) :][: 1 + ways]
                out = outs[number]

                def step(where, columns, carry, left=left, others=others, out=out):
                    right = chosen_rows(rank_ref, level, others, where, columns)
                    out[layer, where, columns] = weighted(mine, left[where, columns], theirs, right)
                    return carry

                tiles(rows, width, step, 0)

    shape = jax.ShapeDtypeStruct((layers, rows, width), jnp.bfloat16)
    inputs = [sums]
    for layer in range(layers):
        for left, others in zip(kept[layer], received[layer]):
            inputs += [left] + list(others)
    return call(kernel, "pair_combine", rank, inputs, [shape] * count)


def level_masks(levels):
    masks = [1 << level for level in range(levels)]
    if levels >= 3:
        masks[-1] |= masks[-2]
    return masks


def spread(code, masks):
    value = 0
    for bit, mask in enumerate(masks):
        if code >> bit & 1:
            value ^= mask
    return value


def swap(value, mask, middle=None):
    pairs = [(i, i ^ mask) for i in range(lax.axis_size("rep"))]
    if middle is not None:
        high = mask.bit_length() - 1
        pairs = [(i, j) for i, j in pairs if ((i >> high & 1) != (i >> (high - 1) & 1)) == middle]
    return lax.ppermute(value, "rep", pairs)


def body(activations, output_grads):
    replicas = lax.axis_size("rep")
    par = lax.axis_size("par")
    levels = replicas.bit_length() - 1
    layers, tokens, width = activations.shape
    rows = width // replicas
    rank = lax.axis_index("rep")
    position = jnp.reshape(rank, (1,)).astype(jnp.int32)
    masks = level_masks(levels)
    tails = [tail << 2 for tail in reversed(range(replicas // GROUP))]

    def near_pair(inputs, layer, code):
        return block_pair(position, inputs, output_grads, layer, spread(code, masks), rows)

    own, crossed, far, far_crossed = {}, {}, {}, {}
    rounds = []
    for layer in range(layers):
        codes = [2 | tail for tail in tails] + tails
        second = [(own, far, 2 | tail) for tail in tails]
        second += [(crossed, far_crossed, 2 | tail) for tail in tails]
        rounds += [(layer, code) + unit for code, unit in zip(codes, second)]
    window = 2

    def settle(number, sends):
        layer, code, _, target, block = rounds[number]
        key, other = (layer, code), (layer, block ^ 2)
        sends, (crossed[key], target[other]) = tied(sends, [crossed[key], target[other]])
        return sends

    spans = []
    stride = 1
    while stride < par:
        spans.append(("par", stride))
        stride *= 2

    def summed(value, hops):
        for axis, mask in hops:
            value = value + exchange(value, axis, mask)
        return value

    def layer_gram(layer):
        gram = None
        for tail in tails:
            parts = [held[layer, tail] for held in (own, crossed, far, far_crossed)]
            cost = GRAM_COST if layer == layers - 1 else COST
            gram = gram_rows(position, parts, gram, cost)
        return gram

    def group_result(layer, gram):
        parts = [
            [held[layer, tail] for held in (own, crossed, far, far_crossed)] for tail in tails
        ]
        return dict(zip(tails, group_combine(position, gram, parts)))

    def receive(blocks, level, middle):
        mask = masks[level]
        sends = [blocks[tail | 1 << level] for tail in blocks if not tail >> level & 1]
        if mask == 1 << level:
            return [[swap(sent, mask)] if middle else [] for sent in sends]
        return [[swap(sent, mask, middle)] for sent in sends]

    def receive_all(blocks, level):
        return [a + b for a, b in zip(receive(blocks, level, True), receive(blocks, level, False))]

    def tied_ways(values, ways):
        flat = [part for way in ways for part in way]
        values, flat = tied(values, flat)
        return values, [[flat.pop(0) for _ in way] for way in ways]

    inputs = activations
    per_layer = len(rounds) // layers
    combined, received = [], []
    for number in range(len(rounds)):
        layer, code, source, target, block = rounds[number]
        if number >= 2 * window:
            (inputs,) = settle(number - 2 * window, [inputs])
        own[layer, code], sent = near_pair(inputs, layer, code)
        passed = source[layer, block]
        if number >= window:
            sent, passed = settle(number - window, [sent, passed])
        done, step = divmod(number - window + 1, per_layer)
        if done >= 1 and step == 0:
            gram = layer_gram(done - 1)
            gram = total(
                [gram] + [exchange(gram, "rep", mask) for mask in range(1, GROUP)], CROSS_COST
            )
            combined.append(group_result(done - 1, summed(gram, spans)))
            received.append(receive(combined[-1], 2, True))
        crossed[layer, code] = exchange(sent, "rep", masks[0])
        target[layer, block ^ 2] = exchange(passed, "rep", masks[1])

    first = (layers - 1, tails[0])
    for layer in range(layers - 1):
        names = list(combined[layer])
        values, (own[first],) = tied([combined[layer][tail] for tail in names], [own[first]])
        combined[layer] = dict(zip(names, values))
    gram = summed(layer_gram(layers - 1), [("rep", masks[1])])
    for layer in range(layers - 1):
        names = list(combined[layer])
        values, (gram,) = tied([combined[layer][tail] for tail in names], [gram])
        combined[layer] = dict(zip(names, values))
        outer = receive(combined[layer], 2, False)
        gram = summed(gram, spans[:1])
        (gram,), received[layer] = tied_ways([gram], received[layer])
        received[layer] = [a + b for a, b in zip(received[layer], outer)]
    gram = summed(gram, (spans[1:] if layers > 1 else spans) + [("rep", masks[0])])
    combined.append(group_result(layers - 1, gram))
    names = list(combined[-1])
    values = [combined[-1][tail] for tail in names]
    for layer in range(layers - 1):
        values, received[layer] = tied_ways(values, received[layer])
    combined[-1] = dict(zip(names, values))
    received.append(receive_all(combined[-1], 2))

    for level in range(2, levels):
        keep = [tail for tail in tails if not tail >> level & 1 and tail in combined[0]]
        kept = [[combined[layer][tail] for tail in keep] for layer in range(layers)]
        totals = None
        for layer in range(layers):
            totals = pair_rows(position, kept[layer], received[layer], level, layer, layers, totals)
        totals = summed(totals, spans + [("rep", 1 << bit) for bit in range(level + 1)])
        results = pair_combine(position, totals, kept, received, level)
        if level < levels - 1:
            combined = [
                {tail: result[layer] for tail, result in zip(keep, results)} for layer in range(layers)
            ]
            received = [receive_all(combined[layer], level + 1) for layer in range(layers)]
    return results[0]


def solution(mesh):
    return jax.shard_map(
        body,
        mesh=mesh,
        in_specs=(P(None, "rep", "par"), P(None, "rep", None)),
        out_specs=P(None, ("par", "rep"), None),
        check_vma=False,
    )
```

time: 191 us -> 166 us (0.87)
  Pallas kernels: 9.46 us -> 62.4 us
  matrix products: 40.4 us -> 0 us
  waiting for transfers between devices: 78.5 us -> 56.7 us
  starting transfers between devices: 58.4 us -> 46.1 us
  local copies, waits for them, and re-layouts: 3.58 us -> 0.01 us
    pallas_call x0 -> x9, Pallas kernels: none -> 46.7 us  [the longest x8 46.7 us: block_pair(): pl.pallas_call(kernel, grid_spec=pltpu.PrefetchScalarGridSpec(num_scalar_...]
    dot_general x8 -> x0, matrix products: 40.4 us -> none  [near_pair(): lax.dot_general(columns, output_grads[layer], (((0,), (0,)), ((), ())), p...]
    ppermute x31 -> x30, waiting for transfers between devices: 78.5 us -> 43.4 us  [exchange(): lax.ppermute(value, axis, [(i, i ^ mask) for i in range(lax.axis_size(axi...]
    ppermute x31 -> x30, starting transfers between devices: 58.4 us -> 36.9 us  [exchange(): lax.ppermute(value, axis, [(i, i ^ mask) for i in range(lax.axis_size(axi...]
    ppermute x0 -> x4, waiting for transfers between devices: none -> 13.3 us  [swap(): return lax.ppermute(value, 'rep', pairs)]
    ppermute x0 -> x4, starting transfers between devices: none -> 9.19 us  [swap(): return lax.ppermute(value, 'rep', pairs)]
    pallas_call x9, Pallas kernels: 9.46 us -> 15.7 us  [call(): pl.pallas_call(kernel, in_specs=[pl.BlockSpec(memory_space=pltpu.SMEM)] +...]
    dynamic_slice x8 -> x0, local copies, waits for them, and re-layouts: 3.55 us -> none  [the longest x6 3.41 us: near_pair(): lax.dynamic_slice_in_dim(product, side * rows, rows, 0)]
  transfers between devices with their start and end apart: 31 -> 34, of which waited for: 24 -> 20; matrix products, arithmetic and copies ran while one was open for 20% -> 0% of each run, Pallas kernels for 4% -> 33%
where the time goes in v3:
time: 166 us; the launch traced here: 165 us
  Pallas kernels  62.4 us (38%)
  waiting for transfers between devices  56.7 us (34%)
  starting transfers between devices  46.1 us (28%)
    pallas_call x8, Pallas kernels, block_pair(): pl.pallas_call(kernel, grid_spec=pltpu.PrefetchScalarGridSpec(num_scalar_...  46.7 us
    ppermute x30, waiting for transfers between devices, exchange(): lax.ppermute(value, axis, [(i, i ^ mask) for i in range(lax.axis_size(axi...  43.4 us
    ppermute x30, starting transfers between devices, exchange(): lax.ppermute(value, axis, [(i, i ^ mask) for i in range(lax.axis_size(axi...  36.9 us
    pallas_call x9, Pallas kernels, call(): pl.pallas_call(kernel, in_specs=[pl.BlockSpec(memory_space=pltpu.SMEM)] +...  15.7 us
    ppermute x4, waiting for transfers between devices, swap(): return lax.ppermute(value, 'rep', pairs)  13.3 us
    ppermute x4, starting transfers between devices, swap(): return lax.ppermute(value, 'rep', pairs)  9.19 us
  transfers between devices with their start and end apart: 34, of which 20 were waited for; matrix products, arithmetic and copies ran while one was open for 0% of the time, Pallas kernels for 33%

profile of v3, /device:TPU:0, one launch (start us, length us, event | category | flops | bytes accessed | tf_op | source)
XLA Modules:
  0.0 165.4 jit_solution(10805477145022011856)
XLA Ops:
  0.0 5.8 %block_pair.10 = (bf16[256,1024]{1,0:T(8,128)(2,1)}, bf16[256,1024]{1,0:T(8,128)(2,1)}) custom-call(s32[1]{0:T(128)} %bitcast.rank_ref, bf16[2,2048,2048]{2,1,0:T(8,128)(2,1)} %a_ref.11, bf16[2,2048,1024]{2,1,0:T(8,128)(2,1)} %b_ref.15), custom_call_target="tpu_custom_call" | custom-call | flops 1600000000 | bytes 1024 | tf_op jit(solution)/shard_map/block_pair/pallas_call | solution.py:56
  5.8 2.9 %collective-permute-start = (bf16[256,1024]{1,0:T(8,128)(2,1)}, bf16[256,1024]{1,0:T(8,128)(2,1)}, u32[]{:S(2)}, u32[]{:S(2)}) collective-permute-start(bf16[256,1024]{1,0:T(8,128)(2,1)} %get-tuple-element.65), channel_id=1, source_target_pairs={{0,4},{4,0},{8,12},{12,8},{16,20},{20,16},{24,28},{28,24},{1,5},{5... | collective-permute-start | bytes 1572872 | tf_op jit(solution)/shard_map/ppermute | solution.py:22
  10.3 5.8 %block_pair.11 = (bf16[256,1024]{1,0:T(8,128)(2,1)}, bf16[256,1024]{1,0:T(8,128)(2,1)}) custom-call(s32[1]{0:T(128)} %bitcast.rank_ref, bf16[2,2048,2048]{2,1,0:T(8,128)(2,1)} %a_ref.11, bf16[2,2048,1024]{2,1,0:T(8,128)(2,1)} %b_ref.15), custom_call_target="tpu_custom_call" | custom-call | flops 1600000000 | bytes 1024 | tf_op jit(solution)/shard_map/block_pair/pallas_call | solution.py:56
  16.6 5.8 %block_pair.9 = (bf16[256,1024]{1,0:T(8,128)(2,1)}, bf16[256,1024]{1,0:T(8,128)(2,1)}) custom-call(s32[1]{0:T(128)} %bitcast.rank_ref, bf16[2,2048,2048]{2,1,0:T(8,128)(2,1)} %a_ref.11, bf16[2,2048,1024]{2,1,0:T(8,128)(2,1)} %b_ref.15), custom_call_target="tpu_custom_call" | custom-call | flops 1600000000 | bytes 1024 | tf_op jit(solution)/shard_map/block_pair/pallas_call | solution.py:56
  26.1 5.8 %block_pair.8 = (bf16[256,1024]{1,0:T(8,128)(2,1)}, bf16[256,1024]{1,0:T(8,128)(2,1)}) custom-call(s32[1]{0:T(128)} %bitcast.rank_ref, bf16[2,2048,2048]{2,1,0:T(8,128)(2,1)} %a_ref.11, bf16[2,2048,1024]{2,1,0:T(8,128)(2,1)} %b_ref.15), custom_call_target="tpu_custom_call" | custom-call | flops 1600000000 | bytes 1024 | tf_op jit(solution)/shard_map/block_pair/pallas_call | solution.py:56
  37.1 5.9 %block_pair.13 = (bf16[256,1024]{1,0:T(8,128)(2,1)}, bf16[256,1024]{1,0:T(8,128)(2,1)}) custom-call(s32[1]{0:T(128)} %bitcast.rank_ref, bf16[2,2048,2048]{2,1,0:T(8,128)(2,1)} %a_ref.11, bf16[2,2048,1024]{2,1,0:T(8,128)(2,1)} %b_ref.15), custom_call_target="tpu_custom_call" | custom-call | flops 1600000000 | bytes 1024 | tf_op jit(solution)/shard_map/block_pair/pallas_call | solution.py:56
  43.0 5.9 %block_pair.12 = (bf16[256,1024]{1,0:T(8,128)(2,1)}, bf16[256,1024]{1,0:T(8,128)(2,1)}) custom-call(s32[1]{0:T(128)} %bitcast.rank_ref, bf16[2,2048,2048]{2,1,0:T(8,128)(2,1)} %a_ref.11, bf16[2,2048,1024]{2,1,0:T(8,128)(2,1)} %b_ref.15), custom_call_target="tpu_custom_call" | custom-call | flops 1600000000 | bytes 1024 | tf_op jit(solution)/shard_map/block_pair/pallas_call | solution.py:56
  50.9 4.5 %collective-permute-done.4.refs_1_.refs_5_ = bf16[256,1024]{1,0:T(8,128)(2,1)S(1)} collective-permute-done((bf16[256,1024]{1,0:T(8,128)(2,1)}, bf16[256,1024]{1,0:T(8,128)(2,1)S(1)}, u32[]{:S(2)}, u32[]{:S(2)}) %collective-permute-start.4) | collective-permute-done | bytes 524320 | tf_op jit(solution)/shard_map/ppermute | solution.py:22
  55.4 2.2 %collective-permute-done.5.refs_3_.refs_7_ = bf16[256,1024]{1,0:T(8,128)(2,1)} collective-permute-done((bf16[256,1024]{1,0:T(8,128)(2,1)}, bf16[256,1024]{1,0:T(8,128)(2,1)}, u32[]{:S(2)}, u32[]{:S(2)}) %collective-permute-start.5) | collective-permute-done | bytes 524320 | tf_op jit(solution)/shard_map/ppermute | solution.py:22
  64.3 5.9 %block_pair.14 = (bf16[256,1024]{1,0:T(8,128)(2,1)}, bf16[256,1024]{1,0:T(8,128)(2,1)}) custom-call(s32[1]{0:T(128)} %bitcast.rank_ref, bf16[2,2048,2048]{2,1,0:T(8,128)(2,1)} %a_ref.11, bf16[2,2048,1024]{2,1,0:T(8,128)(2,1)} %b_ref.15), custom_call_target="tpu_custom_call" | custom-call | flops 1600000000 | bytes 1024 | tf_op jit(solution)/shard_map/block_pair/pallas_call | solution.py:56
  72.2 5.1 %collective-permute-done.13 = bf16[256,1024]{1,0:T(8,128)(2,1)} collective-permute-done((bf16[256,1024]{1,0:T(8,128)(2,1)}, bf16[256,1024]{1,0:T(8,128)(2,1)}, u32[]{:S(2)}, u32[]{:S(2)}) %collective-permute-start.13) | collective-permute-done | bytes 524320 | tf_op jit(solution)/shard_map/ppermute | solution.py:22
  80.6 5.8 %block_pair.15 = (bf16[256,1024]{1,0:T(8,128)(2,1)}, bf16[256,1024]{1,0:T(8,128)(2,1)}) custom-call(s32[1]{0:T(128)} %bitcast.rank_ref, bf16[2,2048,2048]{2,1,0:T(8,128)(2,1)} %a_ref.11, bf16[2,2048,1024]{2,1,0:T(8,128)(2,1)} %b_ref.15), custom_call_target="tpu_custom_call" | custom-call | flops 1600000000 | bytes 1024 | tf_op jit(solution)/shard_map/block_pair/pallas_call | solution.py:56
  92.1 2.6 %group_combine.2 = (bf16[256,1024]{1,0:T(8,128)(2,1)S(1)}, bf16[256,1024]{1,0:T(8,128)(2,1)S(1)}) custom-call(s32[1]{0:T(128)} %bitcast.rank_ref, f32[16,128]{1,0:T(8,128)S(1)} %add.34.gram_ref, bf16[256,1024]{1,0:T(8,128)(2,1)S(1)} %copy-done, bf16[256,1024]{1,0:T(8,128)(2,1)S(1)} %collective-permute-done.6.refs_1_, ...), custom_call_target="tpu_custom_call" | custom-call | flops 1024 | bytes 1024 | tf_op jit(solution)/shard_map/group_combine/pallas_call | solution.py:31
  95.4 2.3 %gram_rows.6.refs_4_ = f32[16,128]{1,0:T(8,128)S(1)} custom-call(s32[1]{0:T(128)} %bitcast.rank_ref, bf16[256,1024]{1,0:T(8,128)(2,1)S(1)} %copy-done.2, bf16[256,1024]{1,0:T(8,128)(2,1)} %collective-permute-done.19.refs_1_, bf16[256,1024]{1,0:T(8,128)(2,1)} %collective-permute-done.18.refs_2_, bf16[256,1024]{1,0:T(8,128)(2,1)} %collective-permute-done.20.refs_3_), custom_call_target="tpu_custom_call" | custom-call | flops 3200000000 | bytes 1024 | tf_op jit(solution)/shard_map/gram_rows/pallas_call | solution.py:31
  97.8 3.9 %collective-permute-done.15.refs_1_.refs_5_ = bf16[256,1024]{1,0:T(8,128)(2,1)S(1)} collective-permute-done((bf16[256,1024]{1,0:T(8,128)(2,1)}, bf16[256,1024]{1,0:T(8,128)(2,1)S(1)}, u32[]{:S(2)}, u32[]{:S(2)}) %collective-permute-start.15) | collective-permute-done | bytes 524320 | tf_op jit(solution)/shard_map/ppermute | solution.py:22
  108.6 5.5 %collective-permute-start.26 = (bf16[256,1024]{1,0:T(8,128)(2,1)S(1)}, bf16[256,1024]{1,0:T(8,128)(2,1)S(1)}, u32[]{:S(2)}, u32[]{:S(2)}) collective-permute-start(bf16[256,1024]{1,0:T(8,128)(2,1)S(1)} %get-tuple-element.115), channel_id=1, source_target_pairs={{0,24},{4,28},{24,0},{28,4},{1,25},{5,29},{25,1},{29,5},{2,26},{6,... | collective-permute-start | bytes 1572872 | tf_op jit(solution)/shard_map/ppermute | solution.py:310
  116.9 2.1 %collective-permute-done.24 = f32[16,128]{1,0:T(8,128)S(1)} collective-permute-done((f32[16,128]{1,0:T(8,128)S(1)}, f32[16,128]{1,0:T(8,128)S(1)}, u32[]{:S(2)}, u32[]{:S(2)}) %collective-permute-start.24) | collective-permute-done | bytes 8224 | tf_op jit(solution)/shard_map/ppermute | solution.py:22
  119.6 3.1 %collective-permute-done.25 = f32[16,128]{1,0:T(8,128)S(1)} collective-permute-done((f32[16,128]{1,0:T(8,128)S(1)}, f32[16,128]{1,0:T(8,128)S(1)}, u32[]{:S(2)}, u32[]{:S(2)}) %collective-permute-start.25) | collective-permute-done | bytes 8224 | tf_op jit(solution)/shard_map/ppermute | solution.py:22
  122.7 3.0 %group_combine.3 = (bf16[256,1024]{1,0:T(8,128)(2,1)S(1)}, bf16[256,1024]{1,0:T(8,128)(2,1)S(1)}) custom-call(s32[1]{0:T(128)} %bitcast.rank_ref, f32[16,128]{1,0:T(8,128)S(1)} %add.38.gram_ref, bf16[256,1024]{1,0:T(8,128)(2,1)S(1)} %copy-done.2, bf16[256,1024]{1,0:T(8,128)(2,1)} %collective-permute-done.19.refs_1_, ...), custom_call_target="tpu_custom_call" | custom-call | flops 1024 | bytes 1024 | tf_op jit(solution)/shard_map/group_combine/pallas_call | solution.py:31
  126.4 2.3 %collective-permute-start.28 = (bf16[256,1024]{1,0:T(8,128)(2,1)S(1)}, bf16[256,1024]{1,0:T(8,128)(2,1)S(1)}, u32[]{:S(2)}, u32[]{:S(2)}) collective-permute-start(bf16[256,1024]{1,0:T(8,128)(2,1)S(1)} %get-tuple-element.117), channel_id=1, source_target_pairs={{0,24},{4,28},{24,0},{28,4},{1,25},{5,29},{25,1},{29,5},{2,26},{6,... | collective-permute-start | bytes 1572872 | tf_op jit(solution)/shard_map/ppermute | solution.py:310
  129.2 13.3 %collective-permute-done.28.refs_2_.refs_5_ = bf16[256,1024]{1,0:T(8,128)(2,1)S(1)} collective-permute-done((bf16[256,1024]{1,0:T(8,128)(2,1)S(1)}, bf16[256,1024]{1,0:T(8,128)(2,1)S(1)}, u32[]{:S(2)}, u32[]{:S(2)}) %collective-permute-start.28) | collective-permute-done | bytes 524320 | tf_op jit(solution)/shard_map/ppermute | solution.py:310
  148.3 3.1 %collective-permute-done.31 = f32[8,128]{1,0:T(8,128)S(1)} collective-permute-done((f32[8,128]{1,0:T(8,128)S(1)}, f32[8,128]{1,0:T(8,128)S(1)}, u32[]{:S(2)}, u32[]{:S(2)}) %collective-permute-start.31) | collective-permute-done | bytes 4128 | tf_op jit(solution)/shard_map/ppermute | solution.py:22
  151.4 6.1 %collective-permute-start.32 = (f32[8,128]{1,0:T(8,128)S(1)}, f32[8,128]{1,0:T(8,128)S(1)}, u32[]{:S(2)}, u32[]{:S(2)}) collective-permute-start(f32[8,128]{1,0:T(8,128)S(1)} %add.41), channel_id=1, source_target_pairs={{0,8},{4,12},{8,0},{12,4},{16,24},{20,28},{24,16},{28,20},{1,9},{5... | collective-permute-start | bytes 12296 | tf_op jit(solution)/shard_map/ppermute | solution.py:22
  160.8 2.7 %collective-permute-done.33 = f32[8,128]{1,0:T(8,128)S(1)} collective-permute-done((f32[8,128]{1,0:T(8,128)S(1)}, f32[8,128]{1,0:T(8,128)S(1)}, u32[]{:S(2)}, u32[]{:S(2)}) %collective-permute-start.33) | collective-permute-done | bytes 4128 | tf_op jit(solution)/shard_map/ppermute | solution.py:22
  (81 shorter events, 53.7 us)
Async XLA Ops:
  5.8 16.7 %collective-permute-start = (bf16[256,1024]{1,0:T(8,128)(2,1)}, bf16[256,1024]{1,0:T(8,128)(2,1)}, u32[]{:S(2)}, u32[]{:S(2)}) collective-permute-start(bf16[256,1024]{1,0:T(8,128)(2,1)} %get-tuple-element.65), channel_id=1, source_target_pairs={{0,4},{4,0},{8,12},{12,8},{16,20},{20,16},{24,28},{28,24},{1,5},{5... | collective-permute-start | bytes 1572872 | tf_op jit(solution)/shard_map/ppermute | solution.py:22
  8.7 15.1 %collective-permute-start.1 = (bf16[256,1024]{1,0:T(8,128)(2,1)}, bf16[256,1024]{1,0:T(8,128)(2,1)S(1)}, u32[]{:S(2)}, u32[]{:S(2)}) collective-permute-start(bf16[256,1024]{1,0:T(8,128)(2,1)} %get-tuple-element.66), channel_id=1, source_target_pairs={{0,8},{4,12},{8,0},{12,4},{16,24},{20,28},{24,16},{28,20},{1,9},{5... | collective-permute-start | bytes 1572872 | tf_op jit(solution)/shard_map/ppermute | solution.py:22
  16.1 16.9 %collective-permute-start.2 = (bf16[256,1024]{1,0:T(8,128)(2,1)}, bf16[256,1024]{1,0:T(8,128)(2,1)}, u32[]{:S(2)}, u32[]{:S(2)}) collective-permute-start(bf16[256,1024]{1,0:T(8,128)(2,1)} %get-tuple-element.70), channel_id=1, source_target_pairs={{0,4},{4,0},{8,12},{12,8},{16,20},{20,16},{24,28},{28,24},{1,5},{5... | collective-permute-start | bytes 1572872 | tf_op jit(solution)/shard_map/ppermute | solution.py:22
  16.6 18.4 %collective-permute-start.3 = (bf16[256,1024]{1,0:T(8,128)(2,1)}, bf16[256,1024]{1,0:T(8,128)(2,1)S(1)}, u32[]{:S(2)}, u32[]{:S(2)}) collective-permute-start(bf16[256,1024]{1,0:T(8,128)(2,1)} %get-tuple-element.71), channel_id=1, source_target_pairs={{0,8},{4,12},{8,0},{12,4},{16,24},{20,28},{24,16},{28,20},{1,9},{5... | collective-permute-start | bytes 1572872 | tf_op jit(solution)/shard_map/ppermute | solution.py:22
  23.8 25.1 %collective-permute-start.6 = (bf16[256,1024]{1,0:T(8,128)(2,1)}, bf16[256,1024]{1,0:T(8,128)(2,1)S(1)}, u32[]{:S(2)}, u32[]{:S(2)}) collective-permute-start(bf16[256,1024]{1,0:T(8,128)(2,1)} %get-tuple-element.84), channel_id=1, source_target_pairs={{0,4},{4,0},{8,12},{12,8},{16,20},{20,16},{24,28},{28,24},{1,5},{5... | collective-permute-start | bytes 1572872 | tf_op jit(solution)/shard_map/ppermute | solution.py:22
  24.5 24.4 %collective-permute-start.7 = (bf16[256,1024]{1,0:T(8,128)(2,1)}, bf16[256,1024]{1,0:T(8,128)(2,1)S(1)}, u32[]{:S(2)}, u32[]{:S(2)}) collective-permute-start(bf16[256,1024]{1,0:T(8,128)(2,1)} %collective-permute-done), channel_id=1, source_target_pairs={{0,8},{4,12},{8,0},{12,4},{16,24},{20,28},{24,16},{28,20},{1,9},{5... | collective-permute-start | bytes 1572872 | tf_op jit(solution)/shard_map/ppermute | solution.py:22
  35.0 20.4 %collective-permute-start.4 = (bf16[256,1024]{1,0:T(8,128)(2,1)}, bf16[256,1024]{1,0:T(8,128)(2,1)S(1)}, u32[]{:S(2)}, u32[]{:S(2)}) collective-permute-start(bf16[256,1024]{1,0:T(8,128)(2,1)} %get-tuple-element.76), channel_id=1, source_target_pairs={{0,4},{4,0},{8,12},{12,8},{16,20},{20,16},{24,28},{28,24},{1,5},{5... | collective-permute-start | bytes 1572872 | tf_op jit(solution)/shard_map/ppermute | solution.py:22
  35.1 22.5 %collective-permute-start.5 = (bf16[256,1024]{1,0:T(8,128)(2,1)}, bf16[256,1024]{1,0:T(8,128)(2,1)}, u32[]{:S(2)}, u32[]{:S(2)}) collective-permute-start(bf16[256,1024]{1,0:T(8,128)(2,1)} %collective-permute-done.2), channel_id=1, source_target_pairs={{0,8},{4,12},{8,0},{12,4},{16,24},{20,28},{24,16},{28,20},{1,9},{5... | collective-permute-start | bytes 1572872 | tf_op jit(solution)/shard_map/ppermute | solution.py:22
  48.9 21.3 %collective-permute-start.17 = (bf16[256,1024]{1,0:T(8,128)(2,1)}, bf16[256,1024]{1,0:T(8,128)(2,1)}, u32[]{:S(2)}, u32[]{:S(2)}) collective-permute-start(bf16[256,1024]{1,0:T(8,128)(2,1)} %get-tuple-element.105), channel_id=1, source_target_pairs={{0,4},{4,0},{8,12},{12,8},{16,20},{20,16},{24,28},{28,24},{1,5},{5... | collective-permute-start | bytes 1572872 | tf_op jit(solution)/shard_map/ppermute | solution.py:22
  50.4 20.2 %collective-permute-start.18 = (bf16[256,1024]{1,0:T(8,128)(2,1)}, bf16[256,1024]{1,0:T(8,128)(2,1)}, u32[]{:S(2)}, u32[]{:S(2)}) collective-permute-start(bf16[256,1024]{1,0:T(8,128)(2,1)} %get-tuple-element.106), channel_id=1, source_target_pairs={{0,8},{4,12},{8,0},{12,4},{16,24},{20,28},{24,16},{28,20},{1,9},{5... | collective-permute-start | bytes 1572872 | tf_op jit(solution)/shard_map/ppermute | solution.py:22
  57.6 19.6 %collective-permute-start.13 = (bf16[256,1024]{1,0:T(8,128)(2,1)}, bf16[256,1024]{1,0:T(8,128)(2,1)}, u32[]{:S(2)}, u32[]{:S(2)}) collective-permute-start(bf16[256,1024]{1,0:T(8,128)(2,1)} %get-tuple-element.98), channel_id=1, source_target_pairs={{0,4},{4,0},{8,12},{12,8},{16,20},{20,16},{24,28},{28,24},{1,5},{5... | collective-permute-start | bytes 1572872 | tf_op jit(solution)/shard_map/ppermute | solution.py:22
  57.7 21.4 %collective-permute-start.14 = (bf16[256,1024]{1,0:T(8,128)(2,1)}, bf16[256,1024]{1,0:T(8,128)(2,1)}, u32[]{:S(2)}, u32[]{:S(2)}) collective-permute-start(bf16[256,1024]{1,0:T(8,128)(2,1)} %get-tuple-element.99), channel_id=1, source_target_pairs={{0,8},{4,12},{8,0},{12,4},{16,24},{20,28},{24,16},{28,20},{1,9},{5... | collective-permute-start | bytes 1572872 | tf_op jit(solution)/shard_map/ppermute | solution.py:22
  62.8 23.7 %collective-permute-start.8 = (f32[16,128]{1,0:T(8,128)S(1)}, f32[16,128]{1,0:T(8,128)S(1)}, u32[]{:S(2)}, u32[]{:S(2)}) collective-permute-start(f32[16,128]{1,0:T(8,128)S(1)} %gram_rows.5.refs_0_), channel_id=1, source_target_pairs={{0,4},{4,0},{8,12},{12,8},{16,20},{20,16},{24,28},{28,24},{1,5},{5... | collective-permute-start | bytes 24584 | tf_op jit(solution)/shard_map/ppermute | solution.py:22
  70.2 16.9 %collective-permute-start.9 = (f32[16,128]{1,0:T(8,128)S(1)}, f32[16,128]{1,0:T(8,128)S(1)}, u32[]{:S(2)}, u32[]{:S(2)}) collective-permute-start(f32[16,128]{1,0:T(8,128)S(1)} %gram_rows.5.refs_0_), channel_id=1, source_target_pairs={{0,8},{4,12},{8,0},{12,4},{16,24},{20,28},{24,16},{28,20},{1,9},{5... | collective-permute-start | bytes 24584 | tf_op jit(solution)/shard_map/ppermute | solution.py:22
  70.6 16.6 %collective-permute-start.10 = (f32[16,128]{1,0:T(8,128)S(1)}, f32[16,128]{1,0:T(8,128)S(1)}, u32[]{:S(2)}, u32[]{:S(2)}) collective-permute-start(f32[16,128]{1,0:T(8,128)S(1)} %gram_rows.5.refs_0_), channel_id=1, source_target_pairs={{0,12},{4,8},{8,4},{12,0},{16,28},{20,24},{24,20},{28,16},{1,13},{... | collective-permute-start | bytes 24584 | tf_op jit(solution)/shard_map/ppermute | solution.py:22
  77.2 18.1 %collective-permute-start.19 = (bf16[256,1024]{1,0:T(8,128)(2,1)}, bf16[256,1024]{1,0:T(8,128)(2,1)}, u32[]{:S(2)}, u32[]{:S(2)}) collective-permute-start(bf16[256,1024]{1,0:T(8,128)(2,1)} %get-tuple-element.107), channel_id=1, source_target_pairs={{0,4},{4,0},{8,12},{12,8},{16,20},{20,16},{24,28},{28,24},{1,5},{5... | collective-permute-start | bytes 1572872 | tf_op jit(solution)/shard_map/ppermute | solution.py:22
  79.1 16.3 %collective-permute-start.20 = (bf16[256,1024]{1,0:T(8,128)(2,1)}, bf16[256,1024]{1,0:T(8,128)(2,1)}, u32[]{:S(2)}, u32[]{:S(2)}) collective-permute-start(bf16[256,1024]{1,0:T(8,128)(2,1)} %collective-permute-done.17), channel_id=1, source_target_pairs={{0,8},{4,12},{8,0},{12,4},{16,24},{20,28},{24,16},{28,20},{1,9},{5... | collective-permute-start | bytes 1572872 | tf_op jit(solution)/shard_map/ppermute | solution.py:22
  86.5 15.2 %collective-permute-start.15 = (bf16[256,1024]{1,0:T(8,128)(2,1)}, bf16[256,1024]{1,0:T(8,128)(2,1)S(1)}, u32[]{:S(2)}, u32[]{:S(2)}) collective-permute-start(bf16[256,1024]{1,0:T(8,128)(2,1)} %get-tuple-element.100), channel_id=1, source_target_pairs={{0,4},{4,0},{8,12},{12,8},{16,20},{20,16},{24,28},{28,24},{1,5},{5... | collective-permute-start | bytes 1572872 | tf_op jit(solution)/shard_map/ppermute | solution.py:22
  87.1 15.8 %collective-permute-start.16 = (bf16[256,1024]{1,0:T(8,128)(2,1)}, bf16[256,1024]{1,0:T(8,128)(2,1)S(1)}, u32[]{:S(2)}, u32[]{:S(2)}) collective-permute-start(bf16[256,1024]{1,0:T(8,128)(2,1)} %collective-permute-done.13), channel_id=1, source_target_pairs={{0,8},{4,12},{8,0},{12,4},{16,24},{20,28},{24,16},{28,20},{1,9},{5... | collective-permute-start | bytes 1572872 | tf_op jit(solution)/shard_map/ppermute | solution.py:22
  94.7 20.7 %collective-permute-start.23 = (bf16[256,1024]{1,0:T(8,128)(2,1)S(1)}, bf16[256,1024]{1,0:T(8,128)(2,1)S(1)}, u32[]{:S(2)}, u32[]{:S(2)}) collective-permute-start(bf16[256,1024]{1,0:T(8,128)(2,1)S(1)} %get-tuple-element.115), channel_id=1, source_target_pairs={{8,16},{12,20},{16,8},{20,12},{9,17},{13,21},{17,9},{21,13},{10,18... | collective-permute-start | bytes 1572872 | tf_op jit(solution)/shard_map/ppermute | solution.py:310
  108.6 17.1 %collective-permute-start.26 = (bf16[256,1024]{1,0:T(8,128)(2,1)S(1)}, bf16[256,1024]{1,0:T(8,128)(2,1)S(1)}, u32[]{:S(2)}, u32[]{:S(2)}) collective-permute-start(bf16[256,1024]{1,0:T(8,128)(2,1)S(1)} %get-tuple-element.115), channel_id=1, source_target_pairs={{0,24},{4,28},{24,0},{28,4},{1,25},{5,29},{25,1},{29,5},{2,26},{6,... | collective-permute-start | bytes 1572872 | tf_op jit(solution)/shard_map/ppermute | solution.py:310
  126.4 16.1 %collective-permute-start.28 = (bf16[256,1024]{1,0:T(8,128)(2,1)S(1)}, bf16[256,1024]{1,0:T(8,128)(2,1)S(1)}, u32[]{:S(2)}, u32[]{:S(2)}) collective-permute-start(bf16[256,1024]{1,0:T(8,128)(2,1)S(1)} %get-tuple-element.117), channel_id=1, source_target_pairs={{0,24},{4,28},{24,0},{28,4},{1,25},{5,29},{25,1},{29,5},{2,26},{6,... | collective-permute-start | bytes 1572872 | tf_op jit(solution)/shard_map/ppermute | solution.py:310
  151.4 7.7 %collective-permute-start.32 = (f32[8,128]{1,0:T(8,128)S(1)}, f32[8,128]{1,0:T(8,128)S(1)}, u32[]{:S(2)}, u32[]{:S(2)}) collective-permute-start(f32[8,128]{1,0:T(8,128)S(1)} %add.41), channel_id=1, source_target_pairs={{0,8},{4,12},{8,0},{12,4},{16,24},{20,28},{24,16},{28,20},{1,9},{5... | collective-permute-start | bytes 12296 | tf_op jit(solution)/shard_map/ppermute | solution.py:22
  159.1 4.5 %collective-permute-start.33 = (f32[8,128]{1,0:T(8,128)S(1)}, f32[8,128]{1,0:T(8,128)S(1)}, u32[]{:S(2)}, u32[]{:S(2)}) collective-permute-start(f32[8,128]{1,0:T(8,128)S(1)} %add.42), channel_id=1, source_target_pairs={{0,16},{4,20},{8,24},{12,28},{16,0},{20,4},{24,8},{28,12},{1,17},{... | collective-permute-start | bytes 12296 | tf_op jit(solution)/shard_map/ppermute | solution.py:22
  (14 other events, 88.8 us)

commit v4 on v3

--- a/solution.py
+++ b/solution.py
@@ -14,12 +14,30 @@
 GRAM_ROWS = 16
 COST = 1024
 BLOCK_COST = 1_600_000_000
+MESH_HOPS = True
+KEPT_COST = 5_000_000_000
+BATCHES = ((1, 2), (1,))
+FIRST_COST = 3_200_000_000
 GRAM_COST = 3_200_000_000
-CROSS_COST = 4_000_000_000
+CROSS_COST = 6_000_000_000
 
 
 def exchange(value, axis, mask):
     return lax.ppermute(value, axis, [(i, i ^ mask) for i in range(lax.axis_size(axis))])
+
+
+def exchange_all(value, masks):
+    if len(masks) == 1:
+        ((axis, mask),) = masks.items()
+        return exchange(value, axis, mask)
+    axes = ("rep", "par")
+    inner = lax.axis_size("par")
+    pairs = [
+        (i * inner + j, (i ^ masks[axes[0]]) * inner + (j ^ masks[axes[1]]))
+        for i in range(lax.axis_size(axes[0]))
+        for j in range(inner)
+    ]
+    return lax.ppermute(value, axes, pairs)
 
 
 def tied(values, others):
@@ -40,36 +58,54 @@
     )(rank, *inputs)
 
 
-def block_pair(rank, activations, output_grads, layer, offset, rows):
+def block_pairs(rank, activations, output_grads, layer, offsets, rows):
     tokens, width_out = output_grads.shape[1:]
     columns = min(512, width_out)
-
-    def kernel(rank_ref, a_ref, b_ref, kept, sent, product):
+    count = len(offsets)
+
+    def offset_of(number):
+        value = offsets[0]
+        for index in range(1, count):
+            value = jnp.where(number == index, offsets[index], value)
+        return value
+
+    def kernel(rank_ref, a_ref, b_ref, *refs):
+        outs, product = refs[:-1], refs[-1]
+        number = pl.program_id(1)
         product[...] = lax.dot_general(
             a_ref[0], b_ref[0], (((0,), (0,)), ((), ())), preferred_element_type=jnp.float32
         )
-        side = (rank_ref[0] ^ offset) & 1
-        kept[...] = product[pl.ds(pl.multiple_of(side * rows, rows), rows), :].astype(jnp.bfloat16)
-        sent[...] = product[pl.ds(pl.multiple_of((1 - side) * rows, rows), rows), :].astype(jnp.bfloat16)
+        side = (rank_ref[0] ^ offset_of(number)) & 1
+        kept = product[pl.ds(pl.multiple_of(side * rows, rows), rows), :].astype(jnp.bfloat16)
+        sent = product[pl.ds(pl.multiple_of((1 - side) * rows, rows), rows), :].astype(jnp.bfloat16)
+        for index in range(count):
+
+            @pl.when(number == index)
+            def _(index=index):
+                outs[2 * index][...] = kept
+                outs[2 * index + 1][...] = sent
 
     shape = jax.ShapeDtypeStruct((rows, width_out), jnp.bfloat16)
-    return pl.pallas_call(
+    values = pl.pallas_call(
         kernel,
         grid_spec=pltpu.PrefetchScalarGridSpec(
             num_scalar_prefetch=1,
-            grid=(width_out // columns,),
+            grid=(width_out // columns, count),
             in_specs=[
-                pl.BlockSpec((1, tokens, 2 * rows), lambda j, rank: (layer, 0, (rank[0] ^ offset) >> 1)),
-                pl.BlockSpec((1, tokens, columns), lambda j, rank: (layer, 0, j)),
+                pl.BlockSpec(
+                    (1, tokens, 2 * rows), lambda j, i, rank: (layer, 0, (rank[0] ^ offset_of(i)) >> 1)
+                ),
+                pl.BlockSpec((1, tokens, columns), lambda j, i, rank: (layer, 0, j)),
             ],
-            out_specs=[pl.BlockSpec((rows, columns), lambda j, rank: (0, j))] * 2,
+            out_specs=[pl.BlockSpec((rows, columns), lambda j, i, rank: (0, j))] * (2 * count),
             scratch_shapes=[pltpu.VMEM((2 * rows, columns), jnp.float32)],
         ),
-        out_shape=[shape, shape],
+        out_shape=[shape] * (2 * count),
         compiler_params=pltpu.CompilerParams(vmem_limit_bytes=LARGE_LIMIT),
         cost_estimate=pl.CostEstimate(flops=BLOCK_COST, bytes_accessed=COST, transcendentals=0),
-        name="block_pair",
+        name="block_pairs",
     )(rank, activations, output_grads)
+    return list(zip(values[::2], values[1::2]))
 
 
 def pair_row(first, second):
@@ -146,7 +182,7 @@
     return result.astype(jnp.bfloat16)
 
 
-def group_combine(rank, gram, block_parts):
+def group_combine(rank, gram, block_parts, cost=COST):
     rows, width = block_parts[0][0].shape
 
     def kernel(rank_ref, gram_ref, *refs):
@@ -208,7 +244,7 @@
 
     shape = jax.ShapeDtypeStruct((rows, width), jnp.bfloat16)
     inputs = [gram] + [part for parts in block_parts for part in parts]
-    return call(kernel, "group_combine", rank, inputs, [shape] * len(block_parts))
+    return call(kernel, "group_combine", rank, inputs, [shape] * len(block_parts), cost)
 
 
 def chosen_rows(rank_ref, level, candidates, where, columns):
@@ -321,9 +357,6 @@
     masks = level_masks(levels)
     tails = [tail << 2 for tail in reversed(range(replicas // GROUP))]
 
-    def near_pair(inputs, layer, code):
-        return block_pair(position, inputs, output_grads, layer, spread(code, masks), rows)
-
     own, crossed, far, far_crossed = {}, {}, {}, {}
     rounds = []
     for layer in range(layers):
@@ -342,19 +375,28 @@
     spans = []
     stride = 1
     while stride < par:
-        spans.append(("par", stride))
+        spans.append([("par", stride)])
         stride *= 2
 
     def summed(value, hops):
-        for axis, mask in hops:
-            value = value + exchange(value, axis, mask)
+        for hop in hops:
+            if len(hop) == 2 and MESH_HOPS:
+                first, second = hop
+                both = {}
+                for axis, mask in hop:
+                    both[axis] = both.get(axis, 0) ^ mask
+                parts = [value] + [exchange(value, *one) for one in hop] + [exchange_all(value, both)]
+                value = total(parts, COST)
+            else:
+                for axis, mask in hop:
+                    value = value + exchange(value, axis, mask)
         return value
 
     def layer_gram(layer):
         gram = None
         for tail in tails:
             parts = [held[layer, tail] for held in (own, crossed, far, far_crossed)]
-            cost = GRAM_COST if layer == layers - 1 else COST
+            cost = COST if layer < layers - 1 else FIRST_COST if gram is None else GRAM_COST
             gram = gram_rows(position, parts, gram, cost)
         return gram
 
@@ -362,7 +404,12 @@
         parts = [
             [held[layer, tail] for held in (own, crossed, far, far_crossed)] for tail in tails
         ]
-        return dict(zip(tails, group_combine(position, gram, parts)))
+        return {
+            tail: group_combine(
+                position, gram, [block_parts], KEPT_COST if layer == layers - 1 and tail == 0 else COST
+            )[0]
+            for tail, block_parts in zip(tails, parts)
+        }
 
     def receive(blocks, level, middle):
         mask = masks[level]
@@ -381,22 +428,33 @@
 
     inputs = activations
     per_layer = len(rounds) // layers
-    combined, received = [], []
+    combined, received, sends = [], [], {}
+
+    def multiply(number):
+        nonlocal inputs
+        if number >= 2 * window:
+            (inputs,) = settle(number - 2 * window, [inputs])
+        layer = rounds[number][0]
+        batch = [number]
+        while (batch[-1] + 1) % per_layer and (batch[-1] + 1) % per_layer not in BATCHES[layer > 0]:
+            batch.append(batch[-1] + 1)
+        offsets = [spread(rounds[index][1], masks) for index in batch]
+        values = block_pairs(position, inputs, output_grads, layer, offsets, rows)
+        for index, (kept, sent) in zip(batch, values):
+            own[layer, rounds[index][1]], sends[index] = kept, sent
+
     for number in range(len(rounds)):
         layer, code, source, target, block = rounds[number]
-        if number >= 2 * window:
-            (inputs,) = settle(number - 2 * window, [inputs])
-        own[layer, code], sent = near_pair(inputs, layer, code)
-        passed = source[layer, block]
+        if number not in sends:
+            multiply(number)
+        sent, passed = sends[number], source[layer, block]
+        done, step = divmod(number - window + 1, per_layer)
         if number >= window:
             sent, passed = settle(number - window, [sent, passed])
-        done, step = divmod(number - window + 1, per_layer)
-        if done >= 1 and step == 0:
-            gram = layer_gram(done - 1)
-            gram = total(
-                [gram] + [exchange(gram, "rep", mask) for mask in range(1, GROUP)], CROSS_COST
-            )
-            combined.append(group_result(done - 1, summed(gram, spans)))
+        if done >= 1 and step == 1:
+            (sent, passed), (gram,) = tied([sent, passed], [layer_gram(done - 1)])
+            parts = [gram] + [exchange(gram, "rep", mask) for mask in range(1, GROUP)]
+            combined.append(group_result(done - 1, summed(total(parts, CROSS_COST), spans)))
             received.append(receive(combined[-1], 2, True))
         crossed[layer, code] = exchange(sent, "rep", masks[0])
         target[layer, block ^ 2] = exchange(passed, "rep", masks[1])
@@ -404,9 +462,10 @@
     first = (layers - 1, tails[0])
     for layer in range(layers - 1):
         names = list(combined[layer])
-        values, (own[first],) = tied([combined[layer][tail] for tail in names], [own[first]])
+        values = [combined[layer][tail] for tail in names]
+        values, (own[first],) = tied(values, [own[first]])
         combined[layer] = dict(zip(names, values))
-    gram = summed(layer_gram(layers - 1), [("rep", masks[1])])
+    gram = summed(layer_gram(layers - 1), [[("rep", masks[1])]])
     for layer in range(layers - 1):
         names = list(combined[layer])
         values, (gram,) = tied([combined[layer][tail] for tail in names], [gram])
@@ -415,13 +474,13 @@
         gram = summed(gram, spans[:1])
         (gram,), received[layer] = tied_ways([gram], received[layer])
         received[layer] = [a + b for a, b in zip(received[layer], outer)]
-    gram = summed(gram, (spans[1:] if layers > 1 else spans) + [("rep", masks[0])])
+    gram = summed(gram, spans[1:-1] + [spans[-1] + [("rep", masks[0])]])
     combined.append(group_result(layers - 1, gram))
-    names = list(combined[-1])
+    names = [tail for tail in tails if tail >> 2 & 1]
     values = [combined[-1][tail] for tail in names]
     for layer in range(layers - 1):
         values, received[layer] = tied_ways(values, received[layer])
-    combined[-1] = dict(zip(names, values))
+    combined[-1].update(zip(names, values))
     received.append(receive_all(combined[-1], 2))
 
     for level in range(2, levels):
@@ -430,7 +489,9 @@
         totals = None
         for layer in range(layers):
             totals = pair_rows(position, kept[layer], received[layer], level, layer, layers, totals)
-        totals = summed(totals, spans + [("rep", 1 << bit) for bit in range(level + 1)])
+        bits = [("rep", 1 << bit) for bit in range(level + 1)]
+        hops = spans[:-1] + [spans[-1] + bits[:1]] + [bits[i : i + 2] for i in range(1, level + 1, 2)]
+        totals = summed(totals, hops)
         results = pair_combine(position, totals, kept, received, level)
         if level < levels - 1:
             combined = [

time: 166 us -> 161 us (0.970)
  Pallas kernels: 62.4 us -> 54.7 us
  starting transfers between devices: 46.1 us -> 53.4 us
  waiting for transfers between devices: 56.7 us -> 52.1 us
    pallas_call x8 -> x5, Pallas kernels: 46.7 us -> 40.5 us  [block_pairs(): pl.pallas_call(kernel, grid_spec=pltpu.PrefetchScalarGridSpec(num_scalar_...]
    ppermute x30 -> x31, waiting for transfers between devices: 43.4 us -> 39.8 us  [exchange(): lax.ppermute(value, axis, [(i, i ^ mask) for i in range(lax.axis_size(axi...]
    ppermute x30 -> x31, starting transfers between devices: 36.9 us -> 40.3 us  [exchange(): lax.ppermute(value, axis, [(i, i ^ mask) for i in range(lax.axis_size(axi...]
    ppermute x4, waiting for transfers between devices: 13.3 us -> 10.2 us  [swap(): return lax.ppermute(value, 'rep', pairs)]
    ppermute x0 -> x2, waiting for transfers between devices: none -> 2.08 us  [exchange_all(): return lax.ppermute(value, axes, pairs)]
    ppermute x0 -> x2, starting transfers between devices: none -> 2 us  [exchange_all(): return lax.ppermute(value, axes, pairs)]
    ppermute x4, starting transfers between devices: 9.19 us -> 11 us  [swap(): return lax.ppermute(value, 'rep', pairs)]
    pallas_call x9 -> x11, Pallas kernels: 15.7 us -> 14.2 us  [call(): pl.pallas_call(kernel, in_specs=[pl.BlockSpec(memory_space=pltpu.SMEM)] +...]
  transfers between devices with their start and end apart: 34 -> 37, of which waited for: 20 -> 24; matrix products, arithmetic and copies ran while one was open for 0% -> 0% of each run, Pallas kernels for 33% -> 29%
where the time goes in v4:
time: 161 us; the launch traced here: 160 us
  Pallas kernels  54.7 us (34%)
  starting transfers between devices  53.4 us (33%)
  waiting for transfers between devices  52.1 us (32%)
    pallas_call x5, Pallas kernels, block_pairs(): pl.pallas_call(kernel, grid_spec=pltpu.PrefetchScalarGridSpec(num_scalar_...  40.5 us
    ppermute x31, starting transfers between devices, exchange(): lax.ppermute(value, axis, [(i, i ^ mask) for i in range(lax.axis_size(axi...  40.3 us
    ppermute x31, waiting for transfers between devices, exchange(): lax.ppermute(value, axis, [(i, i ^ mask) for i in range(lax.axis_size(axi...  39.8 us
    pallas_call x11, Pallas kernels, call(): pl.pallas_call(kernel, in_specs=[pl.BlockSpec(memory_space=pltpu.SMEM)] +...  14.2 us
    ppermute x4, starting transfers between devices, swap(): return lax.ppermute(value, 'rep', pairs)  11 us
    ppermute x4, waiting for transfers between devices, swap(): return lax.ppermute(value, 'rep', pairs)  10.2 us
  transfers between devices with their start and end apart: 37, of which 24 were waited for; matrix products, arithmetic and copies ran while one was open for 0% of the time, Pallas kernels for 29%

profile of v4, /device:TPU:0, one launch (start us, length us, event | category | flops | bytes accessed | tf_op | source)
XLA Modules:
  0.0 160.4 jit_solution(5565381435435247610)
XLA Ops:
  0.0 5.8 %block_pairs.6 = (bf16[256,1024]{1,0:T(8,128)(2,1)}, bf16[256,1024]{1,0:T(8,128)(2,1)}) custom-call(s32[1]{0:T(128)} %bitcast.rank_ref, bf16[2,2048,2048]{2,1,0:T(8,128)(2,1)} %a_ref.7, bf16[2,2048,1024]{2,1,0:T(8,128)(2,1)} %b_ref.9), custom_call_target="tpu_custom_call" | custom-call | flops 1600000000 | bytes 1024 | tf_op jit(solution)/shard_map/block_pairs/pallas_call | solution.py:89
  5.8 2.9 %collective-permute-start = (bf16[256,1024]{1,0:T(8,128)(2,1)}, bf16[256,1024]{1,0:T(8,128)(2,1)}, u32[]{:S(2)}, u32[]{:S(2)}) collective-permute-start(bf16[256,1024]{1,0:T(8,128)(2,1)} %get-tuple-element.60), channel_id=1, source_target_pairs={{0,4},{4,0},{8,12},{12,8},{16,20},{20,16},{24,28},{28,24},{1,5},{5... | collective-permute-start | bytes 1572872 | tf_op jit(solution)/shard_map/ppermute | solution.py:26
  10.3 5.9 %block_pairs.7 = (bf16[256,1024]{1,0:T(8,128)(2,1)}, bf16[256,1024]{1,0:T(8,128)(2,1)}) custom-call(s32[1]{0:T(128)} %bitcast.rank_ref, bf16[2,2048,2048]{2,1,0:T(8,128)(2,1)} %a_ref.7, bf16[2,2048,1024]{2,1,0:T(8,128)(2,1)} %b_ref.9), custom_call_target="tpu_custom_call" | custom-call | flops 1600000000 | bytes 1024 | tf_op jit(solution)/shard_map/block_pairs/pallas_call | solution.py:89
  16.7 9.8 %block_pairs.5 = (bf16[256,1024]{1,0:T(8,128)(2,1)}, bf16[256,1024]{1,0:T(8,128)(2,1)}, bf16[256,1024]{1,0:T(8,128)(2,1)}, bf16[256,1024]{1,0:T(8,128)(2,1)}) custom-call(s32[1]{0:T(128)} %bitcast.rank_ref, bf16[2,2048,2048]{2,1,0:T(8,128)(2,1)} %a_ref.7, bf16[2,2048,1024]{2,1,0:T(8,128)(2,1)} %b_ref.9), custom_call_target="tpu_custom_call" | custom-call | flops 1600000000 | bytes 1024 | tf_op jit(solution)/shard_map/block_pairs/pallas_call | solution.py:89
  26.6 2.0 %collective-permute-start.4 = (bf16[256,1024]{1,0:T(8,128)(2,1)}, bf16[256,1024]{1,0:T(8,128)(2,1)S(1)}, u32[]{:S(2)}, u32[]{:S(2)}) collective-permute-start(bf16[256,1024]{1,0:T(8,128)(2,1)} %get-tuple-element.72), channel_id=1, source_target_pairs={{0,4},{4,0},{8,12},{12,8},{16,20},{20,16},{24,28},{28,24},{1,5},{5... | collective-permute-start | bytes 1572872 | tf_op jit(solution)/shard_map/ppermute | solution.py:26
  30.1 2.9 %collective-permute-done.2 = bf16[256,1024]{1,0:T(8,128)(2,1)} collective-permute-done((bf16[256,1024]{1,0:T(8,128)(2,1)}, bf16[256,1024]{1,0:T(8,128)(2,1)}, u32[]{:S(2)}, u32[]{:S(2)}) %collective-permute-start.2) | collective-permute-done | bytes 524320 | tf_op jit(solution)/shard_map/ppermute | solution.py:26
  35.1 2.0 %collective-permute-start.9 = (bf16[256,1024]{1,0:T(8,128)(2,1)}, bf16[256,1024]{1,0:T(8,128)(2,1)}, u32[]{:S(2)}, u32[]{:S(2)}) collective-permute-start(bf16[256,1024]{1,0:T(8,128)(2,1)} %collective-permute-done.2), channel_id=1, source_target_pairs={{0,8},{4,12},{8,0},{12,4},{16,24},{20,28},{24,16},{28,20},{1,9},{5... | collective-permute-start | bytes 1572872 | tf_op jit(solution)/shard_map/ppermute | solution.py:26
  37.1 5.9 %block_pairs.9 = (bf16[256,1024]{1,0:T(8,128)(2,1)}, bf16[256,1024]{1,0:T(8,128)(2,1)}) custom-call(s32[1]{0:T(128)} %bitcast.rank_ref, bf16[2,2048,2048]{2,1,0:T(8,128)(2,1)} %a_ref.7, bf16[2,2048,1024]{2,1,0:T(8,128)(2,1)} %b_ref.9), custom_call_target="tpu_custom_call" | custom-call | flops 1600000000 | bytes 1024 | tf_op jit(solution)/shard_map/block_pairs/pallas_call | solution.py:89
  44.2 2.1 %collective-permute-done.5.refs_3_ = bf16[256,1024]{1,0:T(8,128)(2,1)S(1)} collective-permute-done((bf16[256,1024]{1,0:T(8,128)(2,1)}, bf16[256,1024]{1,0:T(8,128)(2,1)S(1)}, u32[]{:S(2)}, u32[]{:S(2)}) %collective-permute-start.5) | collective-permute-done | bytes 524320 | tf_op jit(solution)/shard_map/ppermute | solution.py:26
  46.3 2.1 %collective-permute-start.7 = (bf16[256,1024]{1,0:T(8,128)(2,1)}, bf16[256,1024]{1,0:T(8,128)(2,1)}, u32[]{:S(2)}, u32[]{:S(2)}) collective-permute-start(bf16[256,1024]{1,0:T(8,128)(2,1)} %get-tuple-element.75), channel_id=1, source_target_pairs={{0,8},{4,12},{8,0},{12,4},{16,24},{20,28},{24,16},{28,20},{1,9},{5... | collective-permute-start | bytes 1572872 | tf_op jit(solution)/shard_map/ppermute | solution.py:26
  48.4 13.1 %block_pairs.8 = (bf16[256,1024]{1,0:T(8,128)(2,1)}, bf16[256,1024]{1,0:T(8,128)(2,1)}, bf16[256,1024]{1,0:T(8,128)(2,1)}, bf16[256,1024]{1,0:T(8,128)(2,1)}, bf...) custom-call(s32[1]{0:T(128)} %bitcast.rank_ref, bf16[2,2048,2048]{2,1,0:T(8,128)(2,1)} %a_ref.7, ...), custom_call_target="tpu_custom_call" | custom-call | flops 1600000000 | bytes 1024 | tf_op jit(solution)/shard_map/block_pairs/pallas_call | solution.py:89
  64.5 2.0 %gram_rows.5.refs_0_ = f32[16,128]{1,0:T(8,128)S(1)} custom-call(s32[1]{0:T(128)} %bitcast.rank_ref, bf16[256,1024]{1,0:T(8,128)(2,1)S(1)} %copy-done, bf16[256,1024]{1,0:T(8,128)(2,1)S(1)} %collective-permute-done.8.refs_1_, bf16[256,1024]{1,0:T(8,128)(2,1)S(1)} %collective-permute-done.3.refs_2_, bf16[256,1024]{1,0:T(8,128)(2,1)} %collective-permute-done.9.refs_3_, ...), custom_call_target="tpu_custom_call" | custom-call | flops 1024 | bytes 1024 | tf_op jit(solution)/shard_map/gram_rows/pallas_call | solution.py:49
  66.8 2.1 %collective-permute-done.7.refs_2_ = bf16[256,1024]{1,0:T(8,128)(2,1)} collective-permute-done((bf16[256,1024]{1,0:T(8,128)(2,1)}, bf16[256,1024]{1,0:T(8,128)(2,1)}, u32[]{:S(2)}, u32[]{:S(2)}) %collective-permute-start.7) | collective-permute-done | bytes 524320 | tf_op jit(solution)/shard_map/ppermute | solution.py:26
  72.4 4.8 %collective-permute-done.15 = bf16[256,1024]{1,0:T(8,128)(2,1)S(1)} collective-permute-done((bf16[256,1024]{1,0:T(8,128)(2,1)}, bf16[256,1024]{1,0:T(8,128)(2,1)S(1)}, u32[]{:S(2)}, u32[]{:S(2)}) %collective-permute-start.15) | collective-permute-done | bytes 524320 | tf_op jit(solution)/shard_map/ppermute | solution.py:26
  84.6 2.1 %collective-permute-done.14 = f32[16,128]{1,0:T(8,128)S(1)} collective-permute-done((f32[16,128]{1,0:T(8,128)S(1)}, f32[16,128]{1,0:T(8,128)S(1)}, u32[]{:S(2)}, u32[]{:S(2)}) %collective-permute-start.14) | collective-permute-done | bytes 8224 | tf_op jit(solution)/shard_map/ppermute | solution.py:26
  90.1 2.1 %collective-permute-done.19.refs_1_ = bf16[256,1024]{1,0:T(8,128)(2,1)S(1)} collective-permute-done((bf16[256,1024]{1,0:T(8,128)(2,1)}, bf16[256,1024]{1,0:T(8,128)(2,1)S(1)}, u32[]{:S(2)}, u32[]{:S(2)}) %collective-permute-start.19) | collective-permute-done | bytes 524320 | tf_op jit(solution)/shard_map/ppermute | solution.py:26
  94.0 2.0 %gram_rows.6.refs_4_ = f32[16,128]{1,0:T(8,128)S(1)} custom-call(s32[1]{0:T(128)} %bitcast.rank_ref, bf16[256,1024]{1,0:T(8,128)(2,1)S(1)} %copy-done.2, bf16[256,1024]{1,0:T(8,128)(2,1)S(1)} %collective-permute-done.19.refs_1_, bf16[256,1024]{1,0:T(8,128)(2,1)} %collective-permute-done.7.refs_2_, bf16[256,1024]{1,0:T(8,128)(2,1)S(1)} %collective-permute-done.20.refs_3_), custom_call_target="tpu_custom_call" | custom-call | flops 3200000000 | bytes 1024 | tf_op jit(solution)/shard_map/gram_rows/pallas_call | solution.py:49
  96.1 5.5 %collective-permute-done.17.refs_1_ = bf16[256,1024]{1,0:T(8,128)(2,1)S(1)} collective-permute-done((bf16[256,1024]{1,0:T(8,128)(2,1)}, bf16[256,1024]{1,0:T(8,128)(2,1)S(1)}, u32[]{:S(2)}, u32[]{:S(2)}) %collective-permute-start.17) | collective-permute-done | bytes 524320 | tf_op jit(solution)/shard_map/ppermute | solution.py:26
  105.4 2.1 %collective-permute-done.21 = f32[16,128]{1,0:T(8,128)S(1)} collective-permute-done((f32[16,128]{1,0:T(8,128)S(1)}, f32[16,128]{1,0:T(8,128)S(1)}, u32[]{:S(2)}, u32[]{:S(2)}) %collective-permute-start.21) | collective-permute-done | bytes 8224 | tf_op jit(solution)/shard_map/ppermute | solution.py:26
  107.5 5.5 %collective-permute-start.27 = (bf16[256,1024]{1,0:T(8,128)(2,1)S(1)}, bf16[256,1024]{1,0:T(8,128)(2,1)S(1)}, u32[]{:S(2)}, u32[]{:S(2)}) collective-permute-start(bf16[256,1024]{1,0:T(8,128)(2,1)S(1)} %group_combine.4), channel_id=1, source_target_pairs={{0,24},{4,28},{24,0},{28,4},{1,25},{5,29},{25,1},{29,5},{2,26},{6,... | collective-permute-start | bytes 1572872 | tf_op jit(solution)/shard_map/ppermute | solution.py:346
  122.7 4.2 %collective-permute-start.29 = (bf16[256,1024]{1,0:T(8,128)(2,1)S(1)}, bf16[256,1024]{1,0:T(8,128)(2,1)S(1)}, u32[]{:S(2)}, u32[]{:S(2)}) collective-permute-start(bf16[256,1024]{1,0:T(8,128)(2,1)S(1)} %group_combine.7), channel_id=1, source_target_pairs={{0,24},{4,28},{24,0},{28,4},{1,25},{5,29},{25,1},{29,5},{2,26},{6,... | collective-permute-start | bytes 1572872 | tf_op jit(solution)/shard_map/ppermute | solution.py:346
  128.9 10.2 %collective-permute-done.29.refs_2_.refs_5_ = bf16[256,1024]{1,0:T(8,128)(2,1)S(1)} collective-permute-done((bf16[256,1024]{1,0:T(8,128)(2,1)S(1)}, bf16[256,1024]{1,0:T(8,128)(2,1)S(1)}, u32[]{:S(2)}, u32[]{:S(2)}) %collective-permute-start.29) | collective-permute-done | bytes 524320 | tf_op jit(solution)/shard_map/ppermute | solution.py:346
  146.7 8.2 %collective-permute-start.35 = (f32[8,128]{1,0:T(8,128)S(1)}, f32[8,128]{1,0:T(8,128)S(1)}, u32[]{:S(2)}, u32[]{:S(2)}) collective-permute-start(f32[8,128]{1,0:T(8,128)S(1)} %total.6.refs_0_), channel_id=1, source_target_pairs={{0,16},{4,20},{8,24},{12,28},{16,0},{20,4},{24,8},{28,12},{1,17},{... | collective-permute-start | bytes 12296 | tf_op jit(solution)/shard_map/ppermute | solution.py:26
  156.5 2.0 %collective-permute-done.34.refs_1_ = f32[8,128]{1,0:T(8,128)S(1)} collective-permute-done((f32[8,128]{1,0:T(8,128)S(1)}, f32[8,128]{1,0:T(8,128)S(1)}, u32[]{:S(2)}, u32[]{:S(2)}) %collective-permute-start.34) | collective-permute-done | bytes 4128 | tf_op jit(solution)/shard_map/ppermute | solution.py:26
  (83 shorter events, 52.8 us)
Async XLA Ops:
  5.8 20.8 %collective-permute-start = (bf16[256,1024]{1,0:T(8,128)(2,1)}, bf16[256,1024]{1,0:T(8,128)(2,1)}, u32[]{:S(2)}, u32[]{:S(2)}) collective-permute-start(bf16[256,1024]{1,0:T(8,128)(2,1)} %get-tuple-element.60), channel_id=1, source_target_pairs={{0,4},{4,0},{8,12},{12,8},{16,20},{20,16},{24,28},{28,24},{1,5},{5... | collective-permute-start | bytes 1572872 | tf_op jit(solution)/shard_map/ppermute | solution.py:26
  8.8 17.8 %collective-permute-start.1 = (bf16[256,1024]{1,0:T(8,128)(2,1)}, bf16[256,1024]{1,0:T(8,128)(2,1)S(1)}, u32[]{:S(2)}, u32[]{:S(2)}) collective-permute-start(bf16[256,1024]{1,0:T(8,128)(2,1)} %get-tuple-element.61), channel_id=1, source_target_pairs={{0,8},{4,12},{8,0},{12,4},{16,24},{20,28},{24,16},{28,20},{1,9},{5... | collective-permute-start | bytes 1572872 | tf_op jit(solution)/shard_map/ppermute | solution.py:26
  16.2 16.9 %collective-permute-start.2 = (bf16[256,1024]{1,0:T(8,128)(2,1)}, bf16[256,1024]{1,0:T(8,128)(2,1)}, u32[]{:S(2)}, u32[]{:S(2)}) collective-permute-start(bf16[256,1024]{1,0:T(8,128)(2,1)} %get-tuple-element.65), channel_id=1, source_target_pairs={{0,4},{4,0},{8,12},{12,8},{16,20},{20,16},{24,28},{28,24},{1,5},{5... | collective-permute-start | bytes 1572872 | tf_op jit(solution)/shard_map/ppermute | solution.py:26
  16.7 18.3 %collective-permute-start.3 = (bf16[256,1024]{1,0:T(8,128)(2,1)}, bf16[256,1024]{1,0:T(8,128)(2,1)S(1)}, u32[]{:S(2)}, u32[]{:S(2)}) collective-permute-start(bf16[256,1024]{1,0:T(8,128)(2,1)} %get-tuple-element.66), channel_id=1, source_target_pairs={{0,8},{4,12},{8,0},{12,4},{16,24},{20,28},{24,16},{28,20},{1,9},{5... | collective-permute-start | bytes 1572872 | tf_op jit(solution)/shard_map/ppermute | solution.py:26
  26.6 17.6 %collective-permute-start.4 = (bf16[256,1024]{1,0:T(8,128)(2,1)}, bf16[256,1024]{1,0:T(8,128)(2,1)S(1)}, u32[]{:S(2)}, u32[]{:S(2)}) collective-permute-start(bf16[256,1024]{1,0:T(8,128)(2,1)} %get-tuple-element.72), channel_id=1, source_target_pairs={{0,4},{4,0},{8,12},{12,8},{16,20},{20,16},{24,28},{28,24},{1,5},{5... | collective-permute-start | bytes 1572872 | tf_op jit(solution)/shard_map/ppermute | solution.py:26
  28.6 17.7 %collective-permute-start.5 = (bf16[256,1024]{1,0:T(8,128)(2,1)}, bf16[256,1024]{1,0:T(8,128)(2,1)S(1)}, u32[]{:S(2)}, u32[]{:S(2)}) collective-permute-start(bf16[256,1024]{1,0:T(8,128)(2,1)} %collective-permute-done), channel_id=1, source_target_pairs={{0,8},{4,12},{8,0},{12,4},{16,24},{20,28},{24,16},{28,20},{1,9},{5... | collective-permute-start | bytes 1572872 | tf_op jit(solution)/shard_map/ppermute | solution.py:26
  35.1 26.4 %collective-permute-start.8 = (bf16[256,1024]{1,0:T(8,128)(2,1)}, bf16[256,1024]{1,0:T(8,128)(2,1)S(1)}, u32[]{:S(2)}, u32[]{:S(2)}) collective-permute-start(bf16[256,1024]{1,0:T(8,128)(2,1)} %get-tuple-element.81), channel_id=1, source_target_pairs={{0,4},{4,0},{8,12},{12,8},{16,20},{20,16},{24,28},{28,24},{1,5},{5... | collective-permute-start | bytes 1572872 | tf_op jit(solution)/shard_map/ppermute | solution.py:26
  35.1 26.4 %collective-permute-start.9 = (bf16[256,1024]{1,0:T(8,128)(2,1)}, bf16[256,1024]{1,0:T(8,128)(2,1)}, u32[]{:S(2)}, u32[]{:S(2)}) collective-permute-start(bf16[256,1024]{1,0:T(8,128)(2,1)} %collective-permute-done.2), channel_id=1, source_target_pairs={{0,8},{4,12},{8,0},{12,4},{16,24},{20,28},{24,16},{28,20},{1,9},{5... | collective-permute-start | bytes 1572872 | tf_op jit(solution)/shard_map/ppermute | solution.py:26
  46.3 20.5 %collective-permute-start.6 = (bf16[256,1024]{1,0:T(8,128)(2,1)}, bf16[256,1024]{1,0:T(8,128)(2,1)}, u32[]{:S(2)}, u32[]{:S(2)}) collective-permute-start(bf16[256,1024]{1,0:T(8,128)(2,1)} %get-tuple-element.74), channel_id=1, source_target_pairs={{0,4},{4,0},{8,12},{12,8},{16,20},{20,16},{24,28},{28,24},{1,5},{5... | collective-permute-start | bytes 1572872 | tf_op jit(solution)/shard_map/ppermute | solution.py:26
  46.3 22.5 %collective-permute-start.7 = (bf16[256,1024]{1,0:T(8,128)(2,1)}, bf16[256,1024]{1,0:T(8,128)(2,1)}, u32[]{:S(2)}, u32[]{:S(2)}) collective-permute-start(bf16[256,1024]{1,0:T(8,128)(2,1)} %get-tuple-element.75), channel_id=1, source_target_pairs={{0,8},{4,12},{8,0},{12,4},{16,24},{20,28},{24,16},{28,20},{1,9},{5... | collective-permute-start | bytes 1572872 | tf_op jit(solution)/shard_map/ppermute | solution.py:26
  61.5 15.6 %collective-permute-start.15 = (bf16[256,1024]{1,0:T(8,128)(2,1)}, bf16[256,1024]{1,0:T(8,128)(2,1)S(1)}, u32[]{:S(2)}, u32[]{:S(2)}) collective-permute-start(bf16[256,1024]{1,0:T(8,128)(2,1)} %get-tuple-element.96), channel_id=1, source_target_pairs={{0,4},{4,0},{8,12},{12,8},{16,20},{20,16},{24,28},{28,24},{1,5},{5... | collective-permute-start | bytes 1572872 | tf_op jit(solution)/shard_map/ppermute | solution.py:26
  63.1 15.9 %collective-permute-start.16 = (bf16[256,1024]{1,0:T(8,128)(2,1)}, bf16[256,1024]{1,0:T(8,128)(2,1)S(1)}, u32[]{:S(2)}, u32[]{:S(2)}) collective-permute-start(bf16[256,1024]{1,0:T(8,128)(2,1)} %get-tuple-element.97), channel_id=1, source_target_pairs={{0,8},{4,12},{8,0},{12,4},{16,24},{20,28},{24,16},{28,20},{1,9},{5... | collective-permute-start | bytes 1572872 | tf_op jit(solution)/shard_map/ppermute | solution.py:26
  68.9 11.7 %collective-permute-start.12 = (f32[16,128]{1,0:T(8,128)S(1)}, f32[16,128]{1,0:T(8,128)S(1)}, u32[]{:S(2)}, u32[]{:S(2)}) collective-permute-start(f32[16,128]{1,0:T(8,128)S(1)} %gram_rows.5.refs_0_), channel_id=1, source_target_pairs={{0,12},{4,8},{8,4},{12,0},{16,28},{20,24},{24,20},{28,16},{1,13},{... | collective-permute-start | bytes 24584 | tf_op jit(solution)/shard_map/ppermute | solution.py:26
  70.4 10.7 %collective-permute-start.11 = (f32[16,128]{1,0:T(8,128)S(1)}, f32[16,128]{1,0:T(8,128)S(1)}, u32[]{:S(2)}, u32[]{:S(2)}) collective-permute-start(f32[16,128]{1,0:T(8,128)S(1)} %gram_rows.5.refs_0_), channel_id=1, source_target_pairs={{0,8},{4,12},{8,0},{12,4},{16,24},{20,28},{24,16},{28,20},{1,9},{5... | collective-permute-start | bytes 24584 | tf_op jit(solution)/shard_map/ppermute | solution.py:26
  70.4 11.4 %collective-permute-start.10 = (f32[16,128]{1,0:T(8,128)S(1)}, f32[16,128]{1,0:T(8,128)S(1)}, u32[]{:S(2)}, u32[]{:S(2)}) collective-permute-start(f32[16,128]{1,0:T(8,128)S(1)} %gram_rows.5.refs_0_), channel_id=1, source_target_pairs={{0,4},{4,0},{8,12},{12,8},{16,20},{20,16},{24,28},{28,24},{1,5},{5... | collective-permute-start | bytes 24584 | tf_op jit(solution)/shard_map/ppermute | solution.py:26
  77.1 15.1 %collective-permute-start.19 = (bf16[256,1024]{1,0:T(8,128)(2,1)}, bf16[256,1024]{1,0:T(8,128)(2,1)S(1)}, u32[]{:S(2)}, u32[]{:S(2)}) collective-permute-start(bf16[256,1024]{1,0:T(8,128)(2,1)} %get-tuple-element.102), channel_id=1, source_target_pairs={{0,4},{4,0},{8,12},{12,8},{16,20},{20,16},{24,28},{28,24},{1,5},{5... | collective-permute-start | bytes 1572872 | tf_op jit(solution)/shard_map/ppermute | solution.py:26
  79.0 15.1 %collective-permute-start.20 = (bf16[256,1024]{1,0:T(8,128)(2,1)}, bf16[256,1024]{1,0:T(8,128)(2,1)S(1)}, u32[]{:S(2)}, u32[]{:S(2)}) collective-permute-start(bf16[256,1024]{1,0:T(8,128)(2,1)} %collective-permute-done.6), channel_id=1, source_target_pairs={{0,8},{4,12},{8,0},{12,4},{16,24},{20,28},{24,16},{28,20},{1,9},{5... | collective-permute-start | bytes 1572872 | tf_op jit(solution)/shard_map/ppermute | solution.py:26
  80.6 21.0 %collective-permute-start.17 = (bf16[256,1024]{1,0:T(8,128)(2,1)}, bf16[256,1024]{1,0:T(8,128)(2,1)S(1)}, u32[]{:S(2)}, u32[]{:S(2)}) collective-permute-start(bf16[256,1024]{1,0:T(8,128)(2,1)} %get-tuple-element.98), channel_id=1, source_target_pairs={{0,4},{4,0},{8,12},{12,8},{16,20},{20,16},{24,28},{28,24},{1,5},{5... | collective-permute-start | bytes 1572872 | tf_op jit(solution)/shard_map/ppermute | solution.py:26
  81.1 21.7 %collective-permute-start.18 = (bf16[256,1024]{1,0:T(8,128)(2,1)S(1)}, bf16[256,1024]{1,0:T(8,128)(2,1)S(1)}, u32[]{:S(2)}, u32[]{:S(2)}) collective-permute-start(bf16[256,1024]{1,0:T(8,128)(2,1)S(1)} %collective-permute-done.15), channel_id=1, source_target_pairs={{0,8},{4,12},{8,0},{12,4},{16,24},{20,28},{24,16},{28,20},{1,9},{5... | collective-permute-start | bytes 1572872 | tf_op jit(solution)/shard_map/ppermute | solution.py:26
  89.4 24.8 %collective-permute-start.23 = (bf16[256,1024]{1,0:T(8,128)(2,1)S(1)}, bf16[256,1024]{1,0:T(8,128)(2,1)S(1)}, u32[]{:S(2)}, u32[]{:S(2)}) collective-permute-start(bf16[256,1024]{1,0:T(8,128)(2,1)S(1)} %group_combine.4), channel_id=1, source_target_pairs={{8,16},{12,20},{16,8},{20,12},{9,17},{13,21},{17,9},{21,13},{10,18... | collective-permute-start | bytes 1572872 | tf_op jit(solution)/shard_map/ppermute | solution.py:346
  107.5 15.3 %collective-permute-start.27 = (bf16[256,1024]{1,0:T(8,128)(2,1)S(1)}, bf16[256,1024]{1,0:T(8,128)(2,1)S(1)}, u32[]{:S(2)}, u32[]{:S(2)}) collective-permute-start(bf16[256,1024]{1,0:T(8,128)(2,1)S(1)} %group_combine.4), channel_id=1, source_target_pairs={{0,24},{4,28},{24,0},{28,4},{1,25},{5,29},{25,1},{29,5},{2,26},{6,... | collective-permute-start | bytes 1572872 | tf_op jit(solution)/shard_map/ppermute | solution.py:346
  122.7 16.4 %collective-permute-start.29 = (bf16[256,1024]{1,0:T(8,128)(2,1)S(1)}, bf16[256,1024]{1,0:T(8,128)(2,1)S(1)}, u32[]{:S(2)}, u32[]{:S(2)}) collective-permute-start(bf16[256,1024]{1,0:T(8,128)(2,1)S(1)} %group_combine.7), channel_id=1, source_target_pairs={{0,24},{4,28},{24,0},{28,4},{1,25},{5,29},{25,1},{29,5},{2,26},{6,... | collective-permute-start | bytes 1572872 | tf_op jit(solution)/shard_map/ppermute | solution.py:346
  126.9 12.2 %collective-permute-start.28 = (bf16[256,1024]{1,0:T(8,128)(2,1)S(1)}, bf16[256,1024]{1,0:T(8,128)(2,1)S(1)}, u32[]{:S(2)}, u32[]{:S(2)}) collective-permute-start(bf16[256,1024]{1,0:T(8,128)(2,1)S(1)} %group_combine.7), channel_id=1, source_target_pairs={{8,16},{12,20},{16,8},{20,12},{9,17},{13,21},{17,9},{21,13},{10,18... | collective-permute-start | bytes 1572872 | tf_op jit(solution)/shard_map/ppermute | solution.py:346
  146.7 9.8 %collective-permute-start.35 = (f32[8,128]{1,0:T(8,128)S(1)}, f32[8,128]{1,0:T(8,128)S(1)}, u32[]{:S(2)}, u32[]{:S(2)}) collective-permute-start(f32[8,128]{1,0:T(8,128)S(1)} %total.6.refs_0_), channel_id=1, source_target_pairs={{0,16},{4,20},{8,24},{12,28},{16,0},{20,4},{24,8},{28,12},{1,17},{... | collective-permute-start | bytes 12296 | tf_op jit(solution)/shard_map/ppermute | solution.py:26
  (17 other events, 144.4 us)

commit v5 on v4

--- a/solution.py
+++ b/solution.py
@@ -108,11 +108,6 @@
     return list(zip(values[::2], values[1::2]))
 
 
-def pair_row(first, second):
-    low, high = jnp.minimum(first, second), jnp.maximum(first, second)
-    return low * (2 * GROUP - 1 - low) // 2 + high
-
-
 def tiles(rows, width, step, start):
     def body(index, carry):
         where = pl.ds(pl.multiple_of(index * STRIDE, STRIDE), STRIDE)
@@ -125,26 +120,39 @@
 
 def gram_rows(rank, parts, before, cost):
     rows, width = parts[0].shape
-    pairs = [(u, v) for u in range(GROUP) for v in range(u, GROUP)]
 
     def kernel(rank_ref, *refs):
         ins, out = refs[:GROUP], refs[-1]
 
         def step(where, columns, totals):
             wide = [ref[where, columns].astype(jnp.float32) for ref in ins]
-            new = []
-            for total, (u, v) in zip(totals, pairs):
-                product = wide[u] * wide[v]
-                new.append(total + (product[:8] + product[8:]))
-            return tuple(new)
+            products = []
+            for first, second in (wide[:2], wide[2:]):
+                both, apart = first + second, first - second
+                products += [first * first, second * second, first * second]
+                products += [both * both, apart * apart, both * apart]
+            products += [first * second for first in wide[:2] for second in wide[2:]]
+            return tuple(
+                total + (product[:8] + product[8:]) for total, product in zip(totals, products)
+            )
 
         zero = jnp.zeros((8, LANES), jnp.float32)
-        totals = tiles(rows, width, step, (zero,) * len(pairs))
+        totals = tiles(rows, width, step, (zero,) * GRAM_ROWS)
         out[...] = jnp.zeros_like(out) if before is None else refs[GROUP][...]
-        mine = rank_ref[0] & (GROUP - 1)
-        for total, (u, v) in zip(totals, pairs):
-            row = pl.ds(pair_row(mine ^ u, mine ^ v), 1)
-            out[row, :] = out[row, :] + jnp.sum(total, axis=0, keepdims=True)
+        odd, upper = rank_ref[0] & 1, (rank_ref[0] >> 1) & 1
+        sign = jnp.where(odd == 1, -1.0, 1.0)
+        places = []
+        for base in (6 * upper, 6 - 6 * upper):
+            places += [base + odd, base + 1 - odd] + [base + k for k in range(2, 6)]
+        for u in range(2):
+            for v in range(2):
+                near, far = u ^ odd, v ^ odd
+                places.append(12 + jnp.where(upper == 1, 2 * far + near, 2 * near + far))
+        for number, (place, value) in enumerate(zip(places, totals)):
+            value = jnp.sum(value, axis=0, keepdims=True)
+            if number in (5, 11):
+                value = sign * value
+            out[pl.ds(place, 1), :] = out[pl.ds(place, 1), :] + value
 
     shape = jax.ShapeDtypeStruct((GRAM_ROWS, LANES), jnp.float32)
     inputs = list(parts) + ([] if before is None else [before])
@@ -189,25 +197,29 @@
         ins, outs = refs[: GROUP * len(block_parts)], refs[GROUP * len(block_parts) :]
         sums = jnp.sum(gram_ref[...], axis=1, keepdims=True)
 
-        def entry(i, j):
-            low, high = min(i, j), max(i, j)
-            row = low * (2 * GROUP - 1 - low) // 2 + high
-            return sums[row : row + 1]
-
-        def norm(i, j, left, right):
-            value = left * left * entry(i, i) + right * right * entry(j, j)
-            return jnp.maximum(value + 2.0 * (left * right * entry(i, j)), 0.0)
-
-        low_first, low_second = scale_pair(entry(0, 1), entry(0, 0), entry(1, 1))
-        high_first, high_second = scale_pair(entry(2, 3), entry(2, 2), entry(3, 3))
-        dot_value = (
-            low_first * high_first * entry(0, 2)
-            + low_first * high_second * entry(0, 3)
-            + low_second * high_first * entry(1, 2)
-            + low_second * high_second * entry(1, 3)
-        )
-        norm_low = norm(0, 1, low_first, low_second)
-        norm_high = norm(2, 3, high_first, high_second)
+        entries = [sums[row : row + 1] for row in range(GRAM_ROWS)]
+
+        def scaled(base):
+            first_norm, second_norm, dot_value, both, apart, across = entries[base : base + 6]
+            first, second = scale_pair(dot_value, first_norm, second_norm)
+            half_sum, half_gap = 0.5 * (first + second), 0.5 * (first - second)
+            plain = first * first * first_norm + second * second * second_norm
+            plain_cross = 2.0 * (first * second * dot_value)
+            turned = half_sum * half_sum * both + half_gap * half_gap * apart
+            turned_cross = 2.0 * (half_sum * half_gap * across)
+            norm = jnp.where(
+                plain + jnp.abs(plain_cross) <= turned + jnp.abs(turned_cross),
+                plain + plain_cross,
+                turned + turned_cross,
+            )
+            return first, second, jnp.maximum(norm, 0.0)
+
+        low_first, low_second, norm_low = scaled(0)
+        high_first, high_second, norm_high = scaled(6)
+        dot_value = low_first * (high_first * entries[12] + high_second * entries[13])
+        dot_value = dot_value + low_second * (high_first * entries[14] + high_second * entries[15])
+        limit = jnp.sqrt(norm_low) * jnp.sqrt(norm_high)
+        dot_value = jnp.clip(dot_value, -limit, limit)
         top_first, top_second = scale_pair(dot_value, norm_low, norm_high)
 
         odd = (rank_ref[0] & 1) == 1

time: 161 us -> 161 us (level)
  Pallas kernels: 54.7 us -> 56.9 us
    pallas_call x11, Pallas kernels: 14.2 us -> 16.3 us  [call(): pl.pallas_call(kernel, in_specs=[pl.BlockSpec(memory_space=pltpu.SMEM)] +...]
    ppermute x31, waiting for transfers between devices: 39.8 us -> 38.1 us  [exchange(): lax.ppermute(value, axis, [(i, i ^ mask) for i in range(lax.axis_size(axi...]
  transfers between devices with their start and end apart: 37 -> 37, of which waited for: 24 -> 23; matrix products, arithmetic and copies ran while one was open for 0% -> 0% of each run, Pallas kernels for 29% -> 30%
where the time goes in v5:
time: 161 us
  Pallas kernels  56.9 us (35%)
  starting transfers between devices  53.4 us (33%)
  waiting for transfers between devices  50.5 us (31%)
    pallas_call x5, Pallas kernels, block_pairs(): pl.pallas_call(kernel, grid_spec=pltpu.PrefetchScalarGridSpec(num_scalar_...  40.5 us
    ppermute x31, starting transfers between devices, exchange(): lax.ppermute(value, axis, [(i, i ^ mask) for i in range(lax.axis_size(axi...  40.3 us
    ppermute x31, waiting for transfers between devices, exchange(): lax.ppermute(value, axis, [(i, i ^ mask) for i in range(lax.axis_size(axi...  38.1 us
    pallas_call x11, Pallas kernels, call(): pl.pallas_call(kernel, in_specs=[pl.BlockSpec(memory_space=pltpu.SMEM)] +...  16.3 us
    ppermute x4, starting transfers between devices, swap(): return lax.ppermute(value, 'rep', pairs)  11 us
    ppermute x4, waiting for transfers between devices, swap(): return lax.ppermute(value, 'rep', pairs)  10.2 us
  transfers between devices with their start and end apart: 37, of which 23 were waited for; matrix products, arithmetic and copies ran while one was open for 0% of the time, Pallas kernels for 30%

profile of v5, /device:TPU:0, one launch (start us, length us, event | category | flops | bytes accessed | tf_op | source)
XLA Modules:
  0.0 160.9 jit_solution(536113208596416732)
XLA Ops:
  0.0 5.8 %block_pairs.6 = (bf16[256,1024]{1,0:T(8,128)(2,1)}, bf16[256,1024]{1,0:T(8,128)(2,1)}) custom-call(s32[1]{0:T(128)} %bitcast.rank_ref, bf16[2,2048,2048]{2,1,0:T(8,128)(2,1)} %a_ref.7, bf16[2,2048,1024]{2,1,0:T(8,128)(2,1)} %b_ref.9), custom_call_target="tpu_custom_call" | custom-call | flops 1600000000 | bytes 1024 | tf_op jit(solution)/shard_map/block_pairs/pallas_call | solution.py:89
  5.8 2.9 %collective-permute-start = (bf16[256,1024]{1,0:T(8,128)(2,1)}, bf16[256,1024]{1,0:T(8,128)(2,1)}, u32[]{:S(2)}, u32[]{:S(2)}) collective-permute-start(bf16[256,1024]{1,0:T(8,128)(2,1)} %get-tuple-element.60), channel_id=1, source_target_pairs={{0,4},{4,0},{8,12},{12,8},{16,20},{20,16},{24,28},{28,24},{1,5},{5... | collective-permute-start | bytes 1572872 | tf_op jit(solution)/shard_map/ppermute | solution.py:26
  10.3 5.9 %block_pairs.7 = (bf16[256,1024]{1,0:T(8,128)(2,1)}, bf16[256,1024]{1,0:T(8,128)(2,1)}) custom-call(s32[1]{0:T(128)} %bitcast.rank_ref, bf16[2,2048,2048]{2,1,0:T(8,128)(2,1)} %a_ref.7, bf16[2,2048,1024]{2,1,0:T(8,128)(2,1)} %b_ref.9), custom_call_target="tpu_custom_call" | custom-call | flops 1600000000 | bytes 1024 | tf_op jit(solution)/shard_map/block_pairs/pallas_call | solution.py:89
  16.7 9.8 %block_pairs.5 = (bf16[256,1024]{1,0:T(8,128)(2,1)}, bf16[256,1024]{1,0:T(8,128)(2,1)}, bf16[256,1024]{1,0:T(8,128)(2,1)}, bf16[256,1024]{1,0:T(8,128)(2,1)}) custom-call(s32[1]{0:T(128)} %bitcast.rank_ref, bf16[2,2048,2048]{2,1,0:T(8,128)(2,1)} %a_ref.7, bf16[2,2048,1024]{2,1,0:T(8,128)(2,1)} %b_ref.9), custom_call_target="tpu_custom_call" | custom-call | flops 1600000000 | bytes 1024 | tf_op jit(solution)/shard_map/block_pairs/pallas_call | solution.py:89
  26.6 2.0 %collective-permute-start.4 = (bf16[256,1024]{1,0:T(8,128)(2,1)}, bf16[256,1024]{1,0:T(8,128)(2,1)S(1)}, u32[]{:S(2)}, u32[]{:S(2)}) collective-permute-start(bf16[256,1024]{1,0:T(8,128)(2,1)} %get-tuple-element.72), channel_id=1, source_target_pairs={{0,4},{4,0},{8,12},{12,8},{16,20},{20,16},{24,28},{28,24},{1,5},{5... | collective-permute-start | bytes 1572872 | tf_op jit(solution)/shard_map/ppermute | solution.py:26
  30.1 2.9 %collective-permute-done.2 = bf16[256,1024]{1,0:T(8,128)(2,1)} collective-permute-done((bf16[256,1024]{1,0:T(8,128)(2,1)}, bf16[256,1024]{1,0:T(8,128)(2,1)}, u32[]{:S(2)}, u32[]{:S(2)}) %collective-permute-start.2) | collective-permute-done | bytes 524320 | tf_op jit(solution)/shard_map/ppermute | solution.py:26
  33.1 2.0 %collective-permute-done.3.refs_2_ = bf16[256,1024]{1,0:T(8,128)(2,1)S(1)} collective-permute-done((bf16[256,1024]{1,0:T(8,128)(2,1)}, bf16[256,1024]{1,0:T(8,128)(2,1)S(1)}, u32[]{:S(2)}, u32[]{:S(2)}) %collective-permute-start.3) | collective-permute-done | bytes 524320 | tf_op jit(solution)/shard_map/ppermute | solution.py:26
  35.1 2.0 %collective-permute-start.9 = (bf16[256,1024]{1,0:T(8,128)(2,1)}, bf16[256,1024]{1,0:T(8,128)(2,1)}, u32[]{:S(2)}, u32[]{:S(2)}) collective-permute-start(bf16[256,1024]{1,0:T(8,128)(2,1)} %collective-permute-done.2), channel_id=1, source_target_pairs={{0,8},{4,12},{8,0},{12,4},{16,24},{20,28},{24,16},{28,20},{1,9},{5... | collective-permute-start | bytes 1572872 | tf_op jit(solution)/shard_map/ppermute | solution.py:26
  37.1 5.9 %block_pairs.9 = (bf16[256,1024]{1,0:T(8,128)(2,1)}, bf16[256,1024]{1,0:T(8,128)(2,1)}) custom-call(s32[1]{0:T(128)} %bitcast.rank_ref, bf16[2,2048,2048]{2,1,0:T(8,128)(2,1)} %a_ref.7, bf16[2,2048,1024]{2,1,0:T(8,128)(2,1)} %b_ref.9), custom_call_target="tpu_custom_call" | custom-call | flops 1600000000 | bytes 1024 | tf_op jit(solution)/shard_map/block_pairs/pallas_call | solution.py:89
  44.2 2.1 %collective-permute-done.5.refs_3_ = bf16[256,1024]{1,0:T(8,128)(2,1)S(1)} collective-permute-done((bf16[256,1024]{1,0:T(8,128)(2,1)}, bf16[256,1024]{1,0:T(8,128)(2,1)S(1)}, u32[]{:S(2)}, u32[]{:S(2)}) %collective-permute-start.5) | collective-permute-done | bytes 524320 | tf_op jit(solution)/shard_map/ppermute | solution.py:26
  46.3 2.1 %collective-permute-start.7 = (bf16[256,1024]{1,0:T(8,128)(2,1)}, bf16[256,1024]{1,0:T(8,128)(2,1)}, u32[]{:S(2)}, u32[]{:S(2)}) collective-permute-start(bf16[256,1024]{1,0:T(8,128)(2,1)} %get-tuple-element.75), channel_id=1, source_target_pairs={{0,8},{4,12},{8,0},{12,4},{16,24},{20,28},{24,16},{28,20},{1,9},{5... | collective-permute-start | bytes 1572872 | tf_op jit(solution)/shard_map/ppermute | solution.py:26
  48.4 13.1 %block_pairs.8 = (bf16[256,1024]{1,0:T(8,128)(2,1)}, bf16[256,1024]{1,0:T(8,128)(2,1)}, bf16[256,1024]{1,0:T(8,128)(2,1)}, bf16[256,1024]{1,0:T(8,128)(2,1)}, bf...) custom-call(s32[1]{0:T(128)} %bitcast.rank_ref, bf16[2,2048,2048]{2,1,0:T(8,128)(2,1)} %a_ref.7, ...), custom_call_target="tpu_custom_call" | custom-call | flops 1600000000 | bytes 1024 | tf_op jit(solution)/shard_map/block_pairs/pallas_call | solution.py:89
  65.1 2.6 %gram_rows.5.refs_0_ = f32[16,128]{1,0:T(8,128)S(1)} custom-call(s32[1]{0:T(128)} %bitcast.rank_ref, bf16[256,1024]{1,0:T(8,128)(2,1)S(1)} %copy-done, bf16[256,1024]{1,0:T(8,128)(2,1)S(1)} %collective-permute-done.8.refs_1_, bf16[256,1024]{1,0:T(8,128)(2,1)S(1)} %collective-permute-done.3.refs_2_, bf16[256,1024]{1,0:T(8,128)(2,1)} %collective-permute-done.9.refs_3_, ...), custom_call_target="tpu_custom_call" | custom-call | flops 1024 | bytes 1024 | tf_op jit(solution)/shard_map/gram_rows/pallas_call | solution.py:49
  72.4 4.8 %collective-permute-done.15 = bf16[256,1024]{1,0:T(8,128)(2,1)S(1)} collective-permute-done((bf16[256,1024]{1,0:T(8,128)(2,1)}, bf16[256,1024]{1,0:T(8,128)(2,1)S(1)}, u32[]{:S(2)}, u32[]{:S(2)}) %collective-permute-start.15) | collective-permute-done | bytes 524320 | tf_op jit(solution)/shard_map/ppermute | solution.py:26
  84.6 2.1 %collective-permute-done.14 = f32[16,128]{1,0:T(8,128)S(1)} collective-permute-done((f32[16,128]{1,0:T(8,128)S(1)}, f32[16,128]{1,0:T(8,128)S(1)}, u32[]{:S(2)}, u32[]{:S(2)}) %collective-permute-start.14) | collective-permute-done | bytes 8224 | tf_op jit(solution)/shard_map/ppermute | solution.py:26
  90.2 2.0 %collective-permute-done.19.refs_1_ = bf16[256,1024]{1,0:T(8,128)(2,1)S(1)} collective-permute-done((bf16[256,1024]{1,0:T(8,128)(2,1)}, bf16[256,1024]{1,0:T(8,128)(2,1)S(1)}, u32[]{:S(2)}, u32[]{:S(2)}) %collective-permute-start.19) | collective-permute-done | bytes 524320 | tf_op jit(solution)/shard_map/ppermute | solution.py:26
  94.0 2.6 %gram_rows.6.refs_4_ = f32[16,128]{1,0:T(8,128)S(1)} custom-call(s32[1]{0:T(128)} %bitcast.rank_ref, bf16[256,1024]{1,0:T(8,128)(2,1)S(1)} %copy-done.2, bf16[256,1024]{1,0:T(8,128)(2,1)S(1)} %collective-permute-done.19.refs_1_, bf16[256,1024]{1,0:T(8,128)(2,1)} %collective-permute-done.7.refs_2_, bf16[256,1024]{1,0:T(8,128)(2,1)S(1)} %collective-permute-done.20.refs_3_), custom_call_target="tpu_custom_call" | custom-call | flops 3200000000 | bytes 1024 | tf_op jit(solution)/shard_map/gram_rows/pallas_call | solution.py:49
  96.6 5.0 %collective-permute-done.17.refs_1_ = bf16[256,1024]{1,0:T(8,128)(2,1)S(1)} collective-permute-done((bf16[256,1024]{1,0:T(8,128)(2,1)}, bf16[256,1024]{1,0:T(8,128)(2,1)S(1)}, u32[]{:S(2)}, u32[]{:S(2)}) %collective-permute-start.17) | collective-permute-done | bytes 524320 | tf_op jit(solution)/shard_map/ppermute | solution.py:26
  105.9 2.1 %collective-permute-done.21 = f32[16,128]{1,0:T(8,128)S(1)} collective-permute-done((f32[16,128]{1,0:T(8,128)S(1)}, f32[16,128]{1,0:T(8,128)S(1)}, u32[]{:S(2)}, u32[]{:S(2)}) %collective-permute-start.21) | collective-permute-done | bytes 8224 | tf_op jit(solution)/shard_map/ppermute | solution.py:26
  108.0 5.5 %collective-permute-start.27 = (bf16[256,1024]{1,0:T(8,128)(2,1)S(1)}, bf16[256,1024]{1,0:T(8,128)(2,1)S(1)}, u32[]{:S(2)}, u32[]{:S(2)}) collective-permute-start(bf16[256,1024]{1,0:T(8,128)(2,1)S(1)} %group_combine.4), channel_id=1, source_target_pairs={{0,24},{4,28},{24,0},{28,4},{1,25},{5,29},{25,1},{29,5},{2,26},{6,... | collective-permute-start | bytes 1572872 | tf_op jit(solution)/shard_map/ppermute | solution.py:358
  123.3 4.2 %collective-permute-start.29 = (bf16[256,1024]{1,0:T(8,128)(2,1)S(1)}, bf16[256,1024]{1,0:T(8,128)(2,1)S(1)}, u32[]{:S(2)}, u32[]{:S(2)}) collective-permute-start(bf16[256,1024]{1,0:T(8,128)(2,1)S(1)} %group_combine.7), channel_id=1, source_target_pairs={{0,24},{4,28},{24,0},{28,4},{1,25},{5,29},{25,1},{29,5},{2,26},{6,... | collective-permute-start | bytes 1572872 | tf_op jit(solution)/shard_map/ppermute | solution.py:358
  129.4 10.2 %collective-permute-done.29.refs_2_.refs_5_ = bf16[256,1024]{1,0:T(8,128)(2,1)S(1)} collective-permute-done((bf16[256,1024]{1,0:T(8,128)(2,1)S(1)}, bf16[256,1024]{1,0:T(8,128)(2,1)S(1)}, u32[]{:S(2)}, u32[]{:S(2)}) %collective-permute-start.29) | collective-permute-done | bytes 524320 | tf_op jit(solution)/shard_map/ppermute | solution.py:358
  147.2 8.2 %collective-permute-start.35 = (f32[8,128]{1,0:T(8,128)S(1)}, f32[8,128]{1,0:T(8,128)S(1)}, u32[]{:S(2)}, u32[]{:S(2)}) collective-permute-start(f32[8,128]{1,0:T(8,128)S(1)} %total.6.refs_0_), channel_id=1, source_target_pairs={{0,16},{4,20},{8,24},{12,28},{16,0},{20,4},{24,8},{28,12},{1,17},{... | collective-permute-start | bytes 12296 | tf_op jit(solution)/shard_map/ppermute | solution.py:26
  157.0 2.0 %collective-permute-done.34.refs_1_ = f32[8,128]{1,0:T(8,128)S(1)} collective-permute-done((f32[8,128]{1,0:T(8,128)S(1)}, f32[8,128]{1,0:T(8,128)S(1)}, u32[]{:S(2)}, u32[]{:S(2)}) %collective-permute-start.34) | collective-permute-done | bytes 4128 | tf_op jit(solution)/shard_map/ppermute | solution.py:26
  (83 shorter events, 52.9 us)
Async XLA Ops:
  5.8 20.8 %collective-permute-start = (bf16[256,1024]{1,0:T(8,128)(2,1)}, bf16[256,1024]{1,0:T(8,128)(2,1)}, u32[]{:S(2)}, u32[]{:S(2)}) collective-permute-start(bf16[256,1024]{1,0:T(8,128)(2,1)} %get-tuple-element.60), channel_id=1, source_target_pairs={{0,4},{4,0},{8,12},{12,8},{16,20},{20,16},{24,28},{28,24},{1,5},{5... | collective-permute-start | bytes 1572872 | tf_op jit(solution)/shard_map/ppermute | solution.py:26
  8.8 17.8 %collective-permute-start.1 = (bf16[256,1024]{1,0:T(8,128)(2,1)}, bf16[256,1024]{1,0:T(8,128)(2,1)S(1)}, u32[]{:S(2)}, u32[]{:S(2)}) collective-permute-start(bf16[256,1024]{1,0:T(8,128)(2,1)} %get-tuple-element.61), channel_id=1, source_target_pairs={{0,8},{4,12},{8,0},{12,4},{16,24},{20,28},{24,16},{28,20},{1,9},{5... | collective-permute-start | bytes 1572872 | tf_op jit(solution)/shard_map/ppermute | solution.py:26
  16.2 16.9 %collective-permute-start.2 = (bf16[256,1024]{1,0:T(8,128)(2,1)}, bf16[256,1024]{1,0:T(8,128)(2,1)}, u32[]{:S(2)}, u32[]{:S(2)}) collective-permute-start(bf16[256,1024]{1,0:T(8,128)(2,1)} %get-tuple-element.65), channel_id=1, source_target_pairs={{0,4},{4,0},{8,12},{12,8},{16,20},{20,16},{24,28},{28,24},{1,5},{5... | collective-permute-start | bytes 1572872 | tf_op jit(solution)/shard_map/ppermute | solution.py:26
  16.7 18.3 %collective-permute-start.3 = (bf16[256,1024]{1,0:T(8,128)(2,1)}, bf16[256,1024]{1,0:T(8,128)(2,1)S(1)}, u32[]{:S(2)}, u32[]{:S(2)}) collective-permute-start(bf16[256,1024]{1,0:T(8,128)(2,1)} %get-tuple-element.66), channel_id=1, source_target_pairs={{0,8},{4,12},{8,0},{12,4},{16,24},{20,28},{24,16},{28,20},{1,9},{5... | collective-permute-start | bytes 1572872 | tf_op jit(solution)/shard_map/ppermute | solution.py:26
  26.6 17.6 %collective-permute-start.4 = (bf16[256,1024]{1,0:T(8,128)(2,1)}, bf16[256,1024]{1,0:T(8,128)(2,1)S(1)}, u32[]{:S(2)}, u32[]{:S(2)}) collective-permute-start(bf16[256,1024]{1,0:T(8,128)(2,1)} %get-tuple-element.72), channel_id=1, source_target_pairs={{0,4},{4,0},{8,12},{12,8},{16,20},{20,16},{24,28},{28,24},{1,5},{5... | collective-permute-start | bytes 1572872 | tf_op jit(solution)/shard_map/ppermute | solution.py:26
  28.6 17.7 %collective-permute-start.5 = (bf16[256,1024]{1,0:T(8,128)(2,1)}, bf16[256,1024]{1,0:T(8,128)(2,1)S(1)}, u32[]{:S(2)}, u32[]{:S(2)}) collective-permute-start(bf16[256,1024]{1,0:T(8,128)(2,1)} %collective-permute-done), channel_id=1, source_target_pairs={{0,8},{4,12},{8,0},{12,4},{16,24},{20,28},{24,16},{28,20},{1,9},{5... | collective-permute-start | bytes 1572872 | tf_op jit(solution)/shard_map/ppermute | solution.py:26
  35.1 26.4 %collective-permute-start.8 = (bf16[256,1024]{1,0:T(8,128)(2,1)}, bf16[256,1024]{1,0:T(8,128)(2,1)S(1)}, u32[]{:S(2)}, u32[]{:S(2)}) collective-permute-start(bf16[256,1024]{1,0:T(8,128)(2,1)} %get-tuple-element.81), channel_id=1, source_target_pairs={{0,4},{4,0},{8,12},{12,8},{16,20},{20,16},{24,28},{28,24},{1,5},{5... | collective-permute-start | bytes 1572872 | tf_op jit(solution)/shard_map/ppermute | solution.py:26
  35.1 26.4 %collective-permute-start.9 = (bf16[256,1024]{1,0:T(8,128)(2,1)}, bf16[256,1024]{1,0:T(8,128)(2,1)}, u32[]{:S(2)}, u32[]{:S(2)}) collective-permute-start(bf16[256,1024]{1,0:T(8,128)(2,1)} %collective-permute-done.2), channel_id=1, source_target_pairs={{0,8},{4,12},{8,0},{12,4},{16,24},{20,28},{24,16},{28,20},{1,9},{5... | collective-permute-start | bytes 1572872 | tf_op jit(solution)/shard_map/ppermute | solution.py:26
  46.3 21.4 %collective-permute-start.6 = (bf16[256,1024]{1,0:T(8,128)(2,1)}, bf16[256,1024]{1,0:T(8,128)(2,1)}, u32[]{:S(2)}, u32[]{:S(2)}) collective-permute-start(bf16[256,1024]{1,0:T(8,128)(2,1)} %get-tuple-element.74), channel_id=1, source_target_pairs={{0,4},{4,0},{8,12},{12,8},{16,20},{20,16},{24,28},{28,24},{1,5},{5... | collective-permute-start | bytes 1572872 | tf_op jit(solution)/shard_map/ppermute | solution.py:26
  46.3 22.5 %collective-permute-start.7 = (bf16[256,1024]{1,0:T(8,128)(2,1)}, bf16[256,1024]{1,0:T(8,128)(2,1)}, u32[]{:S(2)}, u32[]{:S(2)}) collective-permute-start(bf16[256,1024]{1,0:T(8,128)(2,1)} %get-tuple-element.75), channel_id=1, source_target_pairs={{0,8},{4,12},{8,0},{12,4},{16,24},{20,28},{24,16},{28,20},{1,9},{5... | collective-permute-start | bytes 1572872 | tf_op jit(solution)/shard_map/ppermute | solution.py:26
  61.5 15.6 %collective-permute-start.15 = (bf16[256,1024]{1,0:T(8,128)(2,1)}, bf16[256,1024]{1,0:T(8,128)(2,1)S(1)}, u32[]{:S(2)}, u32[]{:S(2)}) collective-permute-start(bf16[256,1024]{1,0:T(8,128)(2,1)} %get-tuple-element.96), channel_id=1, source_target_pairs={{0,4},{4,0},{8,12},{12,8},{16,20},{20,16},{24,28},{28,24},{1,5},{5... | collective-permute-start | bytes 1572872 | tf_op jit(solution)/shard_map/ppermute | solution.py:26
  63.1 15.9 %collective-permute-start.16 = (bf16[256,1024]{1,0:T(8,128)(2,1)}, bf16[256,1024]{1,0:T(8,128)(2,1)S(1)}, u32[]{:S(2)}, u32[]{:S(2)}) collective-permute-start(bf16[256,1024]{1,0:T(8,128)(2,1)} %get-tuple-element.97), channel_id=1, source_target_pairs={{0,8},{4,12},{8,0},{12,4},{16,24},{20,28},{24,16},{28,20},{1,9},{5... | collective-permute-start | bytes 1572872 | tf_op jit(solution)/shard_map/ppermute | solution.py:26
  68.9 11.7 %collective-permute-start.12 = (f32[16,128]{1,0:T(8,128)S(1)}, f32[16,128]{1,0:T(8,128)S(1)}, u32[]{:S(2)}, u32[]{:S(2)}) collective-permute-start(f32[16,128]{1,0:T(8,128)S(1)} %gram_rows.5.refs_0_), channel_id=1, source_target_pairs={{0,12},{4,8},{8,4},{12,0},{16,28},{20,24},{24,20},{28,16},{1,13},{... | collective-permute-start | bytes 24584 | tf_op jit(solution)/shard_map/ppermute | solution.py:26
  70.4 10.7 %collective-permute-start.11 = (f32[16,128]{1,0:T(8,128)S(1)}, f32[16,128]{1,0:T(8,128)S(1)}, u32[]{:S(2)}, u32[]{:S(2)}) collective-permute-start(f32[16,128]{1,0:T(8,128)S(1)} %gram_rows.5.refs_0_), channel_id=1, source_target_pairs={{0,8},{4,12},{8,0},{12,4},{16,24},{20,28},{24,16},{28,20},{1,9},{5... | collective-permute-start | bytes 24584 | tf_op jit(solution)/shard_map/ppermute | solution.py:26
  70.4 11.4 %collective-permute-start.10 = (f32[16,128]{1,0:T(8,128)S(1)}, f32[16,128]{1,0:T(8,128)S(1)}, u32[]{:S(2)}, u32[]{:S(2)}) collective-permute-start(f32[16,128]{1,0:T(8,128)S(1)} %gram_rows.5.refs_0_), channel_id=1, source_target_pairs={{0,4},{4,0},{8,12},{12,8},{16,20},{20,16},{24,28},{28,24},{1,5},{5... | collective-permute-start | bytes 24584 | tf_op jit(solution)/shard_map/ppermute | solution.py:26
  77.1 15.1 %collective-permute-start.19 = (bf16[256,1024]{1,0:T(8,128)(2,1)}, bf16[256,1024]{1,0:T(8,128)(2,1)S(1)}, u32[]{:S(2)}, u32[]{:S(2)}) collective-permute-start(bf16[256,1024]{1,0:T(8,128)(2,1)} %get-tuple-element.102), channel_id=1, source_target_pairs={{0,4},{4,0},{8,12},{12,8},{16,20},{20,16},{24,28},{28,24},{1,5},{5... | collective-permute-start | bytes 1572872 | tf_op jit(solution)/shard_map/ppermute | solution.py:26
  79.0 15.1 %collective-permute-start.20 = (bf16[256,1024]{1,0:T(8,128)(2,1)}, bf16[256,1024]{1,0:T(8,128)(2,1)S(1)}, u32[]{:S(2)}, u32[]{:S(2)}) collective-permute-start(bf16[256,1024]{1,0:T(8,128)(2,1)} %collective-permute-done.6), channel_id=1, source_target_pairs={{0,8},{4,12},{8,0},{12,4},{16,24},{20,28},{24,16},{28,20},{1,9},{5... | collective-permute-start | bytes 1572872 | tf_op jit(solution)/shard_map/ppermute | solution.py:26
  80.6 21.0 %collective-permute-start.17 = (bf16[256,1024]{1,0:T(8,128)(2,1)}, bf16[256,1024]{1,0:T(8,128)(2,1)S(1)}, u32[]{:S(2)}, u32[]{:S(2)}) collective-permute-start(bf16[256,1024]{1,0:T(8,128)(2,1)} %get-tuple-element.98), channel_id=1, source_target_pairs={{0,4},{4,0},{8,12},{12,8},{16,20},{20,16},{24,28},{28,24},{1,5},{5... | collective-permute-start | bytes 1572872 | tf_op jit(solution)/shard_map/ppermute | solution.py:26
  81.1 21.7 %collective-permute-start.18 = (bf16[256,1024]{1,0:T(8,128)(2,1)S(1)}, bf16[256,1024]{1,0:T(8,128)(2,1)S(1)}, u32[]{:S(2)}, u32[]{:S(2)}) collective-permute-start(bf16[256,1024]{1,0:T(8,128)(2,1)S(1)} %collective-permute-done.15), channel_id=1, source_target_pairs={{0,8},{4,12},{8,0},{12,4},{16,24},{20,28},{24,16},{28,20},{1,9},{5... | collective-permute-start | bytes 1572872 | tf_op jit(solution)/shard_map/ppermute | solution.py:26
  89.5 25.3 %collective-permute-start.23 = (bf16[256,1024]{1,0:T(8,128)(2,1)S(1)}, bf16[256,1024]{1,0:T(8,128)(2,1)S(1)}, u32[]{:S(2)}, u32[]{:S(2)}) collective-permute-start(bf16[256,1024]{1,0:T(8,128)(2,1)S(1)} %group_combine.4), channel_id=1, source_target_pairs={{8,16},{12,20},{16,8},{20,12},{9,17},{13,21},{17,9},{21,13},{10,18... | collective-permute-start | bytes 1572872 | tf_op jit(solution)/shard_map/ppermute | solution.py:358
  108.0 15.3 %collective-permute-start.27 = (bf16[256,1024]{1,0:T(8,128)(2,1)S(1)}, bf16[256,1024]{1,0:T(8,128)(2,1)S(1)}, u32[]{:S(2)}, u32[]{:S(2)}) collective-permute-start(bf16[256,1024]{1,0:T(8,128)(2,1)S(1)} %group_combine.4), channel_id=1, source_target_pairs={{0,24},{4,28},{24,0},{28,4},{1,25},{5,29},{25,1},{29,5},{2,26},{6,... | collective-permute-start | bytes 1572872 | tf_op jit(solution)/shard_map/ppermute | solution.py:358
  123.3 16.4 %collective-permute-start.29 = (bf16[256,1024]{1,0:T(8,128)(2,1)S(1)}, bf16[256,1024]{1,0:T(8,128)(2,1)S(1)}, u32[]{:S(2)}, u32[]{:S(2)}) collective-permute-start(bf16[256,1024]{1,0:T(8,128)(2,1)S(1)} %group_combine.7), channel_id=1, source_target_pairs={{0,24},{4,28},{24,0},{28,4},{1,25},{5,29},{25,1},{29,5},{2,26},{6,... | collective-permute-start | bytes 1572872 | tf_op jit(solution)/shard_map/ppermute | solution.py:358
  127.4 12.2 %collective-permute-start.28 = (bf16[256,1024]{1,0:T(8,128)(2,1)S(1)}, bf16[256,1024]{1,0:T(8,128)(2,1)S(1)}, u32[]{:S(2)}, u32[]{:S(2)}) collective-permute-start(bf16[256,1024]{1,0:T(8,128)(2,1)S(1)} %group_combine.7), channel_id=1, source_target_pairs={{8,16},{12,20},{16,8},{20,12},{9,17},{13,21},{17,9},{21,13},{10,18... | collective-permute-start | bytes 1572872 | tf_op jit(solution)/shard_map/ppermute | solution.py:358
  147.2 9.8 %collective-permute-start.35 = (f32[8,128]{1,0:T(8,128)S(1)}, f32[8,128]{1,0:T(8,128)S(1)}, u32[]{:S(2)}, u32[]{:S(2)}) collective-permute-start(f32[8,128]{1,0:T(8,128)S(1)} %total.6.refs_0_), channel_id=1, source_target_pairs={{0,16},{4,20},{8,24},{12,28},{16,0},{20,4},{24,8},{28,12},{1,17},{... | collective-permute-start | bytes 12296 | tf_op jit(solution)/shard_map/ppermute | solution.py:26
  (17 other events, 145.0 us)

commit v6 on v5

--- a/solution.py
+++ b/solution.py
@@ -6,7 +6,7 @@
 from jax.sharding import PartitionSpec as P
 
 epsilon = 1e-06
-LARGE_LIMIT = 60 * 1024 * 1024
+LARGE_LIMIT = 48 * 1024 * 1024
 SMALL_LIMIT = 16 * 1024 * 1024
 LANES = 128
 STRIDE = 16
@@ -16,7 +16,7 @@
 BLOCK_COST = 1_600_000_000
 MESH_HOPS = True
 KEPT_COST = 5_000_000_000
-BATCHES = ((1, 2), (1,))
+BATCHES = ((1, 2, 3), (1,))
 FIRST_COST = 3_200_000_000
 GRAM_COST = 3_200_000_000
 CROSS_COST = 6_000_000_000

time: 161 us -> 160 us (level)
  Pallas kernels: 56.9 us -> 49.8 us
  waiting for transfers between devices: 50.5 us -> 55.7 us
    ppermute x31, waiting for transfers between devices: 38.1 us -> 44.5 us  [exchange(): lax.ppermute(value, axis, [(i, i ^ mask) for i in range(lax.axis_size(axi...]
    pallas_call x11, Pallas kernels: 16.3 us -> 12.3 us  [call(): pl.pallas_call(kernel, in_specs=[pl.BlockSpec(memory_space=pltpu.SMEM)] +...]
    pallas_call x5 -> x6, Pallas kernels: 40.5 us -> 37.4 us  [block_pairs(): pl.pallas_call(kernel, grid_spec=pltpu.PrefetchScalarGridSpec(num_scalar_...]
  transfers between devices with their start and end apart: 37 -> 37, of which waited for: 23 -> 26; matrix products, arithmetic and copies ran while one was open for 0% -> 0% of each run, Pallas kernels for 30% -> 26%
where the time goes in v6:
time: 160 us
  waiting for transfers between devices  55.7 us (35%)
  starting transfers between devices  54.2 us (34%)
  Pallas kernels  49.8 us (31%)
    ppermute x31, waiting for transfers between devices, exchange(): lax.ppermute(value, axis, [(i, i ^ mask) for i in range(lax.axis_size(axi...  44.5 us
    ppermute x31, starting transfers between devices, exchange(): lax.ppermute(value, axis, [(i, i ^ mask) for i in range(lax.axis_size(axi...  40.1 us
    pallas_call x6, Pallas kernels, block_pairs(): pl.pallas_call(kernel, grid_spec=pltpu.PrefetchScalarGridSpec(num_scalar_...  37.4 us
    pallas_call x11, Pallas kernels, call(): pl.pallas_call(kernel, in_specs=[pl.BlockSpec(memory_space=pltpu.SMEM)] +...  12.3 us
    ppermute x4, starting transfers between devices, swap(): return lax.ppermute(value, 'rep', pairs)  12.1 us
    ppermute x4, waiting for transfers between devices, swap(): return lax.ppermute(value, 'rep', pairs)  9.1 us
  transfers between devices with their start and end apart: 37, of which 26 were waited for; matrix products, arithmetic and copies ran while one was open for 0% of the time, Pallas kernels for 26%

profile of v6, /device:TPU:0, one launch (start us, length us, event | category | flops | bytes accessed | tf_op | source)
XLA Modules:
  0.0 159.9 jit_solution(4415619704346842819)
XLA Ops:
  0.0 5.1 %block_pairs.7 = (bf16[256,1024]{1,0:T(8,128)(2,1)S(1)}, bf16[256,1024]{1,0:T(8,128)(2,1)S(1)}) custom-call(s32[1]{0:T(128)} %bitcast.rank_ref, bf16[2,2048,2048]{2,1,0:T(8,128)(2,1)} %a_ref.9, bf16[2,2048,1024]{2,1,0:T(8,128)(2,1)} %b_ref.11), custom_call_target="tpu_custom_call" | custom-call | flops 1600000000 | bytes 1024 | tf_op jit(solution)/shard_map/block_pairs/pallas_call | solution.py:89
  5.1 3.0 %collective-permute-start = (bf16[256,1024]{1,0:T(8,128)(2,1)S(1)}, bf16[256,1024]{1,0:T(8,128)(2,1)S(1)}, u32[]{:S(2)}, u32[]{:S(2)}) collective-permute-start(bf16[256,1024]{1,0:T(8,128)(2,1)S(1)} %get-tuple-element.60), channel_id=1, source_target_pairs={{0,4},{4,0},{8,12},{12,8},{16,20},{20,16},{24,28},{28,24},{1,5},{5... | collective-permute-start | bytes 1572872 | tf_op jit(solution)/shard_map/ppermute | solution.py:26
  9.7 5.1 %block_pairs.9 = (bf16[256,1024]{1,0:T(8,128)(2,1)S(1)}, bf16[256,1024]{1,0:T(8,128)(2,1)S(1)}) custom-call(s32[1]{0:T(128)} %bitcast.rank_ref, bf16[2,2048,2048]{2,1,0:T(8,128)(2,1)} %a_ref.9, bf16[2,2048,1024]{2,1,0:T(8,128)(2,1)} %b_ref.11), custom_call_target="tpu_custom_call" | custom-call | flops 1600000000 | bytes 1024 | tf_op jit(solution)/shard_map/block_pairs/pallas_call | solution.py:89
  15.4 5.1 %block_pairs.6 = (bf16[256,1024]{1,0:T(8,128)(2,1)S(1)}, bf16[256,1024]{1,0:T(8,128)(2,1)S(1)}) custom-call(s32[1]{0:T(128)} %bitcast.rank_ref, bf16[2,2048,2048]{2,1,0:T(8,128)(2,1)} %a_ref.9, bf16[2,2048,1024]{2,1,0:T(8,128)(2,1)} %b_ref.11), custom_call_target="tpu_custom_call" | custom-call | flops 1600000000 | bytes 1024 | tf_op jit(solution)/shard_map/block_pairs/pallas_call | solution.py:89
  20.8 2.1 %collective-permute-done.1.refs_2_ = bf16[256,1024]{1,0:T(8,128)(2,1)S(1)} collective-permute-done((bf16[256,1024]{1,0:T(8,128)(2,1)S(1)}, bf16[256,1024]{1,0:T(8,128)(2,1)S(1)}, u32[]{:S(2)}, u32[]{:S(2)}) %collective-permute-start.1) | collective-permute-done | bytes 524320 | tf_op jit(solution)/shard_map/ppermute | solution.py:26
  23.0 2.1 %collective-permute-start.5 = (bf16[256,1024]{1,0:T(8,128)(2,1)S(1)}, bf16[256,1024]{1,0:T(8,128)(2,1)S(1)}, u32[]{:S(2)}, u32[]{:S(2)}) collective-permute-start(bf16[256,1024]{1,0:T(8,128)(2,1)S(1)} %collective-permute-done), channel_id=1, source_target_pairs={{0,8},{4,12},{8,0},{12,4},{16,24},{20,28},{24,16},{28,20},{1,9},{5... | collective-permute-start | bytes 1572872 | tf_op jit(solution)/shard_map/ppermute | solution.py:26
  25.0 5.1 %block_pairs.8 = (bf16[256,1024]{1,0:T(8,128)(2,1)S(1)}, bf16[256,1024]{1,0:T(8,128)(2,1)S(1)}) custom-call(s32[1]{0:T(128)} %bitcast.rank_ref, bf16[2,2048,2048]{2,1,0:T(8,128)(2,1)} %a_ref.9, bf16[2,2048,1024]{2,1,0:T(8,128)(2,1)} %b_ref.11), custom_call_target="tpu_custom_call" | custom-call | flops 1600000000 | bytes 1024 | tf_op jit(solution)/shard_map/block_pairs/pallas_call | solution.py:89
  32.1 2.1 %collective-permute-done.3.refs_2_ = bf16[256,1024]{1,0:T(8,128)(2,1)S(1)} collective-permute-done((bf16[256,1024]{1,0:T(8,128)(2,1)S(1)}, bf16[256,1024]{1,0:T(8,128)(2,1)S(1)}, u32[]{:S(2)}, u32[]{:S(2)}) %collective-permute-start.3) | collective-permute-done | bytes 524320 | tf_op jit(solution)/shard_map/ppermute | solution.py:26
  34.2 2.1 %collective-permute-start.9 = (bf16[256,1024]{1,0:T(8,128)(2,1)S(1)}, bf16[256,1024]{1,0:T(8,128)(2,1)S(1)}, u32[]{:S(2)}, u32[]{:S(2)}) collective-permute-start(bf16[256,1024]{1,0:T(8,128)(2,1)S(1)} %collective-permute-done.2), channel_id=1, source_target_pairs={{0,8},{4,12},{8,0},{12,4},{16,24},{20,28},{24,16},{28,20},{1,9},{5... | collective-permute-start | bytes 1572872 | tf_op jit(solution)/shard_map/ppermute | solution.py:26
  36.3 5.1 %block_pairs.11 = (bf16[256,1024]{1,0:T(8,128)(2,1)S(1)}, bf16[256,1024]{1,0:T(8,128)(2,1)S(1)}) custom-call(s32[1]{0:T(128)} %bitcast.rank_ref, bf16[2,2048,2048]{2,1,0:T(8,128)(2,1)} %a_ref.9, bf16[2,2048,1024]{2,1,0:T(8,128)(2,1)} %b_ref.11), custom_call_target="tpu_custom_call" | custom-call | flops 1600000000 | bytes 1024 | tf_op jit(solution)/shard_map/block_pairs/pallas_call | solution.py:89
  43.3 2.1 %collective-permute-done.5.refs_3_ = bf16[256,1024]{1,0:T(8,128)(2,1)S(1)} collective-permute-done((bf16[256,1024]{1,0:T(8,128)(2,1)S(1)}, bf16[256,1024]{1,0:T(8,128)(2,1)S(1)}, u32[]{:S(2)}, u32[]{:S(2)}) %collective-permute-start.5) | collective-permute-done | bytes 524320 | tf_op jit(solution)/shard_map/ppermute | solution.py:26
  45.5 2.1 %collective-permute-start.7 = (bf16[256,1024]{1,0:T(8,128)(2,1)S(1)}, bf16[256,1024]{1,0:T(8,128)(2,1)S(1)}, u32[]{:S(2)}, u32[]{:S(2)}) collective-permute-start(bf16[256,1024]{1,0:T(8,128)(2,1)S(1)} %get-tuple-element.75), channel_id=1, source_target_pairs={{0,8},{4,12},{8,0},{12,4},{16,24},{20,28},{24,16},{28,20},{1,9},{5... | collective-permute-start | bytes 1572872 | tf_op jit(solution)/shard_map/ppermute | solution.py:26
  47.5 12.1 %block_pairs.10 = (bf16[256,1024]{1,0:T(8,128)(2,1)S(1)}, bf16[256,1024]{1,0:T(8,128)(2,1)S(1)}, bf16[256,1024]{1,0:T(8,128)(2,1)S(1)}, bf16[256,1024]{1,0:T(8,1...) custom-call(s32[1]{0:T(128)} %bitcast.rank_ref, bf16[2,2048,2048]{2,1,0:T(8,128)(2,1)} %a_ref.9, ...), custom_call_target="tpu_custom_call" | custom-call | flops 1600000000 | bytes 1024 | tf_op jit(solution)/shard_map/block_pairs/pallas_call | solution.py:89
  65.8 2.1 %collective-permute-done.7.refs_2_ = bf16[256,1024]{1,0:T(8,128)(2,1)S(1)} collective-permute-done((bf16[256,1024]{1,0:T(8,128)(2,1)S(1)}, bf16[256,1024]{1,0:T(8,128)(2,1)S(1)}, u32[]{:S(2)}, u32[]{:S(2)}) %collective-permute-start.7) | collective-permute-done | bytes 524320 | tf_op jit(solution)/shard_map/ppermute | solution.py:26
  71.4 4.9 %collective-permute-done.15 = bf16[256,1024]{1,0:T(8,128)(2,1)S(1)} collective-permute-done((bf16[256,1024]{1,0:T(8,128)(2,1)S(1)}, bf16[256,1024]{1,0:T(8,128)(2,1)S(1)}, u32[]{:S(2)}, u32[]{:S(2)}) %collective-permute-start.15) | collective-permute-done | bytes 524320 | tf_op jit(solution)/shard_map/ppermute | solution.py:26
  83.7 2.1 %collective-permute-done.14 = f32[16,128]{1,0:T(8,128)S(1)} collective-permute-done((f32[16,128]{1,0:T(8,128)S(1)}, f32[16,128]{1,0:T(8,128)S(1)}, u32[]{:S(2)}, u32[]{:S(2)}) %collective-permute-start.14) | collective-permute-done | bytes 8224 | tf_op jit(solution)/shard_map/ppermute | solution.py:26
  88.3 2.9 %collective-permute-done.19.refs_1_ = bf16[256,1024]{1,0:T(8,128)(2,1)S(1)} collective-permute-done((bf16[256,1024]{1,0:T(8,128)(2,1)S(1)}, bf16[256,1024]{1,0:T(8,128)(2,1)S(1)}, u32[]{:S(2)}, u32[]{:S(2)}) %collective-permute-start.19) | collective-permute-done | bytes 524320 | tf_op jit(solution)/shard_map/ppermute | solution.py:26
  94.5 6.0 %collective-permute-done.17.refs_1_ = bf16[256,1024]{1,0:T(8,128)(2,1)S(1)} collective-permute-done((bf16[256,1024]{1,0:T(8,128)(2,1)S(1)}, bf16[256,1024]{1,0:T(8,128)(2,1)S(1)}, u32[]{:S(2)}, u32[]{:S(2)}) %collective-permute-start.17) | collective-permute-done | bytes 524320 | tf_op jit(solution)/shard_map/ppermute | solution.py:26
  104.9 2.1 %collective-permute-done.21 = f32[16,128]{1,0:T(8,128)S(1)} collective-permute-done((f32[16,128]{1,0:T(8,128)S(1)}, f32[16,128]{1,0:T(8,128)S(1)}, u32[]{:S(2)}, u32[]{:S(2)}) %collective-permute-start.21) | collective-permute-done | bytes 8224 | tf_op jit(solution)/shard_map/ppermute | solution.py:26
  107.0 5.5 %collective-permute-start.27 = (bf16[256,1024]{1,0:T(8,128)(2,1)S(1)}, bf16[256,1024]{1,0:T(8,128)(2,1)S(1)}, u32[]{:S(2)}, u32[]{:S(2)}) collective-permute-start(bf16[256,1024]{1,0:T(8,128)(2,1)S(1)} %group_combine.4), channel_id=1, source_target_pairs={{0,24},{4,28},{24,0},{28,4},{1,25},{5,29},{25,1},{29,5},{2,26},{6,... | collective-permute-start | bytes 1572872 | tf_op jit(solution)/shard_map/ppermute | solution.py:358
  121.2 5.3 %collective-permute-start.29 = (bf16[256,1024]{1,0:T(8,128)(2,1)S(1)}, bf16[256,1024]{1,0:T(8,128)(2,1)S(1)}, u32[]{:S(2)}, u32[]{:S(2)}) collective-permute-start(bf16[256,1024]{1,0:T(8,128)(2,1)S(1)} %group_combine.7), channel_id=1, source_target_pairs={{0,24},{4,28},{24,0},{28,4},{1,25},{5,29},{25,1},{29,5},{2,26},{6,... | collective-permute-start | bytes 1572872 | tf_op jit(solution)/shard_map/ppermute | solution.py:358
  128.5 9.1 %collective-permute-done.29.refs_2_.refs_5_ = bf16[256,1024]{1,0:T(8,128)(2,1)S(1)} collective-permute-done((bf16[256,1024]{1,0:T(8,128)(2,1)S(1)}, bf16[256,1024]{1,0:T(8,128)(2,1)S(1)}, u32[]{:S(2)}, u32[]{:S(2)}) %collective-permute-start.29) | collective-permute-done | bytes 524320 | tf_op jit(solution)/shard_map/ppermute | solution.py:358
  145.9 8.5 %collective-permute-start.35 = (f32[8,128]{1,0:T(8,128)S(1)}, f32[8,128]{1,0:T(8,128)S(1)}, u32[]{:S(2)}, u32[]{:S(2)}) collective-permute-start(f32[8,128]{1,0:T(8,128)S(1)} %total.6.refs_0_), channel_id=1, source_target_pairs={{0,16},{4,20},{8,24},{12,28},{16,0},{20,4},{24,8},{28,12},{1,17},{... | collective-permute-start | bytes 12296 | tf_op jit(solution)/shard_map/ppermute | solution.py:26
  156.0 2.0 %collective-permute-done.34.refs_1_ = f32[8,128]{1,0:T(8,128)S(1)} collective-permute-done((f32[8,128]{1,0:T(8,128)S(1)}, f32[8,128]{1,0:T(8,128)S(1)}, u32[]{:S(2)}, u32[]{:S(2)}) %collective-permute-start.34) | collective-permute-done | bytes 4128 | tf_op jit(solution)/shard_map/ppermute | solution.py:26
  (76 shorter events, 56.2 us)
Async XLA Ops:
  5.1 15.8 %collective-permute-start = (bf16[256,1024]{1,0:T(8,128)(2,1)S(1)}, bf16[256,1024]{1,0:T(8,128)(2,1)S(1)}, u32[]{:S(2)}, u32[]{:S(2)}) collective-permute-start(bf16[256,1024]{1,0:T(8,128)(2,1)S(1)} %get-tuple-element.60), channel_id=1, source_target_pairs={{0,4},{4,0},{8,12},{12,8},{16,20},{20,16},{24,28},{28,24},{1,5},{5... | collective-permute-start | bytes 1572872 | tf_op jit(solution)/shard_map/ppermute | solution.py:26
  8.1 14.8 %collective-permute-start.1 = (bf16[256,1024]{1,0:T(8,128)(2,1)S(1)}, bf16[256,1024]{1,0:T(8,128)(2,1)S(1)}, u32[]{:S(2)}, u32[]{:S(2)}) collective-permute-start(bf16[256,1024]{1,0:T(8,128)(2,1)S(1)} %get-tuple-element.61), channel_id=1, source_target_pairs={{0,8},{4,12},{8,0},{12,4},{16,24},{20,28},{24,16},{28,20},{1,9},{5... | collective-permute-start | bytes 1572872 | tf_op jit(solution)/shard_map/ppermute | solution.py:26
  14.7 17.3 %collective-permute-start.2 = (bf16[256,1024]{1,0:T(8,128)(2,1)S(1)}, bf16[256,1024]{1,0:T(8,128)(2,1)S(1)}, u32[]{:S(2)}, u32[]{:S(2)}) collective-permute-start(bf16[256,1024]{1,0:T(8,128)(2,1)S(1)} %get-tuple-element.65), channel_id=1, source_target_pairs={{0,4},{4,0},{8,12},{12,8},{16,20},{20,16},{24,28},{28,24},{1,5},{5... | collective-permute-start | bytes 1572872 | tf_op jit(solution)/shard_map/ppermute | solution.py:26
  15.3 18.8 %collective-permute-start.3 = (bf16[256,1024]{1,0:T(8,128)(2,1)S(1)}, bf16[256,1024]{1,0:T(8,128)(2,1)S(1)}, u32[]{:S(2)}, u32[]{:S(2)}) collective-permute-start(bf16[256,1024]{1,0:T(8,128)(2,1)S(1)} %get-tuple-element.66), channel_id=1, source_target_pairs={{0,8},{4,12},{8,0},{12,4},{16,24},{20,28},{24,16},{28,20},{1,9},{5... | collective-permute-start | bytes 1572872 | tf_op jit(solution)/shard_map/ppermute | solution.py:26
  22.9 20.4 %collective-permute-start.4 = (bf16[256,1024]{1,0:T(8,128)(2,1)S(1)}, bf16[256,1024]{1,0:T(8,128)(2,1)S(1)}, u32[]{:S(2)}, u32[]{:S(2)}) collective-permute-start(bf16[256,1024]{1,0:T(8,128)(2,1)S(1)} %get-tuple-element.72), channel_id=1, source_target_pairs={{0,4},{4,0},{8,12},{12,8},{16,20},{20,16},{24,28},{28,24},{1,5},{5... | collective-permute-start | bytes 1572872 | tf_op jit(solution)/shard_map/ppermute | solution.py:26
  23.0 22.4 %collective-permute-start.5 = (bf16[256,1024]{1,0:T(8,128)(2,1)S(1)}, bf16[256,1024]{1,0:T(8,128)(2,1)S(1)}, u32[]{:S(2)}, u32[]{:S(2)}) collective-permute-start(bf16[256,1024]{1,0:T(8,128)(2,1)S(1)} %collective-permute-done), channel_id=1, source_target_pairs={{0,8},{4,12},{8,0},{12,4},{16,24},{20,28},{24,16},{28,20},{1,9},{5... | collective-permute-start | bytes 1572872 | tf_op jit(solution)/shard_map/ppermute | solution.py:26
  34.2 25.4 %collective-permute-start.8 = (bf16[256,1024]{1,0:T(8,128)(2,1)S(1)}, bf16[256,1024]{1,0:T(8,128)(2,1)S(1)}, u32[]{:S(2)}, u32[]{:S(2)}) collective-permute-start(bf16[256,1024]{1,0:T(8,128)(2,1)S(1)} %get-tuple-element.81), channel_id=1, source_target_pairs={{0,4},{4,0},{8,12},{12,8},{16,20},{20,16},{24,28},{28,24},{1,5},{5... | collective-permute-start | bytes 1572872 | tf_op jit(solution)/shard_map/ppermute | solution.py:26
  34.2 25.4 %collective-permute-start.9 = (bf16[256,1024]{1,0:T(8,128)(2,1)S(1)}, bf16[256,1024]{1,0:T(8,128)(2,1)S(1)}, u32[]{:S(2)}, u32[]{:S(2)}) collective-permute-start(bf16[256,1024]{1,0:T(8,128)(2,1)S(1)} %collective-permute-done.2), channel_id=1, source_target_pairs={{0,8},{4,12},{8,0},{12,4},{16,24},{20,28},{24,16},{28,20},{1,9},{5... | collective-permute-start | bytes 1572872 | tf_op jit(solution)/shard_map/ppermute | solution.py:26
  45.4 20.4 %collective-permute-start.6 = (bf16[256,1024]{1,0:T(8,128)(2,1)S(1)}, bf16[256,1024]{1,0:T(8,128)(2,1)S(1)}, u32[]{:S(2)}, u32[]{:S(2)}) collective-permute-start(bf16[256,1024]{1,0:T(8,128)(2,1)S(1)} %get-tuple-element.74), channel_id=1, source_target_pairs={{0,4},{4,0},{8,12},{12,8},{16,20},{20,16},{24,28},{28,24},{1,5},{5... | collective-permute-start | bytes 1572872 | tf_op jit(solution)/shard_map/ppermute | solution.py:26
  45.5 22.4 %collective-permute-start.7 = (bf16[256,1024]{1,0:T(8,128)(2,1)S(1)}, bf16[256,1024]{1,0:T(8,128)(2,1)S(1)}, u32[]{:S(2)}, u32[]{:S(2)}) collective-permute-start(bf16[256,1024]{1,0:T(8,128)(2,1)S(1)} %get-tuple-element.75), channel_id=1, source_target_pairs={{0,8},{4,12},{8,0},{12,4},{16,24},{20,28},{24,16},{28,20},{1,9},{5... | collective-permute-start | bytes 1572872 | tf_op jit(solution)/shard_map/ppermute | solution.py:26
  59.6 16.7 %collective-permute-start.15 = (bf16[256,1024]{1,0:T(8,128)(2,1)S(1)}, bf16[256,1024]{1,0:T(8,128)(2,1)S(1)}, u32[]{:S(2)}, u32[]{:S(2)}) collective-permute-start(bf16[256,1024]{1,0:T(8,128)(2,1)S(1)} %get-tuple-element.96), channel_id=1, source_target_pairs={{0,4},{4,0},{8,12},{12,8},{16,20},{20,16},{24,28},{28,24},{1,5},{5... | collective-permute-start | bytes 1572872 | tf_op jit(solution)/shard_map/ppermute | solution.py:26
  61.2 17.0 %collective-permute-start.16 = (bf16[256,1024]{1,0:T(8,128)(2,1)S(1)}, bf16[256,1024]{1,0:T(8,128)(2,1)S(1)}, u32[]{:S(2)}, u32[]{:S(2)}) collective-permute-start(bf16[256,1024]{1,0:T(8,128)(2,1)S(1)} %get-tuple-element.97), channel_id=1, source_target_pairs={{0,8},{4,12},{8,0},{12,4},{16,24},{20,28},{24,16},{28,20},{1,9},{5... | collective-permute-start | bytes 1572872 | tf_op jit(solution)/shard_map/ppermute | solution.py:26
  67.9 11.8 %collective-permute-start.12 = (f32[16,128]{1,0:T(8,128)S(1)}, f32[16,128]{1,0:T(8,128)S(1)}, u32[]{:S(2)}, u32[]{:S(2)}) collective-permute-start(f32[16,128]{1,0:T(8,128)S(1)} %gram_rows.5.refs_0_), channel_id=1, source_target_pairs={{0,12},{4,8},{8,4},{12,0},{16,28},{20,24},{24,20},{28,16},{1,13},{... | collective-permute-start | bytes 24584 | tf_op jit(solution)/shard_map/ppermute | solution.py:26
  69.4 10.8 %collective-permute-start.11 = (f32[16,128]{1,0:T(8,128)S(1)}, f32[16,128]{1,0:T(8,128)S(1)}, u32[]{:S(2)}, u32[]{:S(2)}) collective-permute-start(f32[16,128]{1,0:T(8,128)S(1)} %gram_rows.5.refs_0_), channel_id=1, source_target_pairs={{0,8},{4,12},{8,0},{12,4},{16,24},{20,28},{24,16},{28,20},{1,9},{5... | collective-permute-start | bytes 24584 | tf_op jit(solution)/shard_map/ppermute | solution.py:26
  69.5 11.5 %collective-permute-start.10 = (f32[16,128]{1,0:T(8,128)S(1)}, f32[16,128]{1,0:T(8,128)S(1)}, u32[]{:S(2)}, u32[]{:S(2)}) collective-permute-start(f32[16,128]{1,0:T(8,128)S(1)} %gram_rows.5.refs_0_), channel_id=1, source_target_pairs={{0,4},{4,0},{8,12},{12,8},{16,20},{20,16},{24,28},{28,24},{1,5},{5... | collective-permute-start | bytes 24584 | tf_op jit(solution)/shard_map/ppermute | solution.py:26
  76.3 14.9 %collective-permute-start.19 = (bf16[256,1024]{1,0:T(8,128)(2,1)S(1)}, bf16[256,1024]{1,0:T(8,128)(2,1)S(1)}, u32[]{:S(2)}, u32[]{:S(2)}) collective-permute-start(bf16[256,1024]{1,0:T(8,128)(2,1)S(1)} %get-tuple-element.102), channel_id=1, source_target_pairs={{0,4},{4,0},{8,12},{12,8},{16,20},{20,16},{24,28},{28,24},{1,5},{5... | collective-permute-start | bytes 1572872 | tf_op jit(solution)/shard_map/ppermute | solution.py:26
  78.1 14.9 %collective-permute-start.20 = (bf16[256,1024]{1,0:T(8,128)(2,1)S(1)}, bf16[256,1024]{1,0:T(8,128)(2,1)S(1)}, u32[]{:S(2)}, u32[]{:S(2)}) collective-permute-start(bf16[256,1024]{1,0:T(8,128)(2,1)S(1)} %collective-permute-done.6), channel_id=1, source_target_pairs={{0,8},{4,12},{8,0},{12,4},{16,24},{20,28},{24,16},{28,20},{1,9},{5... | collective-permute-start | bytes 1572872 | tf_op jit(solution)/shard_map/ppermute | solution.py:26
  79.7 20.9 %collective-permute-start.17 = (bf16[256,1024]{1,0:T(8,128)(2,1)S(1)}, bf16[256,1024]{1,0:T(8,128)(2,1)S(1)}, u32[]{:S(2)}, u32[]{:S(2)}) collective-permute-start(bf16[256,1024]{1,0:T(8,128)(2,1)S(1)} %get-tuple-element.98), channel_id=1, source_target_pairs={{0,4},{4,0},{8,12},{12,8},{16,20},{20,16},{24,28},{28,24},{1,5},{5... | collective-permute-start | bytes 1572872 | tf_op jit(solution)/shard_map/ppermute | solution.py:26
  80.2 21.5 %collective-permute-start.18 = (bf16[256,1024]{1,0:T(8,128)(2,1)S(1)}, bf16[256,1024]{1,0:T(8,128)(2,1)S(1)}, u32[]{:S(2)}, u32[]{:S(2)}) collective-permute-start(bf16[256,1024]{1,0:T(8,128)(2,1)S(1)} %collective-permute-done.15), channel_id=1, source_target_pairs={{0,8},{4,12},{8,0},{12,4},{16,24},{20,28},{24,16},{28,20},{1,9},{5... | collective-permute-start | bytes 1572872 | tf_op jit(solution)/shard_map/ppermute | solution.py:26
  87.6 26.1 %collective-permute-start.23 = (bf16[256,1024]{1,0:T(8,128)(2,1)S(1)}, bf16[256,1024]{1,0:T(8,128)(2,1)S(1)}, u32[]{:S(2)}, u32[]{:S(2)}) collective-permute-start(bf16[256,1024]{1,0:T(8,128)(2,1)S(1)} %group_combine.4), channel_id=1, source_target_pairs={{8,16},{12,20},{16,8},{20,12},{9,17},{13,21},{17,9},{21,13},{10,18... | collective-permute-start | bytes 1572872 | tf_op jit(solution)/shard_map/ppermute | solution.py:358
  107.0 14.2 %collective-permute-start.27 = (bf16[256,1024]{1,0:T(8,128)(2,1)S(1)}, bf16[256,1024]{1,0:T(8,128)(2,1)S(1)}, u32[]{:S(2)}, u32[]{:S(2)}) collective-permute-start(bf16[256,1024]{1,0:T(8,128)(2,1)S(1)} %group_combine.4), channel_id=1, source_target_pairs={{0,24},{4,28},{24,0},{28,4},{1,25},{5,29},{25,1},{29,5},{2,26},{6,... | collective-permute-start | bytes 1572872 | tf_op jit(solution)/shard_map/ppermute | solution.py:358
  121.2 16.4 %collective-permute-start.29 = (bf16[256,1024]{1,0:T(8,128)(2,1)S(1)}, bf16[256,1024]{1,0:T(8,128)(2,1)S(1)}, u32[]{:S(2)}, u32[]{:S(2)}) collective-permute-start(bf16[256,1024]{1,0:T(8,128)(2,1)S(1)} %group_combine.7), channel_id=1, source_target_pairs={{0,24},{4,28},{24,0},{28,4},{1,25},{5,29},{25,1},{29,5},{2,26},{6,... | collective-permute-start | bytes 1572872 | tf_op jit(solution)/shard_map/ppermute | solution.py:358
  126.5 11.1 %collective-permute-start.28 = (bf16[256,1024]{1,0:T(8,128)(2,1)S(1)}, bf16[256,1024]{1,0:T(8,128)(2,1)S(1)}, u32[]{:S(2)}, u32[]{:S(2)}) collective-permute-start(bf16[256,1024]{1,0:T(8,128)(2,1)S(1)} %group_combine.7), channel_id=1, source_target_pairs={{8,16},{12,20},{16,8},{20,12},{9,17},{13,21},{17,9},{21,13},{10,18... | collective-permute-start | bytes 1572872 | tf_op jit(solution)/shard_map/ppermute | solution.py:358
  145.9 10.1 %collective-permute-start.35 = (f32[8,128]{1,0:T(8,128)S(1)}, f32[8,128]{1,0:T(8,128)S(1)}, u32[]{:S(2)}, u32[]{:S(2)}) collective-permute-start(f32[8,128]{1,0:T(8,128)S(1)} %total.6.refs_0_), channel_id=1, source_target_pairs={{0,16},{4,20},{8,24},{12,28},{16,0},{20,4},{24,8},{28,12},{1,17},{... | collective-permute-start | bytes 12296 | tf_op jit(solution)/shard_map/ppermute | solution.py:26
  (13 other events, 48.7 us)

commit v7 on v6

--- a/solution.py
+++ b/solution.py
@@ -15,6 +15,8 @@
 COST = 1024
 BLOCK_COST = 1_600_000_000
 MESH_HOPS = True
+COPIED = True
+CHOSEN = True
 KEPT_COST = 5_000_000_000
 BATCHES = ((1, 2, 3), (1,))
 FIRST_COST = 3_200_000_000
@@ -118,14 +120,18 @@
     return lax.fori_loop(0, rows // STRIDE, body, start)
 
 
-def gram_rows(rank, parts, before, cost):
+def gram_rows(rank, parts, before, cost, copied=False):
     rows, width = parts[0].shape
 
     def kernel(rank_ref, *refs):
-        ins, out = refs[:GROUP], refs[-1]
+        ins, outs = refs[:GROUP], refs[GROUP + (before is not None) :]
+        out = outs[0]
 
         def step(where, columns, totals):
-            wide = [ref[where, columns].astype(jnp.float32) for ref in ins]
+            held = [ref[where, columns] for ref in ins]
+            for target, value in zip(outs[1:], held):
+                target[where, columns] = value
+            wide = [value.astype(jnp.float32) for value in held]
             products = []
             for first, second in (wide[:2], wide[2:]):
                 both, apart = first + second, first - second
@@ -156,7 +162,8 @@
 
     shape = jax.ShapeDtypeStruct((GRAM_ROWS, LANES), jnp.float32)
     inputs = list(parts) + ([] if before is None else [before])
-    return call(kernel, "gram_rows", rank, inputs, [shape], cost)[0]
+    copies = [jax.ShapeDtypeStruct(part.shape, part.dtype) for part in parts] if copied else []
+    return call(kernel, "gram_rows", rank, inputs, [shape] + copies, cost)
 
 
 def total(values, cost):
@@ -269,16 +276,22 @@
 def pair_rows(rank, kept, received, level, layer, layers, before):
     rows, width = kept[0].shape
     count, ways = len(kept), len(received[0])
+    chooses = CHOSEN and ways > 1
 
     def kernel(rank_ref, *refs):
-        mine, out = refs[:count], refs[-1]
+        mine = refs[:count]
+        inputs_end = count + count * ways + (before is not None)
+        out, chosen = refs[inputs_end], refs[inputs_end + 1 :]
         totals = (jnp.zeros((8, LANES), jnp.float32),) * 3
         for number, left in enumerate(mine):
             theirs = refs[count + ways * number :][:ways]
 
-            def step(where, columns, totals, left=left, theirs=theirs):
+            def step(where, columns, totals, left=left, theirs=theirs, number=number):
                 a = left[where, columns].astype(jnp.float32)
-                b = chosen_rows(rank_ref, level, theirs, where, columns).astype(jnp.float32)
+                b = chosen_rows(rank_ref, level, theirs, where, columns)
+                if chooses:
+                    chosen[number][where, columns] = b
+                b = b.astype(jnp.float32)
                 new = [
                     total + (product[:8] + product[8:])
                     for total, product in zip(totals, (a * b, a * a, b * b))
@@ -288,16 +301,19 @@
             totals = tiles(rows, width, step, totals)
         upper = ((rank_ref[0] >> level) & 1) == 1
         dot_value, norm_mine, norm_theirs = [jnp.sum(t, axis=0, keepdims=True) for t in totals]
-        out[...] = jnp.zeros_like(out) if before is None else refs[-2][...]
+        out[...] = jnp.zeros_like(out) if before is None else refs[inputs_end - 1][...]
         base = 3 * layer
         out[base : base + 1, :] = dot_value
         out[base + 1 : base + 2, :] = jnp.where(upper, norm_theirs, norm_mine)
         out[base + 2 : base + 3, :] = jnp.where(upper, norm_mine, norm_theirs)
 
-    shape = jax.ShapeDtypeStruct((-(-3 * layers // 8) * 8, LANES), jnp.float32)
+    shapes = [jax.ShapeDtypeStruct((-(-3 * layers // 8) * 8, LANES), jnp.float32)]
+    if chooses:
+        shapes += [jax.ShapeDtypeStruct((rows, width), jnp.bfloat16)] * count
     inputs = list(kept) + [part for parts in received for part in parts]
     inputs += [] if before is None else [before]
-    return call(kernel, "pair_rows", rank, inputs, [shape])[0]
+    sums, *chosen = call(kernel, "pair_rows", rank, inputs, shapes)
+    return sums, [[part] for part in chosen] if chooses else received
 
 
 def pair_combine(rank, sums, kept, received, level):
@@ -409,7 +425,10 @@
         for tail in tails:
             parts = [held[layer, tail] for held in (own, crossed, far, far_crossed)]
             cost = COST if layer < layers - 1 else FIRST_COST if gram is None else GRAM_COST
-            gram = gram_rows(position, parts, gram, cost)
+            copied = COPIED and layer == layers - 1 and gram is None
+            gram, *copies = gram_rows(position, parts, gram, cost, copied)
+            for held, copy in zip((own, crossed, far, far_crossed), copies):
+                held[layer, tail] = copy
         return gram
 
     def group_result(layer, gram):
@@ -500,7 +519,9 @@
         kept = [[combined[layer][tail] for tail in keep] for layer in range(layers)]
         totals = None
         for layer in range(layers):
-            totals = pair_rows(position, kept[layer], received[layer], level, layer, layers, totals)
+            totals, received[layer] = pair_rows(
+                position, kept[layer], received[layer], level, layer, layers, totals
+            )
         bits = [("rep", 1 << bit) for bit in range(level + 1)]
         hops = spans[:-1] + [spans[-1] + bits[:1]] + [bits[i : i + 2] for i in range(1, level + 1, 2)]
         totals = summed(totals, hops)

time: 160 us -> 160 us (level)
  transfers between devices with their start and end apart: 37 -> 37, of which waited for: 26 -> 26; matrix products, arithmetic and copies ran while one was open for 0% -> 0% of each run, Pallas kernels for 26% -> 27%
where the time goes in v7:
time: 160 us
  waiting for transfers between devices  55.6 us (35%)
  starting transfers between devices  54.2 us (34%)
  Pallas kernels  49.7 us (31%)
    ppermute x31, waiting for transfers between devices, exchange(): lax.ppermute(value, axis, [(i, i ^ mask) for i in range(lax.axis_size(axi...  44.4 us
    ppermute x31, starting transfers between devices, exchange(): lax.ppermute(value, axis, [(i, i ^ mask) for i in range(lax.axis_size(axi...  40.1 us
    pallas_call x6, Pallas kernels, block_pairs(): pl.pallas_call(kernel, grid_spec=pltpu.PrefetchScalarGridSpec(num_scalar_...  37.4 us
    pallas_call x11, Pallas kernels, call(): pl.pallas_call(kernel, in_specs=[pl.BlockSpec(memory_space=pltpu.SMEM)] +...  12.3 us
    ppermute x4, starting transfers between devices, swap(): return lax.ppermute(value, 'rep', pairs)  12.1 us
    ppermute x4, waiting for transfers between devices, swap(): return lax.ppermute(value, 'rep', pairs)  9.1 us
  transfers between devices with their start and end apart: 37, of which 26 were waited for; matrix products, arithmetic and copies ran while one was open for 0% of the time, Pallas kernels for 27%

profile of v7, /device:TPU:0, one launch (start us, length us, event | category | flops | bytes accessed | tf_op | source)
XLA Modules:
  0.0 159.7 jit_solution(749189485869642083)
XLA Ops:
  0.0 5.1 %block_pairs.7 = (bf16[256,1024]{1,0:T(8,128)(2,1)S(1)}, bf16[256,1024]{1,0:T(8,128)(2,1)S(1)}) custom-call(s32[1]{0:T(128)} %bitcast.rank_ref, bf16[2,2048,2048]{2,1,0:T(8,128)(2,1)} %a_ref.9, bf16[2,2048,1024]{2,1,0:T(8,128)(2,1)} %b_ref.11), custom_call_target="tpu_custom_call" | custom-call | flops 1600000000 | bytes 1024 | tf_op jit(solution)/shard_map/block_pairs/pallas_call | solution.py:91
  5.1 3.0 %collective-permute-start = (bf16[256,1024]{1,0:T(8,128)(2,1)S(1)}, bf16[256,1024]{1,0:T(8,128)(2,1)S(1)}, u32[]{:S(2)}, u32[]{:S(2)}) collective-permute-start(bf16[256,1024]{1,0:T(8,128)(2,1)S(1)} %get-tuple-element.69), channel_id=1, source_target_pairs={{0,4},{4,0},{8,12},{12,8},{16,20},{20,16},{24,28},{28,24},{1,5},{5... | collective-permute-start | bytes 1572872 | tf_op jit(solution)/shard_map/ppermute | solution.py:28
  9.7 5.1 %block_pairs.9 = (bf16[256,1024]{1,0:T(8,128)(2,1)S(1)}, bf16[256,1024]{1,0:T(8,128)(2,1)S(1)}) custom-call(s32[1]{0:T(128)} %bitcast.rank_ref, bf16[2,2048,2048]{2,1,0:T(8,128)(2,1)} %a_ref.9, bf16[2,2048,1024]{2,1,0:T(8,128)(2,1)} %b_ref.11), custom_call_target="tpu_custom_call" | custom-call | flops 1600000000 | bytes 1024 | tf_op jit(solution)/shard_map/block_pairs/pallas_call | solution.py:91
  15.4 5.1 %block_pairs.6 = (bf16[256,1024]{1,0:T(8,128)(2,1)S(1)}, bf16[256,1024]{1,0:T(8,128)(2,1)S(1)}) custom-call(s32[1]{0:T(128)} %bitcast.rank_ref, bf16[2,2048,2048]{2,1,0:T(8,128)(2,1)} %a_ref.9, bf16[2,2048,1024]{2,1,0:T(8,128)(2,1)} %b_ref.11), custom_call_target="tpu_custom_call" | custom-call | flops 1600000000 | bytes 1024 | tf_op jit(solution)/shard_map/block_pairs/pallas_call | solution.py:91
  20.8 2.1 %collective-permute-done.1.refs_2_ = bf16[256,1024]{1,0:T(8,128)(2,1)S(1)} collective-permute-done((bf16[256,1024]{1,0:T(8,128)(2,1)S(1)}, bf16[256,1024]{1,0:T(8,128)(2,1)S(1)}, u32[]{:S(2)}, u32[]{:S(2)}) %collective-permute-start.1) | collective-permute-done | bytes 524320 | tf_op jit(solution)/shard_map/ppermute | solution.py:28
  23.0 2.1 %collective-permute-start.5 = (bf16[256,1024]{1,0:T(8,128)(2,1)S(1)}, bf16[256,1024]{1,0:T(8,128)(2,1)S(1)}, u32[]{:S(2)}, u32[]{:S(2)}) collective-permute-start(bf16[256,1024]{1,0:T(8,128)(2,1)S(1)} %collective-permute-done), channel_id=1, source_target_pairs={{0,8},{4,12},{8,0},{12,4},{16,24},{20,28},{24,16},{28,20},{1,9},{5... | collective-permute-start | bytes 1572872 | tf_op jit(solution)/shard_map/ppermute | solution.py:28
  25.0 5.1 %block_pairs.8 = (bf16[256,1024]{1,0:T(8,128)(2,1)S(1)}, bf16[256,1024]{1,0:T(8,128)(2,1)S(1)}) custom-call(s32[1]{0:T(128)} %bitcast.rank_ref, bf16[2,2048,2048]{2,1,0:T(8,128)(2,1)} %a_ref.9, bf16[2,2048,1024]{2,1,0:T(8,128)(2,1)} %b_ref.11), custom_call_target="tpu_custom_call" | custom-call | flops 1600000000 | bytes 1024 | tf_op jit(solution)/shard_map/block_pairs/pallas_call | solution.py:91
  32.1 2.1 %collective-permute-done.3.refs_2_ = bf16[256,1024]{1,0:T(8,128)(2,1)S(1)} collective-permute-done((bf16[256,1024]{1,0:T(8,128)(2,1)S(1)}, bf16[256,1024]{1,0:T(8,128)(2,1)S(1)}, u32[]{:S(2)}, u32[]{:S(2)}) %collective-permute-start.3) | collective-permute-done | bytes 524320 | tf_op jit(solution)/shard_map/ppermute | solution.py:28
  34.2 2.1 %collective-permute-start.9 = (bf16[256,1024]{1,0:T(8,128)(2,1)S(1)}, bf16[256,1024]{1,0:T(8,128)(2,1)S(1)}, u32[]{:S(2)}, u32[]{:S(2)}) collective-permute-start(bf16[256,1024]{1,0:T(8,128)(2,1)S(1)} %collective-permute-done.2), channel_id=1, source_target_pairs={{0,8},{4,12},{8,0},{12,4},{16,24},{20,28},{24,16},{28,20},{1,9},{5... | collective-permute-start | bytes 1572872 | tf_op jit(solution)/shard_map/ppermute | solution.py:28
  36.3 5.1 %block_pairs.11 = (bf16[256,1024]{1,0:T(8,128)(2,1)S(1)}, bf16[256,1024]{1,0:T(8,128)(2,1)S(1)}) custom-call(s32[1]{0:T(128)} %bitcast.rank_ref, bf16[2,2048,2048]{2,1,0:T(8,128)(2,1)} %a_ref.9, bf16[2,2048,1024]{2,1,0:T(8,128)(2,1)} %b_ref.11), custom_call_target="tpu_custom_call" | custom-call | flops 1600000000 | bytes 1024 | tf_op jit(solution)/shard_map/block_pairs/pallas_call | solution.py:91
  43.3 2.1 %collective-permute-done.5.refs_3_ = bf16[256,1024]{1,0:T(8,128)(2,1)S(1)} collective-permute-done((bf16[256,1024]{1,0:T(8,128)(2,1)S(1)}, bf16[256,1024]{1,0:T(8,128)(2,1)S(1)}, u32[]{:S(2)}, u32[]{:S(2)}) %collective-permute-start.5) | collective-permute-done | bytes 524320 | tf_op jit(solution)/shard_map/ppermute | solution.py:28
  45.5 2.1 %collective-permute-start.7 = (bf16[256,1024]{1,0:T(8,128)(2,1)S(1)}, bf16[256,1024]{1,0:T(8,128)(2,1)S(1)}, u32[]{:S(2)}, u32[]{:S(2)}) collective-permute-start(bf16[256,1024]{1,0:T(8,128)(2,1)S(1)} %get-tuple-element.84), channel_id=1, source_target_pairs={{0,8},{4,12},{8,0},{12,4},{16,24},{20,28},{24,16},{28,20},{1,9},{5... | collective-permute-start | bytes 1572872 | tf_op jit(solution)/shard_map/ppermute | solution.py:28
  47.5 12.1 %block_pairs.10 = (bf16[256,1024]{1,0:T(8,128)(2,1)S(1)}, bf16[256,1024]{1,0:T(8,128)(2,1)S(1)}, bf16[256,1024]{1,0:T(8,128)(2,1)S(1)}, bf16[256,1024]{1,0:T(8,1...) custom-call(s32[1]{0:T(128)} %bitcast.rank_ref, bf16[2,2048,2048]{2,1,0:T(8,128)(2,1)} %a_ref.9, ...), custom_call_target="tpu_custom_call" | custom-call | flops 1600000000 | bytes 1024 | tf_op jit(solution)/shard_map/block_pairs/pallas_call | solution.py:91
  65.8 2.1 %collective-permute-done.7.refs_2_ = bf16[256,1024]{1,0:T(8,128)(2,1)S(1)} collective-permute-done((bf16[256,1024]{1,0:T(8,128)(2,1)S(1)}, bf16[256,1024]{1,0:T(8,128)(2,1)S(1)}, u32[]{:S(2)}, u32[]{:S(2)}) %collective-permute-start.7) | collective-permute-done | bytes 524320 | tf_op jit(solution)/shard_map/ppermute | solution.py:28
  71.4 4.9 %collective-permute-done.15 = bf16[256,1024]{1,0:T(8,128)(2,1)S(1)} collective-permute-done((bf16[256,1024]{1,0:T(8,128)(2,1)S(1)}, bf16[256,1024]{1,0:T(8,128)(2,1)S(1)}, u32[]{:S(2)}, u32[]{:S(2)}) %collective-permute-start.15) | collective-permute-done | bytes 524320 | tf_op jit(solution)/shard_map/ppermute | solution.py:28
  83.7 2.1 %collective-permute-done.14 = f32[16,128]{1,0:T(8,128)S(1)} collective-permute-done((f32[16,128]{1,0:T(8,128)S(1)}, f32[16,128]{1,0:T(8,128)S(1)}, u32[]{:S(2)}, u32[]{:S(2)}) %collective-permute-start.14) | collective-permute-done | bytes 8224 | tf_op jit(solution)/shard_map/ppermute | solution.py:28
  88.3 2.9 %collective-permute-done.19.refs_1_ = bf16[256,1024]{1,0:T(8,128)(2,1)S(1)} collective-permute-done((bf16[256,1024]{1,0:T(8,128)(2,1)S(1)}, bf16[256,1024]{1,0:T(8,128)(2,1)S(1)}, u32[]{:S(2)}, u32[]{:S(2)}) %collective-permute-start.19) | collective-permute-done | bytes 524320 | tf_op jit(solution)/shard_map/ppermute | solution.py:28
  94.7 5.9 %collective-permute-done.17.refs_1_ = bf16[256,1024]{1,0:T(8,128)(2,1)S(1)} collective-permute-done((bf16[256,1024]{1,0:T(8,128)(2,1)S(1)}, bf16[256,1024]{1,0:T(8,128)(2,1)S(1)}, u32[]{:S(2)}, u32[]{:S(2)}) %collective-permute-start.17) | collective-permute-done | bytes 524320 | tf_op jit(solution)/shard_map/ppermute | solution.py:28
  104.9 2.1 %collective-permute-done.21 = f32[16,128]{1,0:T(8,128)S(1)} collective-permute-done((f32[16,128]{1,0:T(8,128)S(1)}, f32[16,128]{1,0:T(8,128)S(1)}, u32[]{:S(2)}, u32[]{:S(2)}) %collective-permute-start.21) | collective-permute-done | bytes 8224 | tf_op jit(solution)/shard_map/ppermute | solution.py:28
  107.0 5.5 %collective-permute-start.27 = (bf16[256,1024]{1,0:T(8,128)(2,1)S(1)}, bf16[256,1024]{1,0:T(8,128)(2,1)S(1)}, u32[]{:S(2)}, u32[]{:S(2)}) collective-permute-start(bf16[256,1024]{1,0:T(8,128)(2,1)S(1)} %group_combine.4), channel_id=1, source_target_pairs={{0,24},{4,28},{24,0},{28,4},{1,25},{5,29},{25,1},{29,5},{2,26},{6,... | collective-permute-start | bytes 1572872 | tf_op jit(solution)/shard_map/ppermute | solution.py:374
  121.2 5.3 %collective-permute-start.29 = (bf16[256,1024]{1,0:T(8,128)(2,1)S(1)}, bf16[256,1024]{1,0:T(8,128)(2,1)S(1)}, u32[]{:S(2)}, u32[]{:S(2)}) collective-permute-start(bf16[256,1024]{1,0:T(8,128)(2,1)S(1)} %group_combine.7), channel_id=1, source_target_pairs={{0,24},{4,28},{24,0},{28,4},{1,25},{5,29},{25,1},{29,5},{2,26},{6,... | collective-permute-start | bytes 1572872 | tf_op jit(solution)/shard_map/ppermute | solution.py:374
  128.5 9.1 %collective-permute-done.29.refs_2_ = bf16[256,1024]{1,0:T(8,128)(2,1)S(1)} collective-permute-done((bf16[256,1024]{1,0:T(8,128)(2,1)S(1)}, bf16[256,1024]{1,0:T(8,128)(2,1)S(1)}, u32[]{:S(2)}, u32[]{:S(2)}) %collective-permute-start.29) | collective-permute-done | bytes 524320 | tf_op jit(solution)/shard_map/ppermute | solution.py:374
  145.9 8.5 %collective-permute-start.35 = (f32[8,128]{1,0:T(8,128)S(1)}, f32[8,128]{1,0:T(8,128)S(1)}, u32[]{:S(2)}, u32[]{:S(2)}) collective-permute-start(f32[8,128]{1,0:T(8,128)S(1)} %total.6.refs_0_), channel_id=1, source_target_pairs={{0,16},{4,20},{8,24},{12,28},{16,0},{20,4},{24,8},{28,12},{1,17},{... | collective-permute-start | bytes 12296 | tf_op jit(solution)/shard_map/ppermute | solution.py:28
  156.0 2.0 %collective-permute-done.34.refs_1_ = f32[8,128]{1,0:T(8,128)S(1)} collective-permute-done((f32[8,128]{1,0:T(8,128)S(1)}, f32[8,128]{1,0:T(8,128)S(1)}, u32[]{:S(2)}, u32[]{:S(2)}) %collective-permute-start.34) | collective-permute-done | bytes 4128 | tf_op jit(solution)/shard_map/ppermute | solution.py:28
  (76 shorter events, 56.2 us)
Async XLA Ops:
  5.1 15.8 %collective-permute-start = (bf16[256,1024]{1,0:T(8,128)(2,1)S(1)}, bf16[256,1024]{1,0:T(8,128)(2,1)S(1)}, u32[]{:S(2)}, u32[]{:S(2)}) collective-permute-start(bf16[256,1024]{1,0:T(8,128)(2,1)S(1)} %get-tuple-element.69), channel_id=1, source_target_pairs={{0,4},{4,0},{8,12},{12,8},{16,20},{20,16},{24,28},{28,24},{1,5},{5... | collective-permute-start | bytes 1572872 | tf_op jit(solution)/shard_map/ppermute | solution.py:28
  8.1 14.8 %collective-permute-start.1 = (bf16[256,1024]{1,0:T(8,128)(2,1)S(1)}, bf16[256,1024]{1,0:T(8,128)(2,1)S(1)}, u32[]{:S(2)}, u32[]{:S(2)}) collective-permute-start(bf16[256,1024]{1,0:T(8,128)(2,1)S(1)} %get-tuple-element.70), channel_id=1, source_target_pairs={{0,8},{4,12},{8,0},{12,4},{16,24},{20,28},{24,16},{28,20},{1,9},{5... | collective-permute-start | bytes 1572872 | tf_op jit(solution)/shard_map/ppermute | solution.py:28
  14.7 17.3 %collective-permute-start.2 = (bf16[256,1024]{1,0:T(8,128)(2,1)S(1)}, bf16[256,1024]{1,0:T(8,128)(2,1)S(1)}, u32[]{:S(2)}, u32[]{:S(2)}) collective-permute-start(bf16[256,1024]{1,0:T(8,128)(2,1)S(1)} %get-tuple-element.74), channel_id=1, source_target_pairs={{0,4},{4,0},{8,12},{12,8},{16,20},{20,16},{24,28},{28,24},{1,5},{5... | collective-permute-start | bytes 1572872 | tf_op jit(solution)/shard_map/ppermute | solution.py:28
  15.3 18.8 %collective-permute-start.3 = (bf16[256,1024]{1,0:T(8,128)(2,1)S(1)}, bf16[256,1024]{1,0:T(8,128)(2,1)S(1)}, u32[]{:S(2)}, u32[]{:S(2)}) collective-permute-start(bf16[256,1024]{1,0:T(8,128)(2,1)S(1)} %get-tuple-element.75), channel_id=1, source_target_pairs={{0,8},{4,12},{8,0},{12,4},{16,24},{20,28},{24,16},{28,20},{1,9},{5... | collective-permute-start | bytes 1572872 | tf_op jit(solution)/shard_map/ppermute | solution.py:28
  22.9 20.4 %collective-permute-start.4 = (bf16[256,1024]{1,0:T(8,128)(2,1)S(1)}, bf16[256,1024]{1,0:T(8,128)(2,1)S(1)}, u32[]{:S(2)}, u32[]{:S(2)}) collective-permute-start(bf16[256,1024]{1,0:T(8,128)(2,1)S(1)} %get-tuple-element.81), channel_id=1, source_target_pairs={{0,4},{4,0},{8,12},{12,8},{16,20},{20,16},{24,28},{28,24},{1,5},{5... | collective-permute-start | bytes 1572872 | tf_op jit(solution)/shard_map/ppermute | solution.py:28
  23.0 22.4 %collective-permute-start.5 = (bf16[256,1024]{1,0:T(8,128)(2,1)S(1)}, bf16[256,1024]{1,0:T(8,128)(2,1)S(1)}, u32[]{:S(2)}, u32[]{:S(2)}) collective-permute-start(bf16[256,1024]{1,0:T(8,128)(2,1)S(1)} %collective-permute-done), channel_id=1, source_target_pairs={{0,8},{4,12},{8,0},{12,4},{16,24},{20,28},{24,16},{28,20},{1,9},{5... | collective-permute-start | bytes 1572872 | tf_op jit(solution)/shard_map/ppermute | solution.py:28
  34.2 25.4 %collective-permute-start.8 = (bf16[256,1024]{1,0:T(8,128)(2,1)S(1)}, bf16[256,1024]{1,0:T(8,128)(2,1)S(1)}, u32[]{:S(2)}, u32[]{:S(2)}) collective-permute-start(bf16[256,1024]{1,0:T(8,128)(2,1)S(1)} %get-tuple-element.90), channel_id=1, source_target_pairs={{0,4},{4,0},{8,12},{12,8},{16,20},{20,16},{24,28},{28,24},{1,5},{5... | collective-permute-start | bytes 1572872 | tf_op jit(solution)/shard_map/ppermute | solution.py:28
  34.2 25.4 %collective-permute-start.9 = (bf16[256,1024]{1,0:T(8,128)(2,1)S(1)}, bf16[256,1024]{1,0:T(8,128)(2,1)S(1)}, u32[]{:S(2)}, u32[]{:S(2)}) collective-permute-start(bf16[256,1024]{1,0:T(8,128)(2,1)S(1)} %collective-permute-done.2), channel_id=1, source_target_pairs={{0,8},{4,12},{8,0},{12,4},{16,24},{20,28},{24,16},{28,20},{1,9},{5... | collective-permute-start | bytes 1572872 | tf_op jit(solution)/shard_map/ppermute | solution.py:28
  45.4 20.4 %collective-permute-start.6 = (bf16[256,1024]{1,0:T(8,128)(2,1)S(1)}, bf16[256,1024]{1,0:T(8,128)(2,1)S(1)}, u32[]{:S(2)}, u32[]{:S(2)}) collective-permute-start(bf16[256,1024]{1,0:T(8,128)(2,1)S(1)} %get-tuple-element.83), channel_id=1, source_target_pairs={{0,4},{4,0},{8,12},{12,8},{16,20},{20,16},{24,28},{28,24},{1,5},{5... | collective-permute-start | bytes 1572872 | tf_op jit(solution)/shard_map/ppermute | solution.py:28
  45.5 22.4 %collective-permute-start.7 = (bf16[256,1024]{1,0:T(8,128)(2,1)S(1)}, bf16[256,1024]{1,0:T(8,128)(2,1)S(1)}, u32[]{:S(2)}, u32[]{:S(2)}) collective-permute-start(bf16[256,1024]{1,0:T(8,128)(2,1)S(1)} %get-tuple-element.84), channel_id=1, source_target_pairs={{0,8},{4,12},{8,0},{12,4},{16,24},{20,28},{24,16},{28,20},{1,9},{5... | collective-permute-start | bytes 1572872 | tf_op jit(solution)/shard_map/ppermute | solution.py:28
  59.6 16.7 %collective-permute-start.15 = (bf16[256,1024]{1,0:T(8,128)(2,1)S(1)}, bf16[256,1024]{1,0:T(8,128)(2,1)S(1)}, u32[]{:S(2)}, u32[]{:S(2)}) collective-permute-start(bf16[256,1024]{1,0:T(8,128)(2,1)S(1)} %get-tuple-element.105), channel_id=1, source_target_pairs={{0,4},{4,0},{8,12},{12,8},{16,20},{20,16},{24,28},{28,24},{1,5},{5... | collective-permute-start | bytes 1572872 | tf_op jit(solution)/shard_map/ppermute | solution.py:28
  61.2 17.0 %collective-permute-start.16 = (bf16[256,1024]{1,0:T(8,128)(2,1)S(1)}, bf16[256,1024]{1,0:T(8,128)(2,1)S(1)}, u32[]{:S(2)}, u32[]{:S(2)}) collective-permute-start(bf16[256,1024]{1,0:T(8,128)(2,1)S(1)} %get-tuple-element.106), channel_id=1, source_target_pairs={{0,8},{4,12},{8,0},{12,4},{16,24},{20,28},{24,16},{28,20},{1,9},{5... | collective-permute-start | bytes 1572872 | tf_op jit(solution)/shard_map/ppermute | solution.py:28
  67.9 11.8 %collective-permute-start.12 = (f32[16,128]{1,0:T(8,128)S(1)}, f32[16,128]{1,0:T(8,128)S(1)}, u32[]{:S(2)}, u32[]{:S(2)}) collective-permute-start(f32[16,128]{1,0:T(8,128)S(1)} %gram_rows.5.refs_0_), channel_id=1, source_target_pairs={{0,12},{4,8},{8,4},{12,0},{16,28},{20,24},{24,20},{28,16},{1,13},{... | collective-permute-start | bytes 24584 | tf_op jit(solution)/shard_map/ppermute | solution.py:28
  69.4 10.8 %collective-permute-start.11 = (f32[16,128]{1,0:T(8,128)S(1)}, f32[16,128]{1,0:T(8,128)S(1)}, u32[]{:S(2)}, u32[]{:S(2)}) collective-permute-start(f32[16,128]{1,0:T(8,128)S(1)} %gram_rows.5.refs_0_), channel_id=1, source_target_pairs={{0,8},{4,12},{8,0},{12,4},{16,24},{20,28},{24,16},{28,20},{1,9},{5... | collective-permute-start | bytes 24584 | tf_op jit(solution)/shard_map/ppermute | solution.py:28
  69.5 11.5 %collective-permute-start.10 = (f32[16,128]{1,0:T(8,128)S(1)}, f32[16,128]{1,0:T(8,128)S(1)}, u32[]{:S(2)}, u32[]{:S(2)}) collective-permute-start(f32[16,128]{1,0:T(8,128)S(1)} %gram_rows.5.refs_0_), channel_id=1, source_target_pairs={{0,4},{4,0},{8,12},{12,8},{16,20},{20,16},{24,28},{28,24},{1,5},{5... | collective-permute-start | bytes 24584 | tf_op jit(solution)/shard_map/ppermute | solution.py:28
  76.3 14.9 %collective-permute-start.19 = (bf16[256,1024]{1,0:T(8,128)(2,1)S(1)}, bf16[256,1024]{1,0:T(8,128)(2,1)S(1)}, u32[]{:S(2)}, u32[]{:S(2)}) collective-permute-start(bf16[256,1024]{1,0:T(8,128)(2,1)S(1)} %get-tuple-element.111), channel_id=1, source_target_pairs={{0,4},{4,0},{8,12},{12,8},{16,20},{20,16},{24,28},{28,24},{1,5},{5... | collective-permute-start | bytes 1572872 | tf_op jit(solution)/shard_map/ppermute | solution.py:28
  78.1 14.9 %collective-permute-start.20 = (bf16[256,1024]{1,0:T(8,128)(2,1)S(1)}, bf16[256,1024]{1,0:T(8,128)(2,1)S(1)}, u32[]{:S(2)}, u32[]{:S(2)}) collective-permute-start(bf16[256,1024]{1,0:T(8,128)(2,1)S(1)} %collective-permute-done.6), channel_id=1, source_target_pairs={{0,8},{4,12},{8,0},{12,4},{16,24},{20,28},{24,16},{28,20},{1,9},{5... | collective-permute-start | bytes 1572872 | tf_op jit(solution)/shard_map/ppermute | solution.py:28
  79.7 20.9 %collective-permute-start.17 = (bf16[256,1024]{1,0:T(8,128)(2,1)S(1)}, bf16[256,1024]{1,0:T(8,128)(2,1)S(1)}, u32[]{:S(2)}, u32[]{:S(2)}) collective-permute-start(bf16[256,1024]{1,0:T(8,128)(2,1)S(1)} %get-tuple-element.107), channel_id=1, source_target_pairs={{0,4},{4,0},{8,12},{12,8},{16,20},{20,16},{24,28},{28,24},{1,5},{5... | collective-permute-start | bytes 1572872 | tf_op jit(solution)/shard_map/ppermute | solution.py:28
  80.2 21.5 %collective-permute-start.18 = (bf16[256,1024]{1,0:T(8,128)(2,1)S(1)}, bf16[256,1024]{1,0:T(8,128)(2,1)S(1)}, u32[]{:S(2)}, u32[]{:S(2)}) collective-permute-start(bf16[256,1024]{1,0:T(8,128)(2,1)S(1)} %collective-permute-done.15), channel_id=1, source_target_pairs={{0,8},{4,12},{8,0},{12,4},{16,24},{20,28},{24,16},{28,20},{1,9},{5... | collective-permute-start | bytes 1572872 | tf_op jit(solution)/shard_map/ppermute | solution.py:28
  87.6 26.1 %collective-permute-start.23 = (bf16[256,1024]{1,0:T(8,128)(2,1)S(1)}, bf16[256,1024]{1,0:T(8,128)(2,1)S(1)}, u32[]{:S(2)}, u32[]{:S(2)}) collective-permute-start(bf16[256,1024]{1,0:T(8,128)(2,1)S(1)} %group_combine.4), channel_id=1, source_target_pairs={{8,16},{12,20},{16,8},{20,12},{9,17},{13,21},{17,9},{21,13},{10,18... | collective-permute-start | bytes 1572872 | tf_op jit(solution)/shard_map/ppermute | solution.py:374
  107.0 14.2 %collective-permute-start.27 = (bf16[256,1024]{1,0:T(8,128)(2,1)S(1)}, bf16[256,1024]{1,0:T(8,128)(2,1)S(1)}, u32[]{:S(2)}, u32[]{:S(2)}) collective-permute-start(bf16[256,1024]{1,0:T(8,128)(2,1)S(1)} %group_combine.4), channel_id=1, source_target_pairs={{0,24},{4,28},{24,0},{28,4},{1,25},{5,29},{25,1},{29,5},{2,26},{6,... | collective-permute-start | bytes 1572872 | tf_op jit(solution)/shard_map/ppermute | solution.py:374
  121.2 16.4 %collective-permute-start.29 = (bf16[256,1024]{1,0:T(8,128)(2,1)S(1)}, bf16[256,1024]{1,0:T(8,128)(2,1)S(1)}, u32[]{:S(2)}, u32[]{:S(2)}) collective-permute-start(bf16[256,1024]{1,0:T(8,128)(2,1)S(1)} %group_combine.7), channel_id=1, source_target_pairs={{0,24},{4,28},{24,0},{28,4},{1,25},{5,29},{25,1},{29,5},{2,26},{6,... | collective-permute-start | bytes 1572872 | tf_op jit(solution)/shard_map/ppermute | solution.py:374
  126.5 11.1 %collective-permute-start.28 = (bf16[256,1024]{1,0:T(8,128)(2,1)S(1)}, bf16[256,1024]{1,0:T(8,128)(2,1)S(1)}, u32[]{:S(2)}, u32[]{:S(2)}) collective-permute-start(bf16[256,1024]{1,0:T(8,128)(2,1)S(1)} %group_combine.7), channel_id=1, source_target_pairs={{8,16},{12,20},{16,8},{20,12},{9,17},{13,21},{17,9},{21,13},{10,18... | collective-permute-start | bytes 1572872 | tf_op jit(solution)/shard_map/ppermute | solution.py:374
  145.9 10.1 %collective-permute-start.35 = (f32[8,128]{1,0:T(8,128)S(1)}, f32[8,128]{1,0:T(8,128)S(1)}, u32[]{:S(2)}, u32[]{:S(2)}) collective-permute-start(f32[8,128]{1,0:T(8,128)S(1)} %total.6.refs_0_), channel_id=1, source_target_pairs={{0,16},{4,20},{8,24},{12,28},{16,0},{20,4},{24,8},{28,12},{1,17},{... | collective-permute-start | bytes 12296 | tf_op jit(solution)/shard_map/ppermute | solution.py:28
  (13 other events, 48.7 us)

commit v8 on v6

--- a/solution.py
+++ b/solution.py
@@ -491,7 +491,9 @@
     names = [tail for tail in tails if tail >> 2 & 1]
     values = [combined[-1][tail] for tail in names]
     for layer in range(layers - 1):
-        values, received[layer] = tied_ways(values, received[layer])
+        inner = [way[:1] for way in received[layer]]
+        values, inner = tied_ways(values, inner)
+        received[layer] = [a + b[1:] for a, b in zip(inner, received[layer])]
     combined[-1].update(zip(names, values))
     received.append(receive_all(combined[-1], 2))
 

time: 160 us -> 169 us (1.056)
  waiting for transfers between devices: 55.7 us -> 63.8 us
    ppermute x4, waiting for transfers between devices: 9.1 us -> 17 us  [swap(): return lax.ppermute(value, 'rep', pairs)]
    ppermute x31, starting transfers between devices: 40.1 us -> 44.2 us  [exchange(): lax.ppermute(value, axis, [(i, i ^ mask) for i in range(lax.axis_size(axi...]
    ppermute x4, starting transfers between devices: 12.1 us -> 9.02 us  [swap(): return lax.ppermute(value, 'rep', pairs)]
  transfers between devices with their start and end apart: 37 -> 37, of which waited for: 26 -> 27; matrix products, arithmetic and copies ran while one was open for 0% -> 0% of each run, Pallas kernels for 26% -> 25%
where the time goes in v8:
time: 169 us
  waiting for transfers between devices  63.8 us (38%)
  starting transfers between devices  55.3 us (33%)
  Pallas kernels  49.7 us (29%)
    ppermute x31, waiting for transfers between devices, exchange(): lax.ppermute(value, axis, [(i, i ^ mask) for i in range(lax.axis_size(axi...  44.7 us
    ppermute x31, starting transfers between devices, exchange(): lax.ppermute(value, axis, [(i, i ^ mask) for i in range(lax.axis_size(axi...  44.2 us
    pallas_call x6, Pallas kernels, block_pairs(): pl.pallas_call(kernel, grid_spec=pltpu.PrefetchScalarGridSpec(num_scalar_...  37.4 us
    ppermute x4, waiting for transfers between devices, swap(): return lax.ppermute(value, 'rep', pairs)  17 us
    pallas_call x11, Pallas kernels, call(): pl.pallas_call(kernel, in_specs=[pl.BlockSpec(memory_space=pltpu.SMEM)] +...  12.3 us
    ppermute x4, starting transfers between devices, swap(): return lax.ppermute(value, 'rep', pairs)  9.02 us
  transfers between devices with their start and end apart: 37, of which 27 were waited for; matrix products, arithmetic and copies ran while one was open for 0% of the time, Pallas kernels for 25%

profile of v8, /device:TPU:0, one launch (start us, length us, event | category | flops | bytes accessed | tf_op | source)
XLA Modules:
  0.0 169.0 jit_solution(2413496906601678279)
XLA Ops:
  0.0 5.1 %block_pairs.7 = (bf16[256,1024]{1,0:T(8,128)(2,1)S(1)}, bf16[256,1024]{1,0:T(8,128)(2,1)S(1)}) custom-call(s32[1]{0:T(128)} %bitcast.rank_ref, bf16[2,2048,2048]{2,1,0:T(8,128)(2,1)} %a_ref.9, bf16[2,2048,1024]{2,1,0:T(8,128)(2,1)} %b_ref.11), custom_call_target="tpu_custom_call" | custom-call | flops 1600000000 | bytes 1024 | tf_op jit(solution)/shard_map/block_pairs/pallas_call | solution.py:89
  5.1 3.0 %collective-permute-start = (bf16[256,1024]{1,0:T(8,128)(2,1)S(1)}, bf16[256,1024]{1,0:T(8,128)(2,1)S(1)}, u32[]{:S(2)}, u32[]{:S(2)}) collective-permute-start(bf16[256,1024]{1,0:T(8,128)(2,1)S(1)} %get-tuple-element.59), channel_id=1, source_target_pairs={{0,4},{4,0},{8,12},{12,8},{16,20},{20,16},{24,28},{28,24},{1,5},{5... | collective-permute-start | bytes 1572872 | tf_op jit(solution)/shard_map/ppermute | solution.py:26
  9.7 5.1 %block_pairs.9 = (bf16[256,1024]{1,0:T(8,128)(2,1)S(1)}, bf16[256,1024]{1,0:T(8,128)(2,1)S(1)}) custom-call(s32[1]{0:T(128)} %bitcast.rank_ref, bf16[2,2048,2048]{2,1,0:T(8,128)(2,1)} %a_ref.9, bf16[2,2048,1024]{2,1,0:T(8,128)(2,1)} %b_ref.11), custom_call_target="tpu_custom_call" | custom-call | flops 1600000000 | bytes 1024 | tf_op jit(solution)/shard_map/block_pairs/pallas_call | solution.py:89
  15.4 5.1 %block_pairs.6 = (bf16[256,1024]{1,0:T(8,128)(2,1)S(1)}, bf16[256,1024]{1,0:T(8,128)(2,1)S(1)}) custom-call(s32[1]{0:T(128)} %bitcast.rank_ref, bf16[2,2048,2048]{2,1,0:T(8,128)(2,1)} %a_ref.9, bf16[2,2048,1024]{2,1,0:T(8,128)(2,1)} %b_ref.11), custom_call_target="tpu_custom_call" | custom-call | flops 1600000000 | bytes 1024 | tf_op jit(solution)/shard_map/block_pairs/pallas_call | solution.py:89
  20.8 2.1 %collective-permute-done.1.refs_2_ = bf16[256,1024]{1,0:T(8,128)(2,1)S(1)} collective-permute-done((bf16[256,1024]{1,0:T(8,128)(2,1)S(1)}, bf16[256,1024]{1,0:T(8,128)(2,1)S(1)}, u32[]{:S(2)}, u32[]{:S(2)}) %collective-permute-start.1) | collective-permute-done | bytes 524320 | tf_op jit(solution)/shard_map/ppermute | solution.py:26
  23.0 2.1 %collective-permute-start.5 = (bf16[256,1024]{1,0:T(8,128)(2,1)S(1)}, bf16[256,1024]{1,0:T(8,128)(2,1)S(1)}, u32[]{:S(2)}, u32[]{:S(2)}) collective-permute-start(bf16[256,1024]{1,0:T(8,128)(2,1)S(1)} %collective-permute-done), channel_id=1, source_target_pairs={{0,8},{4,12},{8,0},{12,4},{16,24},{20,28},{24,16},{28,20},{1,9},{5... | collective-permute-start | bytes 1572872 | tf_op jit(solution)/shard_map/ppermute | solution.py:26
  25.0 5.1 %block_pairs.8 = (bf16[256,1024]{1,0:T(8,128)(2,1)S(1)}, bf16[256,1024]{1,0:T(8,128)(2,1)S(1)}) custom-call(s32[1]{0:T(128)} %bitcast.rank_ref, bf16[2,2048,2048]{2,1,0:T(8,128)(2,1)} %a_ref.9, bf16[2,2048,1024]{2,1,0:T(8,128)(2,1)} %b_ref.11), custom_call_target="tpu_custom_call" | custom-call | flops 1600000000 | bytes 1024 | tf_op jit(solution)/shard_map/block_pairs/pallas_call | solution.py:89
  32.1 2.1 %collective-permute-done.3.refs_2_ = bf16[256,1024]{1,0:T(8,128)(2,1)S(1)} collective-permute-done((bf16[256,1024]{1,0:T(8,128)(2,1)S(1)}, bf16[256,1024]{1,0:T(8,128)(2,1)S(1)}, u32[]{:S(2)}, u32[]{:S(2)}) %collective-permute-start.3) | collective-permute-done | bytes 524320 | tf_op jit(solution)/shard_map/ppermute | solution.py:26
  34.2 2.1 %collective-permute-start.9 = (bf16[256,1024]{1,0:T(8,128)(2,1)S(1)}, bf16[256,1024]{1,0:T(8,128)(2,1)S(1)}, u32[]{:S(2)}, u32[]{:S(2)}) collective-permute-start(bf16[256,1024]{1,0:T(8,128)(2,1)S(1)} %collective-permute-done.2), channel_id=1, source_target_pairs={{0,8},{4,12},{8,0},{12,4},{16,24},{20,28},{24,16},{28,20},{1,9},{5... | collective-permute-start | bytes 1572872 | tf_op jit(solution)/shard_map/ppermute | solution.py:26
  36.3 5.1 %block_pairs.11 = (bf16[256,1024]{1,0:T(8,128)(2,1)S(1)}, bf16[256,1024]{1,0:T(8,128)(2,1)S(1)}) custom-call(s32[1]{0:T(128)} %bitcast.rank_ref, bf16[2,2048,2048]{2,1,0:T(8,128)(2,1)} %a_ref.9, bf16[2,2048,1024]{2,1,0:T(8,128)(2,1)} %b_ref.11), custom_call_target="tpu_custom_call" | custom-call | flops 1600000000 | bytes 1024 | tf_op jit(solution)/shard_map/block_pairs/pallas_call | solution.py:89
  43.3 2.1 %collective-permute-done.5.refs_3_ = bf16[256,1024]{1,0:T(8,128)(2,1)S(1)} collective-permute-done((bf16[256,1024]{1,0:T(8,128)(2,1)S(1)}, bf16[256,1024]{1,0:T(8,128)(2,1)S(1)}, u32[]{:S(2)}, u32[]{:S(2)}) %collective-permute-start.5) | collective-permute-done | bytes 524320 | tf_op jit(solution)/shard_map/ppermute | solution.py:26
  47.5 12.1 %block_pairs.10 = (bf16[256,1024]{1,0:T(8,128)(2,1)S(1)}, bf16[256,1024]{1,0:T(8,128)(2,1)S(1)}, bf16[256,1024]{1,0:T(8,128)(2,1)S(1)}, bf16[256,1024]{1,0:T(8,1...) custom-call(s32[1]{0:T(128)} %bitcast.rank_ref, bf16[2,2048,2048]{2,1,0:T(8,128)(2,1)} %a_ref.9, ...), custom_call_target="tpu_custom_call" | custom-call | flops 1600000000 | bytes 1024 | tf_op jit(solution)/shard_map/block_pairs/pallas_call | solution.py:89
  65.8 2.1 %collective-permute-done.7.refs_2_ = bf16[256,1024]{1,0:T(8,128)(2,1)S(1)} collective-permute-done((bf16[256,1024]{1,0:T(8,128)(2,1)S(1)}, bf16[256,1024]{1,0:T(8,128)(2,1)S(1)}, u32[]{:S(2)}, u32[]{:S(2)}) %collective-permute-start.7) | collective-permute-done | bytes 524320 | tf_op jit(solution)/shard_map/ppermute | solution.py:26
  71.4 4.9 %collective-permute-done.15 = bf16[256,1024]{1,0:T(8,128)(2,1)S(1)} collective-permute-done((bf16[256,1024]{1,0:T(8,128)(2,1)S(1)}, bf16[256,1024]{1,0:T(8,128)(2,1)S(1)}, u32[]{:S(2)}, u32[]{:S(2)}) %collective-permute-start.15) | collective-permute-done | bytes 524320 | tf_op jit(solution)/shard_map/ppermute | solution.py:26
  83.7 2.1 %collective-permute-done.14 = f32[16,128]{1,0:T(8,128)S(1)} collective-permute-done((f32[16,128]{1,0:T(8,128)S(1)}, f32[16,128]{1,0:T(8,128)S(1)}, u32[]{:S(2)}, u32[]{:S(2)}) %collective-permute-start.14) | collective-permute-done | bytes 8224 | tf_op jit(solution)/shard_map/ppermute | solution.py:26
  88.3 2.9 %collective-permute-done.19.refs_1_ = bf16[256,1024]{1,0:T(8,128)(2,1)S(1)} collective-permute-done((bf16[256,1024]{1,0:T(8,128)(2,1)S(1)}, bf16[256,1024]{1,0:T(8,128)(2,1)S(1)}, u32[]{:S(2)}, u32[]{:S(2)}) %collective-permute-start.19) | collective-permute-done | bytes 524320 | tf_op jit(solution)/shard_map/ppermute | solution.py:26
  94.5 6.0 %collective-permute-done.17.refs_1_ = bf16[256,1024]{1,0:T(8,128)(2,1)S(1)} collective-permute-done((bf16[256,1024]{1,0:T(8,128)(2,1)S(1)}, bf16[256,1024]{1,0:T(8,128)(2,1)S(1)}, u32[]{:S(2)}, u32[]{:S(2)}) %collective-permute-start.17) | collective-permute-done | bytes 524320 | tf_op jit(solution)/shard_map/ppermute | solution.py:26
  104.9 2.1 %collective-permute-done.21 = f32[16,128]{1,0:T(8,128)S(1)} collective-permute-done((f32[16,128]{1,0:T(8,128)S(1)}, f32[16,128]{1,0:T(8,128)S(1)}, u32[]{:S(2)}, u32[]{:S(2)}) %collective-permute-start.21) | collective-permute-done | bytes 8224 | tf_op jit(solution)/shard_map/ppermute | solution.py:26
  114.8 5.5 %collective-permute-start.29 = (bf16[256,1024]{1,0:T(8,128)(2,1)S(1)}, bf16[256,1024]{1,0:T(8,128)(2,1)S(1)}, u32[]{:S(2)}, u32[]{:S(2)}) collective-permute-start(bf16[256,1024]{1,0:T(8,128)(2,1)S(1)} %group_combine.4), channel_id=1, source_target_pairs={{0,24},{4,28},{24,0},{28,4},{1,25},{5,29},{25,1},{29,5},{2,26},{6,... | collective-permute-start | bytes 1572872 | tf_op jit(solution)/shard_map/ppermute | solution.py:358
  121.1 2.1 %collective-permute-start.28 = (bf16[256,1024]{1,0:T(8,128)(2,1)S(1)}, bf16[256,1024]{1,0:T(8,128)(2,1)S(1)}, u32[]{:S(2)}, u32[]{:S(2)}) collective-permute-start(bf16[256,1024]{1,0:T(8,128)(2,1)S(1)} %group_combine.7), channel_id=1, source_target_pairs={{0,24},{4,28},{24,0},{28,4},{1,25},{5,29},{25,1},{29,5},{2,26},{6,... | collective-permute-start | bytes 1572872 | tf_op jit(solution)/shard_map/ppermute | solution.py:358
  124.8 8.6 %collective-permute-done.29.refs_2_ = bf16[256,1024]{1,0:T(8,128)(2,1)S(1)} collective-permute-done((bf16[256,1024]{1,0:T(8,128)(2,1)S(1)}, bf16[256,1024]{1,0:T(8,128)(2,1)S(1)}, u32[]{:S(2)}, u32[]{:S(2)}) %collective-permute-start.29) | collective-permute-done | bytes 524320 | tf_op jit(solution)/shard_map/ppermute | solution.py:358
  133.8 8.5 %collective-permute-done.28.refs_2_.refs_5_ = bf16[256,1024]{1,0:T(8,128)(2,1)S(1)} collective-permute-done((bf16[256,1024]{1,0:T(8,128)(2,1)S(1)}, bf16[256,1024]{1,0:T(8,128)(2,1)S(1)}, u32[]{:S(2)}, u32[]{:S(2)}) %collective-permute-start.28) | collective-permute-done | bytes 524320 | tf_op jit(solution)/shard_map/ppermute | solution.py:358
  149.7 3.5 %collective-permute-start.36 = (f32[8,128]{1,0:T(8,128)S(1)}, f32[8,128]{1,0:T(8,128)S(1)}, u32[]{:S(2)}, u32[]{:S(2)}) collective-permute-start(f32[8,128]{1,0:T(8,128)S(1)} %total.6.refs_0_), channel_id=1, source_target_pairs={{0,24},{4,28},{8,16},{12,20},{16,8},{20,12},{24,0},{28,4},{1,25},{... | collective-permute-start | bytes 12296 | tf_op jit(solution)/shard_map/ppermute | solution.py:26
  153.2 10.3 %collective-permute-start.35 = (f32[8,128]{1,0:T(8,128)S(1)}, f32[8,128]{1,0:T(8,128)S(1)}, u32[]{:S(2)}, u32[]{:S(2)}) collective-permute-start(f32[8,128]{1,0:T(8,128)S(1)} %total.6.refs_0_), channel_id=1, source_target_pairs={{0,16},{4,20},{8,24},{12,28},{16,0},{20,4},{24,8},{28,12},{1,17},{... | collective-permute-start | bytes 12296 | tf_op jit(solution)/shard_map/ppermute | solution.py:26
  (76 shorter events, 59.3 us)
Async XLA Ops:
  5.1 15.8 %collective-permute-start = (bf16[256,1024]{1,0:T(8,128)(2,1)S(1)}, bf16[256,1024]{1,0:T(8,128)(2,1)S(1)}, u32[]{:S(2)}, u32[]{:S(2)}) collective-permute-start(bf16[256,1024]{1,0:T(8,128)(2,1)S(1)} %get-tuple-element.59), channel_id=1, source_target_pairs={{0,4},{4,0},{8,12},{12,8},{16,20},{20,16},{24,28},{28,24},{1,5},{5... | collective-permute-start | bytes 1572872 | tf_op jit(solution)/shard_map/ppermute | solution.py:26
  8.1 14.8 %collective-permute-start.1 = (bf16[256,1024]{1,0:T(8,128)(2,1)S(1)}, bf16[256,1024]{1,0:T(8,128)(2,1)S(1)}, u32[]{:S(2)}, u32[]{:S(2)}) collective-permute-start(bf16[256,1024]{1,0:T(8,128)(2,1)S(1)} %get-tuple-element.60), channel_id=1, source_target_pairs={{0,8},{4,12},{8,0},{12,4},{16,24},{20,28},{24,16},{28,20},{1,9},{5... | collective-permute-start | bytes 1572872 | tf_op jit(solution)/shard_map/ppermute | solution.py:26
  14.7 17.3 %collective-permute-start.2 = (bf16[256,1024]{1,0:T(8,128)(2,1)S(1)}, bf16[256,1024]{1,0:T(8,128)(2,1)S(1)}, u32[]{:S(2)}, u32[]{:S(2)}) collective-permute-start(bf16[256,1024]{1,0:T(8,128)(2,1)S(1)} %get-tuple-element.64), channel_id=1, source_target_pairs={{0,4},{4,0},{8,12},{12,8},{16,20},{20,16},{24,28},{28,24},{1,5},{5... | collective-permute-start | bytes 1572872 | tf_op jit(solution)/shard_map/ppermute | solution.py:26
  15.3 18.8 %collective-permute-start.3 = (bf16[256,1024]{1,0:T(8,128)(2,1)S(1)}, bf16[256,1024]{1,0:T(8,128)(2,1)S(1)}, u32[]{:S(2)}, u32[]{:S(2)}) collective-permute-start(bf16[256,1024]{1,0:T(8,128)(2,1)S(1)} %get-tuple-element.65), channel_id=1, source_target_pairs={{0,8},{4,12},{8,0},{12,4},{16,24},{20,28},{24,16},{28,20},{1,9},{5... | collective-permute-start | bytes 1572872 | tf_op jit(solution)/shard_map/ppermute | solution.py:26
  22.9 20.4 %collective-permute-start.4 = (bf16[256,1024]{1,0:T(8,128)(2,1)S(1)}, bf16[256,1024]{1,0:T(8,128)(2,1)S(1)}, u32[]{:S(2)}, u32[]{:S(2)}) collective-permute-start(bf16[256,1024]{1,0:T(8,128)(2,1)S(1)} %get-tuple-element.71), channel_id=1, source_target_pairs={{0,4},{4,0},{8,12},{12,8},{16,20},{20,16},{24,28},{28,24},{1,5},{5... | collective-permute-start | bytes 1572872 | tf_op jit(solution)/shard_map/ppermute | solution.py:26
  23.0 22.4 %collective-permute-start.5 = (bf16[256,1024]{1,0:T(8,128)(2,1)S(1)}, bf16[256,1024]{1,0:T(8,128)(2,1)S(1)}, u32[]{:S(2)}, u32[]{:S(2)}) collective-permute-start(bf16[256,1024]{1,0:T(8,128)(2,1)S(1)} %collective-permute-done), channel_id=1, source_target_pairs={{0,8},{4,12},{8,0},{12,4},{16,24},{20,28},{24,16},{28,20},{1,9},{5... | collective-permute-start | bytes 1572872 | tf_op jit(solution)/shard_map/ppermute | solution.py:26
  34.2 25.4 %collective-permute-start.8 = (bf16[256,1024]{1,0:T(8,128)(2,1)S(1)}, bf16[256,1024]{1,0:T(8,128)(2,1)S(1)}, u32[]{:S(2)}, u32[]{:S(2)}) collective-permute-start(bf16[256,1024]{1,0:T(8,128)(2,1)S(1)} %get-tuple-element.80), channel_id=1, source_target_pairs={{0,4},{4,0},{8,12},{12,8},{16,20},{20,16},{24,28},{28,24},{1,5},{5... | collective-permute-start | bytes 1572872 | tf_op jit(solution)/shard_map/ppermute | solution.py:26
  34.2 25.4 %collective-permute-start.9 = (bf16[256,1024]{1,0:T(8,128)(2,1)S(1)}, bf16[256,1024]{1,0:T(8,128)(2,1)S(1)}, u32[]{:S(2)}, u32[]{:S(2)}) collective-permute-start(bf16[256,1024]{1,0:T(8,128)(2,1)S(1)} %collective-permute-done.2), channel_id=1, source_target_pairs={{0,8},{4,12},{8,0},{12,4},{16,24},{20,28},{24,16},{28,20},{1,9},{5... | collective-permute-start | bytes 1572872 | tf_op jit(solution)/shard_map/ppermute | solution.py:26
  45.4 20.4 %collective-permute-start.6 = (bf16[256,1024]{1,0:T(8,128)(2,1)S(1)}, bf16[256,1024]{1,0:T(8,128)(2,1)S(1)}, u32[]{:S(2)}, u32[]{:S(2)}) collective-permute-start(bf16[256,1024]{1,0:T(8,128)(2,1)S(1)} %get-tuple-element.73), channel_id=1, source_target_pairs={{0,4},{4,0},{8,12},{12,8},{16,20},{20,16},{24,28},{28,24},{1,5},{5... | collective-permute-start | bytes 1572872 | tf_op jit(solution)/shard_map/ppermute | solution.py:26
  45.5 22.4 %collective-permute-start.7 = (bf16[256,1024]{1,0:T(8,128)(2,1)S(1)}, bf16[256,1024]{1,0:T(8,128)(2,1)S(1)}, u32[]{:S(2)}, u32[]{:S(2)}) collective-permute-start(bf16[256,1024]{1,0:T(8,128)(2,1)S(1)} %get-tuple-element.74), channel_id=1, source_target_pairs={{0,8},{4,12},{8,0},{12,4},{16,24},{20,28},{24,16},{28,20},{1,9},{5... | collective-permute-start | bytes 1572872 | tf_op jit(solution)/shard_map/ppermute | solution.py:26
  59.6 16.7 %collective-permute-start.15 = (bf16[256,1024]{1,0:T(8,128)(2,1)S(1)}, bf16[256,1024]{1,0:T(8,128)(2,1)S(1)}, u32[]{:S(2)}, u32[]{:S(2)}) collective-permute-start(bf16[256,1024]{1,0:T(8,128)(2,1)S(1)} %get-tuple-element.95), channel_id=1, source_target_pairs={{0,4},{4,0},{8,12},{12,8},{16,20},{20,16},{24,28},{28,24},{1,5},{5... | collective-permute-start | bytes 1572872 | tf_op jit(solution)/shard_map/ppermute | solution.py:26
  61.2 17.0 %collective-permute-start.16 = (bf16[256,1024]{1,0:T(8,128)(2,1)S(1)}, bf16[256,1024]{1,0:T(8,128)(2,1)S(1)}, u32[]{:S(2)}, u32[]{:S(2)}) collective-permute-start(bf16[256,1024]{1,0:T(8,128)(2,1)S(1)} %get-tuple-element.96), channel_id=1, source_target_pairs={{0,8},{4,12},{8,0},{12,4},{16,24},{20,28},{24,16},{28,20},{1,9},{5... | collective-permute-start | bytes 1572872 | tf_op jit(solution)/shard_map/ppermute | solution.py:26
  67.9 11.8 %collective-permute-start.12 = (f32[16,128]{1,0:T(8,128)S(1)}, f32[16,128]{1,0:T(8,128)S(1)}, u32[]{:S(2)}, u32[]{:S(2)}) collective-permute-start(f32[16,128]{1,0:T(8,128)S(1)} %gram_rows.5.refs_0_), channel_id=1, source_target_pairs={{0,12},{4,8},{8,4},{12,0},{16,28},{20,24},{24,20},{28,16},{1,13},{... | collective-permute-start | bytes 24584 | tf_op jit(solution)/shard_map/ppermute | solution.py:26
  69.5 11.5 %collective-permute-start.10 = (f32[16,128]{1,0:T(8,128)S(1)}, f32[16,128]{1,0:T(8,128)S(1)}, u32[]{:S(2)}, u32[]{:S(2)}) collective-permute-start(f32[16,128]{1,0:T(8,128)S(1)} %gram_rows.5.refs_0_), channel_id=1, source_target_pairs={{0,4},{4,0},{8,12},{12,8},{16,20},{20,16},{24,28},{28,24},{1,5},{5... | collective-permute-start | bytes 24584 | tf_op jit(solution)/shard_map/ppermute | solution.py:26
  76.3 14.9 %collective-permute-start.19 = (bf16[256,1024]{1,0:T(8,128)(2,1)S(1)}, bf16[256,1024]{1,0:T(8,128)(2,1)S(1)}, u32[]{:S(2)}, u32[]{:S(2)}) collective-permute-start(bf16[256,1024]{1,0:T(8,128)(2,1)S(1)} %get-tuple-element.101), channel_id=1, source_target_pairs={{0,4},{4,0},{8,12},{12,8},{16,20},{20,16},{24,28},{28,24},{1,5},{5... | collective-permute-start | bytes 1572872 | tf_op jit(solution)/shard_map/ppermute | solution.py:26
  78.1 14.9 %collective-permute-start.20 = (bf16[256,1024]{1,0:T(8,128)(2,1)S(1)}, bf16[256,1024]{1,0:T(8,128)(2,1)S(1)}, u32[]{:S(2)}, u32[]{:S(2)}) collective-permute-start(bf16[256,1024]{1,0:T(8,128)(2,1)S(1)} %collective-permute-done.6), channel_id=1, source_target_pairs={{0,8},{4,12},{8,0},{12,4},{16,24},{20,28},{24,16},{28,20},{1,9},{5... | collective-permute-start | bytes 1572872 | tf_op jit(solution)/shard_map/ppermute | solution.py:26
  79.7 20.9 %collective-permute-start.17 = (bf16[256,1024]{1,0:T(8,128)(2,1)S(1)}, bf16[256,1024]{1,0:T(8,128)(2,1)S(1)}, u32[]{:S(2)}, u32[]{:S(2)}) collective-permute-start(bf16[256,1024]{1,0:T(8,128)(2,1)S(1)} %get-tuple-element.97), channel_id=1, source_target_pairs={{0,4},{4,0},{8,12},{12,8},{16,20},{20,16},{24,28},{28,24},{1,5},{5... | collective-permute-start | bytes 1572872 | tf_op jit(solution)/shard_map/ppermute | solution.py:26
  80.2 21.5 %collective-permute-start.18 = (bf16[256,1024]{1,0:T(8,128)(2,1)S(1)}, bf16[256,1024]{1,0:T(8,128)(2,1)S(1)}, u32[]{:S(2)}, u32[]{:S(2)}) collective-permute-start(bf16[256,1024]{1,0:T(8,128)(2,1)S(1)} %collective-permute-done.15), channel_id=1, source_target_pairs={{0,8},{4,12},{8,0},{12,4},{16,24},{20,28},{24,16},{28,20},{1,9},{5... | collective-permute-start | bytes 1572872 | tf_op jit(solution)/shard_map/ppermute | solution.py:26
  87.6 20.6 %collective-permute-start.23 = (bf16[256,1024]{1,0:T(8,128)(2,1)S(1)}, bf16[256,1024]{1,0:T(8,128)(2,1)S(1)}, u32[]{:S(2)}, u32[]{:S(2)}) collective-permute-start(bf16[256,1024]{1,0:T(8,128)(2,1)S(1)} %group_combine.4), channel_id=1, source_target_pairs={{8,16},{12,20},{16,8},{20,12},{9,17},{13,21},{17,9},{21,13},{10,18... | collective-permute-start | bytes 1572872 | tf_op jit(solution)/shard_map/ppermute | solution.py:358
  114.8 18.6 %collective-permute-start.29 = (bf16[256,1024]{1,0:T(8,128)(2,1)S(1)}, bf16[256,1024]{1,0:T(8,128)(2,1)S(1)}, u32[]{:S(2)}, u32[]{:S(2)}) collective-permute-start(bf16[256,1024]{1,0:T(8,128)(2,1)S(1)} %group_combine.4), channel_id=1, source_target_pairs={{0,24},{4,28},{24,0},{28,4},{1,25},{5,29},{25,1},{29,5},{2,26},{6,... | collective-permute-start | bytes 1572872 | tf_op jit(solution)/shard_map/ppermute | solution.py:358
  121.1 21.2 %collective-permute-start.28 = (bf16[256,1024]{1,0:T(8,128)(2,1)S(1)}, bf16[256,1024]{1,0:T(8,128)(2,1)S(1)}, u32[]{:S(2)}, u32[]{:S(2)}) collective-permute-start(bf16[256,1024]{1,0:T(8,128)(2,1)S(1)} %group_combine.7), channel_id=1, source_target_pairs={{0,24},{4,28},{24,0},{28,4},{1,25},{5,29},{25,1},{29,5},{2,26},{6,... | collective-permute-start | bytes 1572872 | tf_op jit(solution)/shard_map/ppermute | solution.py:358
  123.3 19.0 %collective-permute-start.27 = (bf16[256,1024]{1,0:T(8,128)(2,1)S(1)}, bf16[256,1024]{1,0:T(8,128)(2,1)S(1)}, u32[]{:S(2)}, u32[]{:S(2)}) collective-permute-start(bf16[256,1024]{1,0:T(8,128)(2,1)S(1)} %group_combine.7), channel_id=1, source_target_pairs={{8,16},{12,20},{16,8},{20,12},{9,17},{13,21},{17,9},{21,13},{10,18... | collective-permute-start | bytes 1572872 | tf_op jit(solution)/shard_map/ppermute | solution.py:358
  149.7 14.4 %collective-permute-start.36 = (f32[8,128]{1,0:T(8,128)S(1)}, f32[8,128]{1,0:T(8,128)S(1)}, u32[]{:S(2)}, u32[]{:S(2)}) collective-permute-start(f32[8,128]{1,0:T(8,128)S(1)} %total.6.refs_0_), channel_id=1, source_target_pairs={{0,24},{4,28},{8,16},{12,20},{16,8},{20,12},{24,0},{28,4},{1,25},{... | collective-permute-start | bytes 12296 | tf_op jit(solution)/shard_map/ppermute | solution.py:26
  153.2 11.9 %collective-permute-start.35 = (f32[8,128]{1,0:T(8,128)S(1)}, f32[8,128]{1,0:T(8,128)S(1)}, u32[]{:S(2)}, u32[]{:S(2)}) collective-permute-start(f32[8,128]{1,0:T(8,128)S(1)} %total.6.refs_0_), channel_id=1, source_target_pairs={{0,16},{4,20},{8,24},{12,28},{16,0},{20,4},{24,8},{28,12},{1,17},{... | collective-permute-start | bytes 12296 | tf_op jit(solution)/shard_map/ppermute | solution.py:26
  (13 other events, 49.3 us)
